TPU v7x, 512 devices: a whole 4x4x16 slice. The times are simulated.
512 devices in a mesh: section: 4 (over x), seq: 128 (over z, y, core).
Axes of the slice: x: 4, y: 4, z: 16, core: 2. Of those that a mesh axis runs over, the one named last changes fastest.
Arguments:
- feats: bfloat16 [4096, 8, 8, 768], P(('section', 'seq'))
- dw_weight: float32 [7, 7, 768], replicated, may hold values from -0.875 to 0.875
- dw_bias: float32 [768], replicated, may hold values from -3 to 3
- ln1_gain: float32 [768], replicated, may hold values from 0.5 to 2
- w_up: bfloat16 [1536, 768], P('section'), may hold values from -0.21875 to 0.21875
- b_up: bfloat16 [1536], P('section'), may hold values from -3 to 3
- w_down: bfloat16 [1536, 768], P('section'), may hold values from -0.15625 to 0.15625
- b_down: float32 [768], replicated, may hold values from -3 to 3
- layer_scale: float32 [768], replicated, may hold values from 0.3 to 1.5
- lnf_gain: float32 [768], replicated, may hold values from 0.5 to 2
- w_head: bfloat16 [768, 1536], P(None, 'section'), may hold values from -0.21875 to 0.21875
- prior: bfloat16 [77824, 1536], P(('section', 'seq')), may hold values from -6 to 6
- counts: int32 [512], P(('section', 'seq')), may hold values from 0 to 152, as said below
- positions: int32 [81920], P(('section', 'seq')), may hold values from 0 to 32767, as said below
- w_in: bfloat16 [1536, 768], P('section')
- ln_gain: float32 [768], replicated, may hold values from 0.5 to 2
- w_qkv: bfloat16 [768, 2304], P(None, 'section'), may hold values from -0.21875 to 0.21875
- qn_gain: float32 [64], replicated, may hold values from 0.5 to 2
- kn_gain: float32 [64], replicated, may hold values from 0.5 to 2
- offsets: int32 [12], replicated, may hold values from 0 to 15
- w_out: bfloat16 [768, 768], P('section'), may hold values from -6 to 6
Outputs:
- slide_out: bfloat16 [32768, 768], P('seq', 'section')
Inputs may be any that keep to these rules, and one draw needn't show every extreme that they name: `counts`: slot k of a device is valid when k < 8 + its count. Some device of every section index has count 152. `positions`: only valid slots' entries count. The valid slots of all devices hold every position 0 to 32767 exactly once; a valid slot of a device with section index s holds a position p with (p mod 256) div (64) = s. At most 2 valid slots of one device have the same p div 256, and some device reaches 2.
All inputs are finite; a program needn't handle non-finite values.
Results may differ from a plain program's by a relative error of at most 0.014.
Values may be sent and summed in bfloat16 or wider, within the bound.
No kernel may reach another device: no remote copies, remote signals or barrier semaphores. Data moves between devices by JAX's collectives and lax.ppermute only.
A program may use at most 64 MiB of HBM per device.

v0:
```python
import math

import jax
import jax.numpy as jnp
from jax import lax
from jax.sharding import PartitionSpec as P

HS = 64
RB = 16
ROWS = 256


def layer_norm(values, gain_vec):
    row_mean = jnp.mean(values, axis=-1, keepdims=True)
    centered = values - row_mean
    variance = jnp.mean(centered * centered, axis=-1, keepdims=True)
    return centered * lax.rsqrt(variance + 1e-06) * gain_vec


def rms_scale(values, gain_vec):
    return values * lax.rsqrt(jnp.mean(values * values, axis=-1, keepdims=True) + 1e-06) * gain_vec


def conv_norm(tile_maps, dw_weight, dw_bias, ln1_gain):
    map_side = tile_maps.shape[1]
    kernel = dw_weight.shape[0]
    half_width = (kernel - 1) // 2
    source = tile_maps.astype(jnp.float32)
    padded = jnp.pad(source, ((0, 0), (half_width, half_width), (half_width, half_width), (0, 0)))
    conv_sum = jnp.zeros_like(source) + dw_bias
    for row_off in range(kernel):
        for col_off in range(kernel):
            conv_sum = (
                conv_sum
                + padded[:, row_off : row_off + map_side, col_off : col_off + map_side, :]
                * dw_weight[row_off, col_off]
            )
    channels = source.shape[-1]
    normed_maps = layer_norm(conv_sum, ln1_gain).astype(jnp.bfloat16).reshape(-1, channels)
    return (source, normed_maps)


def pointwise(maps, up_rows, up_bias, down_rows, pixels):
    pre_act = lax.dot_general(
        maps, up_rows, (((1,), (1,)), ((), ())), preferred_element_type=jnp.float32
    ) + up_bias.astype(jnp.float32)
    hidden = jax.nn.gelu(pre_act, approximate=False).astype(jnp.bfloat16)
    branch = jnp.dot(hidden, down_rows, preferred_element_type=jnp.float32)
    return jnp.mean(branch.reshape(maps.shape[0] // pixels, pixels, branch.shape[1]), axis=1)


def shards(
    feats,
    dw_weight,
    dw_bias,
    ln1_gain,
    w_up,
    b_up,
    w_down,
    b_down,
    layer_scale,
    lnf_gain,
    w_head,
    prior,
    counts,
    positions,
    w_in,
    ln_gain,
    w_qkv,
    qn_gain,
    kn_gain,
    offsets,
    w_out,
):
    n_seq = lax.axis_size("seq")
    n_section = lax.axis_size("section")
    section_idx = lax.axis_index("section")
    pixels = feats.shape[1] * feats.shape[2]
    source, normed_maps = conv_norm(feats, dw_weight, dw_bias, ln1_gain)
    up_all, bias_all, down_all, head_all, in_all = (
        lax.all_gather(w_up, "section", axis=0, tiled=True),
        lax.all_gather(b_up, "section", axis=0, tiled=True),
        lax.all_gather(w_down, "section", axis=0, tiled=True),
        lax.all_gather(w_head, "section", axis=1, tiled=True),
        lax.all_gather(w_in, "section", axis=0, tiled=True),
    )
    branch_pooled = pointwise(normed_maps, up_all, bias_all, down_all, pixels)
    pooled = jnp.mean(source, axis=(1, 2)) + layer_scale * (branch_pooled + b_down)
    feature = layer_norm(pooled, lnf_gain).astype(jnp.bfloat16)
    fresh_emb = jnp.dot(feature, head_all, preferred_element_type=jnp.float32).astype(jnp.bfloat16)
    slot_rows = jnp.concatenate([fresh_emb, prior], axis=0)
    slot_total = slot_rows.shape[0]
    q_rows = ROWS // n_section
    capacity = -(-slot_total // n_seq)
    live_mask = jnp.arange(slot_total) < feats.shape[0] + counts[0]
    dest_shard = positions // ROWS
    row_in = positions % ROWS - section_idx * q_rows
    onehot_dest = jnp.logical_and(
        live_mask[:, None], dest_shard[:, None] == jnp.arange(n_seq)[None, :]
    ).astype(jnp.int32)
    before = jnp.cumsum(onehot_dest, axis=0) - onehot_dest
    within = jnp.sum(before * onehot_dest, axis=1)
    bucket = jnp.where(live_mask, dest_shard * capacity + within, -1)
    select = jnp.arange(n_seq * capacity)[:, None] == bucket[None, :]
    send_rows = (jnp.sum(jnp.where(select, row_in[None, :] + 1, 0), axis=1) - 1).reshape(
        n_seq, capacity
    )
    select_mat = select.astype(jnp.bfloat16)
    got_vals = lax.all_to_all(
        jnp.dot(select_mat, slot_rows, preferred_element_type=jnp.float32)
        .astype(jnp.bfloat16)
        .reshape(n_seq, capacity, slot_rows.shape[1]),
        "seq",
        split_axis=0,
        concat_axis=0,
        tiled=True,
    )
    got_rows = lax.all_to_all(send_rows, "seq", split_axis=0, concat_axis=0, tiled=True)
    flat_rows = got_rows.reshape(-1)
    placer = (jnp.arange(q_rows)[:, None] == flat_rows[None, :]).astype(jnp.bfloat16)
    x_local = jnp.dot(
        jnp.dot(
            placer,
            got_vals.reshape(flat_rows.shape[0], got_vals.shape[2]),
            preferred_element_type=jnp.float32,
        ).astype(jnp.bfloat16),
        in_all,
        preferred_element_type=jnp.float32,
    ).astype(jnp.bfloat16)
    x_rows = lax.all_gather(x_local, "section", axis=0, tiled=True)
    rows_total = x_rows.shape[0]
    normed = layer_norm(x_rows.astype(jnp.float32), ln_gain).astype(jnp.bfloat16)
    heads_here = w_qkv.shape[1] // (3 * HS)
    qkv_rows = (
        jnp.dot(normed, w_qkv, preferred_element_type=jnp.float32)
        .astype(jnp.bfloat16)
        .reshape(rows_total, 3, heads_here, HS)
    )
    queries = rms_scale(qkv_rows[:, 0].astype(jnp.float32), qn_gain).astype(jnp.bfloat16)
    keys_here = rms_scale(qkv_rows[:, 1].astype(jnp.float32), kn_gain).astype(jnp.bfloat16)
    values_here = qkv_rows[:, 2]
    score_scale = 1.0 / math.sqrt(HS)
    scores = (
        jnp.einsum("qhd,khd->hqk", queries, keys_here, preferred_element_type=jnp.float32)
        * score_scale
    )
    weights = jnp.exp(scores)
    local_den = jnp.sum(weights, axis=-1)
    local_num = jnp.einsum(
        "hqk,khd->hqd",
        weights.astype(jnp.bfloat16),
        values_here,
        preferred_element_type=jnp.float32,
    )
    my_offsets = lax.dynamic_slice_in_dim(offsets, section_idx * heads_here, heads_here)
    picker = jnp.arange(RB)[None, :] == my_offsets[:, None]
    pick_half = picker.astype(jnp.bfloat16)
    stride_rows = rows_total // RB

    def strided(matrix):
        return jnp.einsum(
            "arhd,hr->ahd",
            matrix.reshape(stride_rows, RB, heads_here, HS),
            pick_half,
            preferred_element_type=jnp.float32,
        ).astype(jnp.bfloat16)

    far_q = strided(queries)
    far_k = strided(keys_here)
    far_v = strided(values_here)
    piece_k = lax.all_gather(far_k, "seq", axis=0, tiled=True)
    piece_v = lax.all_gather(far_v, "seq", axis=0, tiled=True)
    far_scores = (
        jnp.einsum("ahd,bhd->hab", far_q, piece_k, preferred_element_type=jnp.float32) * score_scale
    )
    far_weights = jnp.exp(far_scores)
    far_add = jnp.einsum(
        "hab,bhd->had",
        far_weights.astype(jnp.bfloat16),
        piece_v,
        preferred_element_type=jnp.float32,
    )
    far_den = jnp.sum(far_weights, axis=-1)
    pick_full = picker.astype(jnp.float32)
    far_num_full = (far_add[:, :, None, :] * pick_full[:, None, :, None]).reshape(
        heads_here, rows_total, HS
    )
    far_den_full = (far_den[:, :, None] * pick_full[:, None, :]).reshape(heads_here, rows_total)
    attended = ((local_num + far_num_full) / (local_den + far_den_full)[:, :, None]).astype(
        jnp.bfloat16
    )
    merged = jnp.transpose(attended, (1, 0, 2)).reshape(rows_total, heads_here * HS)
    partial_out = jnp.dot(merged, w_out, preferred_element_type=jnp.float32)
    summed = lax.psum_scatter(partial_out, "section", scatter_dimension=1, tiled=True)
    width_part = summed.shape[1]
    residual = lax.dynamic_slice_in_dim(x_rows, section_idx * width_part, width_part, 1)
    return (residual.astype(jnp.float32) + summed).astype(jnp.bfloat16)


def solution(mesh):
    placed = (
        P(("section", "seq"), None, None, None),
        P(),
        P(),
        P(),
        P("section", None),
        P("section"),
        P("section", None),
        P(),
        P(),
        P(),
        P(None, "section"),
        P(("section", "seq"), None),
        P(("section", "seq")),
        P(("section", "seq")),
        P("section", None),
        P(),
        P(None, "section"),
        P(),
        P(),
        P(),
        P("section", None),
    )
    return jax.shard_map(
        shards, mesh=mesh, in_specs=placed, out_specs=P("seq", "section"), check_vma=False
    )
```

profile of v0, /device:TPU:1, one launch (start us, length us, event | category | flops | bytes accessed | tf_op | source)
XLA Modules:
  0.0 420.5 jit_solution(15630676997760096784)
XLA Ops:
  6.5 0.7 all-gather.6.cloned.1.call-update
  7.3 0.7 all-gather.8.cloned.1.call-update
  8.1 0.7 all-gather.10.cloned.1.call-update
  10.2 0.8 sub.50
  11.0 20.6 %all-to-all-start = ((s32[128,1,2]{2,1,0:T(1,128)}), s32[128,1,2]{2,1,0:T(1,128)S(1)}, u32[]{:S(2)}, u32[]{:S(2)}) async-start(s32[128,1,2]{2,1,0:T(1,128)} %bitcast.5), calls=%async_computation | async-start | bytes 131072 | tf_op jit(solution)/shard_map/all_to_all | solution.py:118
  33.3 9.5 %fusion.199 = (f32[8,8,8]{2,1,0:T(8,128)S(1)}, f32[8,8,8,768]{3,2,1,0:T(8,128)S(1)}) fusion(f32[768]{0:T(1024)S(1)} %get-tuple-element.54, f32[768]{0:T(1024)S(1)} %get-tuple-element.55, f32[768]{0:T(1024)S(1)} %get-tuple-element.8, f32[768]{0:T(1024)S(1)} %get-tuple-element.9, f32[768]{0:T(1024)S(1)} %get-tuple-element.10, f32[768]{0:T(1024)S(1)} %get-tuple-element.11, ...), kind=kLoop, calls=%fused_computation.360 | loop fusion | flops 38927872 | bytes 3301376 | tf_op jit(solution)/shard_map/reduce_sum | solution.py:14
  43.4 9.6 %all-gather = bf16[4,1,384]{2,1,0:T(2,128)(2,1)S(1)} all-gather(bf16[1,1,384]{2,1,0:T(2,128)(2,1)S(1)} %reshape.264), channel_id=1, replica_groups=mesh['section'=4,'seq'=128] {'section'}, dimensions={0}, use_global_device_ids=true | all-gather | bytes 3840 | tf_op jit(solution)/shard_map/all_gather | solution.py:82
  53.4 2.2 all-gather.6.cloned.1.call-done
  55.6 42.8 %all-gather.8.cloned.1.call-done = bf16[1536,768]{1,0:T(8,128)(2,1)} async-done(((bf16[384,768]{1,0:T(8,128)(2,1)}), bf16[1536,768]{1,0:T(8,128)(2,1)}) %all-gather.8.cloned.1.call-update) | async-done | bytes 2359312 | tf_op jit(solution)/shard_map/all_gather | solution.py:83
  98.4 11.2 %bitcast_reduce_fusion = f32[8,768]{1,0:T(8,128)S(1)} fusion(bf16[1536,768]{1,0:T(8,128)(2,1)} %all-gather.8.cloned.1.call-done, bf16[512,768]{1,0:T(8,128)(2,1)S(1)} %bitcast.95, bf16[1536,768]{1,0:T(8,128)(2,1)} %all-gather.6.cloned.1.call-done, f32[1536]{0:T(1024)S(1)} %reshape.266), kind=kOutput, calls=%fused_computation.170 | convolution fusion | flops 2468210688 | bytes 5535744 | tf_op jit(solution)/shard_map/dot_general | solution.py:48
  110.0 31.4 %all-gather.10.cloned.1.call-done = bf16[768,1536]{1,0:T(8,128)(2,1)} async-done(((bf16[768,384]{1,0:T(8,128)(2,1)}), bf16[768,1536]{1,0:T(8,128)(2,1)}) %all-gather.10.cloned.1.call-update) | async-done | bytes 2359312 | tf_op jit(solution)/shard_map/all_gather | solution.py:84
  141.4 2.1 convolution_convert_fusion.2
  144.0 1.2 reshape.255
  145.2 16.6 %all-to-all-start.1 = ((bf16[128,2,1536]{2,1,0:T(2,128)(2,1)}), bf16[128,2,1536]{2,1,0:T(2,128)(2,1)S(1)}, u32[]{:S(2)}, u32[]{:S(2)}) async-start(bf16[128,2,1536]{2,1,0:T(2,128)(2,1)} %reshape.255), calls=%async_computation.1 | async-start | bytes 1572864 | tf_op jit(solution)/shard_map/all_to_all | solution.py:109
  162.9 0.8 reduce.103
  163.9 39.4 %all-to-all-done.1 = bf16[128,2,1536]{2,1,0:T(2,128)(2,1)S(1)} async-done(((bf16[128,2,1536]{2,1,0:T(2,128)(2,1)}), bf16[128,2,1536]{2,1,0:T(2,128)(2,1)S(1)}, u32[]{:S(2)}, u32[]{:S(2)}) %all-to-all-start.1) | async-done | bytes 786464 | tf_op jit(solution)/shard_map/all_to_all | solution.py:109
  203.6 2.3 fusion.112
  206.0 10.3 %all_gather.29 = bf16[256,768]{1,0:T(8,128)(2,1)S(1)} all-gather(bf16[64,768]{1,0:T(8,128)(2,1)S(1)} %fusion.112), channel_id=1, replica_groups=mesh['section'=4,'seq'=128] {'section'}, dimensions={0}, use_global_device_ids=true | all-gather | bytes 491520 | tf_op jit(solution)/shard_map/all_gather | solution.py:130
  218.2 88.5 %all_gather.30 = bf16[2048,3,64]{2,0,1:T(8,128)(2,1)S(1)} all-gather(bf16[16,3,64]{2,0,1:T(8,128)(2,1)S(1)} %convert_bitcast_fusion.1), channel_id=1, replica_groups=mesh['section'=4,'seq'=128] {'seq'}, dimensions={0}, use_global_device_ids=true | all-gather | bytes 792576 | tf_op jit(solution)/shard_map/all_gather | solution.py:171
  308.5 81.0 %all_gather.31 = bf16[2048,3,64]{2,0,1:T(8,128)(2,1)S(1)} all-gather(bf16[16,3,64]{2,0,1:T(8,128)(2,1)S(1)} %convert_bitcast_fusion), channel_id=1, replica_groups=mesh['section'=4,'seq'=128] {'seq'}, dimensions={0}, use_global_device_ids=true | all-gather | bytes 792576 | tf_op jit(solution)/shard_map/all_gather | solution.py:172
  390.5 1.2 convolution_bitcast_fusion
  391.7 20.3 %reduce-scatter.4.cloned.1.call-done = f32[192,256]{1,0:T(8,128)} async-done(((f32[768,256]{1,0:T(8,128)}), f32[192,256]{1,0:T(8,128)}) %reduce-scatter.4.cloned.1.call-update) | async-done | bytes 196624
  412.0 1.1 copy.62
  413.2 0.7 copy.54
  (108 shorter events, 10.4 us)
Async XLA Ops:
  6.5 210.2 %copy-start = (bf16[768,576]{0,1:T(8,128)(2,1)S(1)}, bf16[768,576]{0,1:T(8,128)(2,1)}, u32[]{:S(2)}) copy-start(bf16[768,576]{0,1:T(8,128)(2,1)} %param.37) | copy-start | bytes 2654212
  6.5 2.9 copy-start.9
  6.5 49.0 %all-gather.6.cloned.1.call-start = ((), (), s32[]{:S(2)}) async-start(), calls=%async_computation.3 | async-start | bytes 2949120 | tf_op jit(solution)/shard_map/all_gather | solution.py:81
  7.3 24.9 %copy-start.3 = (f32[7,7,768]{2,1,0:T(8,128)S(1)}, f32[7,7,768]{2,1,0:T(8,128)}, u32[]{:S(2)}) copy-start(f32[7,7,768]{2,1,0:T(8,128)} %param.22) | copy-start | bytes 451588
  7.3 25.3 %copy-start.1 = (bf16[8,8,8,768]{3,2,1,0:T(8,128)(2,1)S(1)}, bf16[8,8,8,768]{3,2,1,0:T(8,128)(2,1)}, u32[]{:S(2)}) copy-start(bf16[8,8,8,768]{3,2,1,0:T(8,128)(2,1)} %param.21) | copy-start | bytes 2359300
  7.3 91.1 %all-gather.8.cloned.1.call-start = ((), (), s32[]{:S(2)}) async-start(), calls=%async_computation.4 | async-start | bytes 2949120 | tf_op jit(solution)/shard_map/all_gather | solution.py:83
  8.0 133.4 %all-gather.10.cloned.1.call-start = ((), (), s32[]{:S(2)}) async-start(), calls=%async_computation.5 | async-start | bytes 2949120 | tf_op jit(solution)/shard_map/all_gather | solution.py:84
  11.0 134.3 %all-to-all-start = ((s32[128,1,2]{2,1,0:T(1,128)}), s32[128,1,2]{2,1,0:T(1,128)S(1)}, u32[]{:S(2)}, u32[]{:S(2)}) async-start(s32[128,1,2]{2,1,0:T(1,128)} %bitcast.5), calls=%async_computation | async-start | bytes 131072 | tf_op jit(solution)/shard_map/all_to_all | solution.py:118
  31.5 172.1 %all-gather.12.cloned.1.call-start = ((), (), s32[]{:S(2)}) async-start(), calls=%async_computation.6 | async-start | bytes 2949120 | tf_op jit(solution)/shard_map/all_gather | solution.py:85
  32.6 0.7 copy-start.4
  42.7 0.7 copy-start.10
  42.7 10.4 %copy-start.5 = (f32[768]{0:T(1024)S(1)}, f32[768]{0:T(1024)}, u32[]{:S(2)}) copy-start(f32[768]{0:T(1024)} %param.24) | copy-start | bytes 9220
  98.4 11.2 %copy-start.7 = (f32[768]{0:T(1024)S(1)}, f32[768]{0:T(1024)}, u32[]{:S(2)}) copy-start(f32[768]{0:T(1024)} %param.28) | copy-start | bytes 9220
  98.4 11.2 %copy-start.8 = (f32[768]{0:T(1024)S(1)}, f32[768]{0:T(1024)}, u32[]{:S(2)}) copy-start(f32[768]{0:T(1024)} %param.29) | copy-start | bytes 9220
  98.4 43.0 %copy-start.6 = (f32[768]{0:T(1024)S(1)}, f32[768]{0:T(1024)}, u32[]{:S(2)}) copy-start(f32[768]{0:T(1024)} %param.30) | copy-start | bytes 9220
  109.6 33.9 %copy-start.13 = (bf16[152,1536]{1,0:T(8,128)(2,1)S(1)}, bf16[152,1536]{1,0:T(8,128)(2,1)}, u32[]{:S(2)}) copy-start(bf16[152,1536]{1,0:T(8,128)(2,1)} %param.32) | copy-start | bytes 1400836
  144.0 18.1 %copy-start.15 = (s32[12]{0:T(128)S(1)}, s32[12]{0:T(128)}, u32[]{:S(2)}) copy-start(s32[12]{0:T(128)} %param.40) | copy-start | bytes 148
  145.2 58.1 %all-to-all-start.1 = ((bf16[128,2,1536]{2,1,0:T(2,128)(2,1)}), bf16[128,2,1536]{2,1,0:T(2,128)(2,1)S(1)}, u32[]{:S(2)}, u32[]{:S(2)}) async-start(bf16[128,2,1536]{2,1,0:T(2,128)(2,1)} %reshape.255), calls=%async_computation.1 | async-start | bytes 1572864 | tf_op jit(solution)/shard_map/all_to_all | solution.py:109
  161.9 250.2 %reduce-scatter.4.cloned.1.call-start = ((), (), s32[]{:S(2)}) async-start(), calls=%async_computation.7 | async-start | bytes 983040
  203.6 13.1 %copy-start.14 = (f32[768]{0:T(1024)S(1)}, f32[768]{0:T(1024)}, u32[]{:S(2)}) copy-start(f32[768]{0:T(1024)} %param.36) | copy-start | bytes 9220
  217.3 0.7 copy-start.11
  217.4 89.3 %copy-start.12 = (f32[64]{0:T(128)S(1)}, f32[64]{0:T(128)}, u32[]{:S(2)}) copy-start(f32[64]{0:T(128)} %param.38) | copy-start | bytes 772
  389.5 1.0 copy-start.2
Sparse Core Ops, SparseCore 0:
  9.5 46.0 all-gather.5
  57.7 40.7 all-gather.7
  100.5 40.8 all-gather.9
  143.3 40.8 all-gather.11
  391.8 20.1 reduce-scatter.3
where the time goes:
time: 421 us; the launch traced here: 420 us
  blocking collectives  189 us (45%)
  waiting for transfers between devices  139 us (33%)
  starting transfers between devices  37.6 us (9%)
  matrix products  20.1 us (5%)
  between operations  14.2 us (3%)
  other arithmetic  12.9 us (3%)
  local copies, waits for them, and re-layouts  7.37 us (2%)
    all_gather x1, blocking collectives, shards(): piece_k = lax.all_gather(far_k, 'seq', axis=0, tiled=True)  88.5 us
    all_gather x1, blocking collectives, shards(): piece_v = lax.all_gather(far_v, 'seq', axis=0, tiled=True)  81 us
    all_gather x1, waiting for transfers between devices, shards(): lax.all_gather(w_down, 'section', axis=0, tiled=True)  42.8 us
    all_to_all x1, waiting for transfers between devices, shards(): lax.all_to_all(jnp.dot(select_mat, slot_rows, preferred_element_type=jnp....  39.4 us
    all_gather x1, waiting for transfers between devices, shards(): lax.all_gather(w_head, 'section', axis=1, tiled=True)  31.4 us
    unnamed x6, waiting for transfers between devices  23 us
    all_to_all x1, starting transfers between devices, shards(): lax.all_to_all(send_rows, 'seq', split_axis=0, concat_axis=0, tiled=True)  20.6 us
    all_to_all x1, starting transfers between devices, shards(): lax.all_to_all(jnp.dot(select_mat, slot_rows, preferred_element_type=jnp....  16.6 us
  transfers between devices with their start and end apart: 7, of which 5 were waited for; matrix products, arithmetic and copies ran while one was open for 7% of the time, Pallas kernels for 0%

commit v1 on v0

v1 whole, which is shorter than its diff:
```python
import math

import jax
import jax.numpy as jnp
from jax import lax
from jax.experimental import pallas as pl
from jax.experimental.pallas import tpu as pltpu
from jax.sharding import Mesh
from jax.sharding import PartitionSpec as P

HS = 64
RB = 16
ROWS = 256
N_SECTION = 4
N_Z, N_Y, N_CORE = 16, 4, 2
SEQ_AXES = ("z", "y", "core")
F32 = jnp.float32
BF16 = jnp.bfloat16


def layer_norm(values, gain_vec):
    row_mean = jnp.mean(values, axis=-1, keepdims=True)
    centered = values - row_mean
    variance = jnp.mean(centered * centered, axis=-1, keepdims=True)
    return centered * lax.rsqrt(variance + 1e-06) * gain_vec


def rms_scale(values, gain_vec):
    return values * lax.rsqrt(jnp.mean(values * values, axis=-1, keepdims=True) + 1e-06) * gain_vec


def conv_norm(tile_maps, dw_weight, dw_bias, ln1_gain):
    map_side = tile_maps.shape[1]
    kernel = dw_weight.shape[0]
    half_width = (kernel - 1) // 2
    source = tile_maps.astype(F32)
    padded = jnp.pad(source, ((0, 0), (half_width, half_width), (half_width, half_width), (0, 0)))
    conv_sum = jnp.zeros_like(source) + dw_bias
    for row_off in range(kernel):
        for col_off in range(kernel):
            conv_sum = (
                conv_sum
                + padded[:, row_off : row_off + map_side, col_off : col_off + map_side, :]
                * dw_weight[row_off, col_off]
            )
    channels = source.shape[-1]
    return layer_norm(conv_sum, ln1_gain).astype(BF16).reshape(-1, channels)


def rotate(block, axis, size, step):
    return lax.ppermute(block, axis, [(i, (i + step) % size) for i in range(size)])


def ring(block, cut):
    left = rotate(block, "section", N_SECTION, 1)
    right = rotate(block, "section", N_SECTION, -1)
    far_low = rotate(left[:cut], "section", N_SECTION, 1)
    far_high = rotate(right[cut:], "section", N_SECTION, -1)
    return jnp.stack([block, left, right, jnp.concatenate([far_low, far_high])])


def spread(block, axis, size):
    return lax.all_to_all(
        jnp.broadcast_to(block[None], (size,) + block.shape), axis, 0, 0, tiled=True
    )


def up_pool_kernel(maps_a, maps_b, up_a, up_b, bias, out):
    nt = (((1,), (1,)), ((), ()))
    pre = (
        lax.dot_general(maps_a[...], up_a[0], nt, preferred_element_type=F32)
        + lax.dot_general(maps_b[...], up_b[0], nt, preferred_element_type=F32)
        + bias[0].astype(F32)
    )
    hidden = (0.5 * pre * (1.0 + lax.erf(pre * (1.0 / math.sqrt(2.0))))).astype(BF16).astype(F32)
    tiles = out.shape[1]
    out[0] = jnp.mean(hidden.reshape(tiles, hidden.shape[0] // tiles, hidden.shape[1]), axis=1)


def up_pool(maps_a, maps_b, up_a, up_b, bias, tiles):
    blocks, width, depth = up_a.shape
    return pl.pallas_call(
        up_pool_kernel,
        grid=(blocks,),
        in_specs=[
            pl.BlockSpec(maps_a.shape, lambda i: (0, 0)),
            pl.BlockSpec(maps_b.shape, lambda i: (0, 0)),
            pl.BlockSpec((1, width, depth), lambda i: (i, 0, 0)),
            pl.BlockSpec((1, width, depth), lambda i: (i, 0, 0)),
            pl.BlockSpec((1, 1, width), lambda i: (i, 0, 0)),
        ],
        out_specs=pl.BlockSpec((1, tiles, width), lambda i: (i, 0, 0)),
        out_shape=jax.ShapeDtypeStruct((blocks, tiles, width), F32),
        compiler_params=pltpu.CompilerParams(vmem_limit_bytes=40 * 2**20),
        cost_estimate=pl.CostEstimate(
            flops=4 * blocks * width * depth * maps_a.shape[0],
            bytes_accessed=4 * blocks * width * depth + 4 * maps_a.size,
            transcendentals=blocks * width * maps_a.shape[0],
        ),
    )(maps_a, maps_b, up_a, up_b, bias)


def shards(
    feats,
    dw_weight,
    dw_bias,
    ln1_gain,
    w_up,
    b_up,
    w_down,
    b_down,
    layer_scale,
    lnf_gain,
    w_head,
    prior,
    counts,
    positions,
    w_in,
    ln_gain,
    w_qkv,
    qn_gain,
    kn_gain,
    offsets,
    w_out,
):
    n_section = N_SECTION
    n_seq = N_Z * N_Y * N_CORE
    section_idx = lax.axis_index("section")
    core = lax.axis_index("core")
    tiles = feats.shape[0]
    channels = feats.shape[3]
    half = channels // N_CORE
    share = w_up.shape[0]

    def mine(matrix, axis):
        return lax.dynamic_slice_in_dim(matrix, core * half, half, axis)

    def other(matrix, axis):
        return lax.dynamic_slice_in_dim(matrix, (1 - core) * half, half, axis)

    bias_rows = jnp.broadcast_to(b_up[None, :], (16, share))
    up_ring = ring(jnp.concatenate([mine(w_up, 1), bias_rows]), 192)
    rest_ring = ring(
        jnp.concatenate([mine(w_down, 1), mine(w_head, 0), mine(w_in, 1)]), 3 * share // 2
    )
    up_swap = rotate(up_ring[:, :share], "core", N_CORE, 1)
    rest_swap = rotate(rest_ring, "core", N_CORE, 1)

    slot_total = tiles + prior.shape[0]
    q_rows = ROWS // n_section
    capacity = -(-slot_total // n_seq)
    slot_ids = jnp.arange(slot_total)
    live_mask = slot_ids < tiles + counts[0]
    dest_shard = positions // ROWS
    row_in = positions % ROWS - section_idx * q_rows
    earlier = (
        (dest_shard[None, :] == dest_shard[:, None])
        & (slot_ids[None, :] < slot_ids[:, None])
        & live_mask[None, :]
    )
    within = jnp.sum(earlier.astype(jnp.int32), axis=1)
    bucket = jnp.where(live_mask, dest_shard * capacity + within, -1)
    select_mat = (jnp.arange(n_seq * capacity)[:, None] == bucket[None, :]).astype(BF16)
    row_code = jnp.broadcast_to((row_in + 1).astype(BF16)[:, None], (slot_total, 128))

    normed_maps = conv_norm(feats, dw_weight, dw_bias, ln1_gain)
    feat_mean = jnp.mean(feats.astype(F32), axis=(1, 2))
    hidden_mean = up_pool(
        mine(normed_maps, 1),
        other(normed_maps, 1),
        up_ring[:, :share],
        up_swap,
        up_ring[:, share : share + 1],
        tiles,
    )
    hidden_rows = jnp.transpose(hidden_mean, (1, 0, 2)).reshape(tiles, n_section * share)

    def joined(a, b):
        return jnp.where(core == 0, jnp.concatenate([a, b], 1), jnp.concatenate([b, a], 1))

    def dot(a, b):
        return jnp.dot(a, b, preferred_element_type=F32)

    def dot_split(a, b):
        high = a.astype(BF16)
        low = (a - high.astype(F32)).astype(BF16)
        return dot(high, b) + dot(low, b)

    def rows_of(stack, part):
        block = stack[:, part * share : (part + 1) * share]
        return block.reshape(n_section * share, half)

    branch = joined(
        dot_split(hidden_rows, rows_of(rest_ring, 0)), dot_split(hidden_rows, rows_of(rest_swap, 0))
    )
    pooled = feat_mean + layer_scale * (branch + b_down)
    feature = layer_norm(pooled, lnf_gain).astype(BF16)
    feature_a, feature_b = mine(feature, 1), other(feature, 1)
    relative = [section_idx, (section_idx + 3) % 4, (section_idx + 1) % 4, (section_idx + 2) % 4]
    fresh_emb = jnp.concatenate(
        [
            dot(feature_a, rest_ring[i, share : 2 * share])
            + dot(feature_b, rest_swap[i, share : 2 * share])
            for i in range(n_section)
        ],
        axis=1,
    ).astype(BF16)
    prior_rel = jnp.concatenate(
        [lax.dynamic_slice_in_dim(prior, r * share, share, 1) for r in relative], axis=1
    )
    slot_emb = jnp.concatenate([fresh_emb, prior_rel], axis=0)
    slot_x = joined(dot(slot_emb, rows_of(rest_ring, 2)), dot(slot_emb, rows_of(rest_swap, 2)))

    payload = dot(select_mat, jnp.concatenate([slot_x.astype(BF16), row_code], axis=1)).astype(BF16)
    got = lax.all_to_all(
        payload.reshape(n_seq, capacity, payload.shape[1]), SEQ_AXES, 0, 0, tiled=True
    ).reshape(n_seq * capacity, payload.shape[1])
    code = got[:, channels].astype(F32)
    placer = (jnp.arange(1, q_rows + 1).astype(F32)[:, None] == code[None, :]).astype(BF16)
    x_local = dot(placer, got[:, :channels]).astype(BF16)
    x_rows = lax.all_gather(x_local, "section", axis=0, tiled=True)

    rows_total = x_rows.shape[0]
    normed = layer_norm(x_rows.astype(F32), ln_gain).astype(BF16)
    heads_here = w_qkv.shape[1] // (3 * HS)
    qkv_rows = dot(normed, w_qkv).astype(BF16).reshape(rows_total, 3, heads_here, HS)
    queries = rms_scale(qkv_rows[:, 0].astype(F32), qn_gain).astype(BF16)
    keys_here = rms_scale(qkv_rows[:, 1].astype(F32), kn_gain).astype(BF16)
    values_here = qkv_rows[:, 2]
    score_scale = 1.0 / math.sqrt(HS)
    my_offsets = lax.dynamic_slice_in_dim(offsets, section_idx * heads_here, heads_here)
    picker = jnp.arange(RB)[None, :] == my_offsets[:, None]
    pick_half = picker.astype(BF16)
    stride_rows = rows_total // RB

    def strided(matrix):
        return jnp.einsum(
            "arhd,hr->ahd",
            matrix.reshape(stride_rows, RB, heads_here, HS),
            pick_half,
            preferred_element_type=F32,
        ).astype(BF16)

    far_q = strided(queries)
    far_kv = jnp.concatenate([strided(keys_here), strided(values_here)], axis=1).reshape(
        stride_rows, 2 * heads_here * HS
    )
    z_kv = spread(far_kv, "z", N_Z).reshape(N_Z * stride_rows, 2 * heads_here * HS)
    all_kv = lax.all_gather(z_kv, ("y", "core"), axis=0, tiled=True)
    all_kv = all_kv.reshape(n_seq * stride_rows, 2, heads_here, HS)
    piece_k, piece_v = all_kv[:, 0], all_kv[:, 1]

    scores = (
        jnp.einsum("qhd,khd->hqk", queries, keys_here, preferred_element_type=F32) * score_scale
    )
    weights = jnp.exp(scores)
    local_den = jnp.sum(weights, axis=-1)
    local_num = jnp.einsum(
        "hqk,khd->hqd", weights.astype(BF16), values_here, preferred_element_type=F32
    )
    far_scores = (
        jnp.einsum("ahd,bhd->hab", far_q, piece_k, preferred_element_type=F32) * score_scale
    )
    far_weights = jnp.exp(far_scores)
    far_add = jnp.einsum(
        "hab,bhd->had", far_weights.astype(BF16), piece_v, preferred_element_type=F32
    )
    far_den = jnp.sum(far_weights, axis=-1)
    pick_full = picker.astype(F32)
    far_num_full = (far_add[:, :, None, :] * pick_full[:, None, :, None]).reshape(
        heads_here, rows_total, HS
    )
    far_den_full = (far_den[:, :, None] * pick_full[:, None, :]).reshape(heads_here, rows_total)
    attended = ((local_num + far_num_full) / (local_den + far_den_full)[:, :, None]).astype(BF16)
    merged = jnp.transpose(attended, (1, 0, 2)).reshape(rows_total, heads_here * HS)
    width_part = w_out.shape[1] // n_section
    partial_out = dot(merged, w_out).reshape(rows_total, n_section, width_part)
    parts = lax.all_to_all(
        jnp.transpose(partial_out, (1, 0, 2)), "section", 0, 0, tiled=True
    )
    residual = lax.dynamic_slice_in_dim(x_rows, section_idx * width_part, width_part, 1)
    return (residual.astype(F32) + jnp.sum(parts, axis=0)).astype(BF16)


def solution(mesh):
    fine = Mesh(
        mesh.devices.reshape(N_SECTION, N_Z, N_Y, N_CORE), ("section",) + SEQ_AXES
    )
    both = ("section",) + SEQ_AXES
    placed = (
        P(both, None, None, None),
        P(),
        P(),
        P(),
        P("section", None),
        P("section"),
        P("section", None),
        P(),
        P(),
        P(),
        P(None, "section"),
        P(both, None),
        P(both),
        P(both),
        P("section", None),
        P(),
        P(None, "section"),
        P(),
        P(),
        P(),
        P("section", None),
    )
    return jax.shard_map(
        shards, mesh=fine, in_specs=placed, out_specs=P(SEQ_AXES, "section"), check_vma=False
    )
```

time: 421 us -> 258 us (0.61)
  blocking collectives: 189 us -> 28 us
  waiting for transfers between devices: 139 us -> 85 us
  starting transfers between devices: 37.6 us -> 65 us
  other arithmetic: 12.9 us -> 21 us
  local copies, waits for them, and re-layouts: 7.37 us -> 14.6 us
  matrix products: 20.1 us -> 24.8 us
    all_gather x3 -> x0, blocking collectives: 179 us -> none  [the longest x1 88.5 us: shards(): piece_k = lax.all_gather(far_k, 'seq', axis=0, tiled=True)]
    all_gather x4 -> x1, waiting for transfers between devices: 76.5 us -> 27.1 us  [shards(): all_kv = lax.all_gather(z_kv, ('y', 'core'), axis=0, tiled=True)]
    ppermute x0 -> x10, starting transfers between devices: none -> 41.2 us  [rotate(): lax.ppermute(block, axis, [(i, (i + step) % size) for i in range(size)])]
    unnamed x6 -> x1, waiting for transfers between devices: 23 us -> 0.02 us
    ppermute x0 -> x10, waiting for transfers between devices: none -> 18.5 us  [rotate(): lax.ppermute(block, axis, [(i, (i + step) % size) for i in range(size)])]
    all_to_all x0 -> x1, blocking collectives: none -> 18.4 us  [spread(): lax.all_to_all(jnp.broadcast_to(block[None], (size,) + block.shape), axis...]
    all_to_all x2, starting transfers between devices: 37.2 us -> 23.6 us  [the longest x1 19.6 us: shards(): lax.all_to_all(payload.reshape(n_seq, capacity, payload.shape[1]), SEQ_AX...]
    dot_general x9 -> x22, matrix products: 18.2 us -> 23.5 us  [the longest x18 18.3 us: dot(): return jnp.dot(a, b, preferred_element_type=F32)]
  transfers between devices with their start and end apart: 7 -> 13, of which waited for: 5 -> 6; matrix products, arithmetic and copies ran while one was open for 7% -> 11% of each run, Pallas kernels for 0% -> 1%
where the time goes in v1:
time: 258 us; the launch traced here: 257 us
  waiting for transfers between devices  85 us (33%)
  starting transfers between devices  65 us (25%)
  blocking collectives  28 us (11%)
  matrix products  24.8 us (10%)
  other arithmetic  21 us (8%)
  between operations  14.9 us (6%)
  local copies, waits for them, and re-layouts  14.6 us (6%)
  Pallas kernels  3.23 us (1%)
    ppermute x10, starting transfers between devices, rotate(): lax.ppermute(block, axis, [(i, (i + step) % size) for i in range(size)])  41.2 us
    all_to_all x1, waiting for transfers between devices, shards(): lax.all_to_all(payload.reshape(n_seq, capacity, payload.shape[1]), SEQ_AX...  27.7 us
    all_gather x1, waiting for transfers between devices, shards(): all_kv = lax.all_gather(z_kv, ('y', 'core'), axis=0, tiled=True)  27.1 us
    all_to_all x1, starting transfers between devices, shards(): lax.all_to_all(payload.reshape(n_seq, capacity, payload.shape[1]), SEQ_AX...  19.6 us
    ppermute x10, waiting for transfers between devices, rotate(): lax.ppermute(block, axis, [(i, (i + step) % size) for i in range(size)])  18.5 us
    all_to_all x1, blocking collectives, spread(): lax.all_to_all(jnp.broadcast_to(block[None], (size,) + block.shape), axis...  18.4 us
    dot_general x18, matrix products, dot(): return jnp.dot(a, b, preferred_element_type=F32)  18.3 us
    all_to_all x1, waiting for transfers between devices, shards(): lax.all_to_all(jnp.transpose(partial_out, (1, 0, 2)), 'section', 0, 0, ti...  11.6 us
  transfers between devices with their start and end apart: 13, of which 6 were waited for; matrix products, arithmetic and copies ran while one was open for 11% of the time, Pallas kernels for 1%

profile of v1, /device:TPU:1, one launch (start us, length us, event | category | flops | bytes accessed | tf_op | source)
XLA Modules:
  0.0 256.6 jit_solution(6289513450332005028)
XLA Ops:
  9.0 4.1 %collective-permute-start.5 = (bf16[1152,384]{1,0:T(8,128)(2,1)S(1)}, bf16[1152,384]{1,0:T(8,128)(2,1)S(1)}, u32[]{:S(2)}, u32[]{:S(2)}) collective-permute-start(bf16[1152,384]{1,0:T(8,128)(2,1)S(1)} %get-tuple-element.61), channel_id=1, source_target_pairs={{0,128},{128,256},{256,384},{384,0},{1,129},{129,257},{257,385},{3... | collective-permute-start | bytes 2654216 | tf_op jit(solution)/shard_map/ppermute | solution.py:51
  13.1 3.2 %collective-permute-start.6 = (bf16[1152,384]{1,0:T(8,128)(2,1)S(1)}, bf16[1152,384]{1,0:T(8,128)(2,1)S(1)}, u32[]{:S(2)}, u32[]{:S(2)}) collective-permute-start(bf16[1152,384]{1,0:T(8,128)(2,1)S(1)} %get-tuple-element.61), channel_id=1, source_target_pairs={{0,384},{128,0},{256,128},{384,256},{1,385},{129,1},{257,129},{385... | collective-permute-start | bytes 2654216 | tf_op jit(solution)/shard_map/ppermute | solution.py:51
  16.3 11.5 %collective-permute-done.5 = bf16[1152,384]{1,0:T(8,128)(2,1)S(1)} collective-permute-done((bf16[1152,384]{1,0:T(8,128)(2,1)S(1)}, bf16[1152,384]{1,0:T(8,128)(2,1)S(1)}, u32[]{:S(2)}, u32[]{:S(2)}) %collective-permute-start.5) | collective-permute-done | bytes 884768 | tf_op jit(solution)/shard_map/ppermute | solution.py:51
  27.9 6.7 %collective-permute-start.7 = (bf16[576,384]{1,0:T(8,128)(2,1)S(1)}, bf16[576,384]{1,0:T(8,128)(2,1)S(1)}, u32[]{:S(2)}, u32[]{:S(2)}) collective-permute-start(bf16[576,384]{1,0:T(8,128)(2,1)S(1)} %slice.493), channel_id=1, source_target_pairs={{0,128},{128,256},{256,384},{384,0},{1,129},{129,257},{257,385},{3... | collective-permute-start | bytes 1327112 | tf_op jit(solution)/shard_map/ppermute | solution.py:51
  34.7 4.2 %collective-permute-start.8 = (bf16[576,384]{1,0:T(8,128)(2,1)S(1)}, bf16[576,384]{1,0:T(8,128)(2,1)S(1)}, u32[]{:S(2)}, u32[]{:S(2)}) collective-permute-start(bf16[576,384]{1,0:T(8,128)(2,1)S(1)} %slice.494), channel_id=1, source_target_pairs={{0,384},{128,0},{256,128},{384,256},{1,385},{129,1},{257,129},{385... | collective-permute-start | bytes 1327112 | tf_op jit(solution)/shard_map/ppermute | solution.py:51
  39.0 3.4 %collective-permute-start.1 = (bf16[400,384]{1,0:T(8,128)(2,1)S(1)}, bf16[400,384]{1,0:T(8,128)(2,1)S(1)}, u32[]{:S(2)}, u32[]{:S(2)}) collective-permute-start(bf16[400,384]{1,0:T(8,128)(2,1)S(1)} %get-tuple-element.69), channel_id=1, source_target_pairs={{0,384},{128,0},{256,128},{384,256},{1,385},{129,1},{257,129},{385... | collective-permute-start | bytes 921608 | tf_op jit(solution)/shard_map/ppermute | solution.py:51
  42.3 1.9 collective-permute-start
  44.9 2.0 collective-permute-done.8
  47.1 2.1 pad_maximum_fusion
  49.2 7.5 %collective-permute-start.9 = (bf16[4,1152,384]{2,1,0:T(8,128)(2,1)}, bf16[4,1152,384]{2,1,0:T(8,128)(2,1)}, u32[]{:S(2)}, u32[]{:S(2)}) collective-permute-start(bf16[4,1152,384]{2,1,0:T(8,128)(2,1)} %pad_maximum_fusion), channel_id=1, source_target_pairs={{0,1},{1,0},{2,3},{3,2},{4,5},{5,4},{6,7},{7,6},{8,9},{9,8},{10,11... | collective-permute-start | bytes 10616840 | tf_op jit(solution)/shard_map/ppermute | solution.py:51
  56.7 9.6 %fusion.180 = (f32[8,8,8]{2,1,0:T(8,128)S(1)}, f32[8,8,8,768]{3,2,1,0:T(8,128)S(1)}) fusion(f32[768]{0:T(1024)S(1)} %get-tuple-element.54, f32[768]{0:T(1024)S(1)} %get-tuple-element.55, f32[768]{0:T(1024)S(1)} %get-tuple-element.8, f32[768]{0:T(1024)S(1)} %get-tuple-element.9, f32[768]{0:T(1024)S(1)} %get-tuple-element.10, f32[768]{0:T(1024)S(1)} %get-tuple-element.11, ...), kind=kLoop, calls=%fused_computation.363 | loop fusion | flops 38927872 | bytes 3301376 | tf_op jit(solution)/shard_map/reduce_sum | solution.py:22
  70.3 5.3 %collective-permute-start.3 = (bf16[208,384]{1,0:T(8,128)(2,1)S(1)}, bf16[208,384]{1,0:T(8,128)(2,1)S(1)}, u32[]{:S(2)}, u32[]{:S(2)}) collective-permute-start(bf16[208,384]{1,0:T(8,128)(2,1)S(1)} %slice.491), channel_id=1, source_target_pairs={{0,384},{128,0},{256,128},{384,256},{1,385},{129,1},{257,129},{385... | collective-permute-start | bytes 479240 | tf_op jit(solution)/shard_map/ppermute | solution.py:51
  75.7 1.9 collective-permute-start.2
  79.0 5.0 %collective-permute-done.2 = bf16[192,384]{1,0:T(8,128)(2,1)S(1)} collective-permute-done((bf16[192,384]{1,0:T(8,128)(2,1)S(1)}, bf16[192,384]{1,0:T(8,128)(2,1)S(1)}, u32[]{:S(2)}, u32[]{:S(2)}) %collective-permute-start.2) | collective-permute-done | bytes 147488 | tf_op jit(solution)/shard_map/ppermute | solution.py:51
  84.7 3.0 %collective-permute-start.4 = (bf16[4,384,384]{2,1,0:T(8,128)(2,1)S(1)}, bf16[4,384,384]{2,1,0:T(8,128)(2,1)S(1)}, u32[]{:S(2)}, u32[]{:S(2)}) collective-permute-start(bf16[4,384,384]{2,1,0:T(8,128)(2,1)S(1)} %slice.492.up_a), channel_id=1, source_target_pairs={{0,1},{1,0},{2,3},{3,2},{4,5},{5,4},{6,7},{7,6},{8,9},{9,8},{10,11... | collective-permute-start | bytes 3538952 | tf_op jit(solution)/shard_map/ppermute | solution.py:51
  89.3 1.8 multiply_convert_fusion
  93.6 3.2 %shard_map.199 = f32[4,8,384]{2,1,0:T(8,128)S(1)} custom-call(bf16[512,384]{1,0:T(8,128)(2,1)S(1)} %get-tuple-element.63.maps_a, bf16[512,384]{1,0:T(8,128)(2,1)S(1)} %get-tuple-element.62.maps_b, bf16[4,384,384]{2,1,0:T(8,128)(2,1)S(1)} %slice.492.up_a, bf16[4,384,384]{2,1,0:T(8,128)(2,1)S(1)} %collective-permute-done.4.up_b, ...), custom_call_target="tpu_custom_call" | custom-call | flops 1207959552 | bytes 3145728 | tf_op jit(solution)/shard_map/pallas_call | solution.py:82
  116.4 19.6 %all-to-all-start = ((bf16[128,2,896]{2,1,0:T(2,128)(2,1)}), bf16[128,2,896]{2,1,0:T(2,128)(2,1)S(1)}, u32[]{:S(2)}, u32[]{:S(2)}) async-start(bf16[128,2,896]{2,1,0:T(2,128)(2,1)} %reshape.256), calls=%async_computation | async-start | bytes 917504 | tf_op jit(solution)/shard_map/all_to_all | solution.py:215
  136.4 27.7 %all-to-all-done = bf16[128,2,896]{2,1,0:T(2,128)(2,1)S(1)} async-done(((bf16[128,2,896]{2,1,0:T(2,128)(2,1)}), bf16[128,2,896]{2,1,0:T(2,128)(2,1)S(1)}, u32[]{:S(2)}, u32[]{:S(2)}) %all-to-all-start) | async-done | bytes 458784 | tf_op jit(solution)/shard_map/all_to_all | solution.py:215
  164.7 9.6 %all_gather.6 = bf16[256,768]{1,0:T(8,128)(2,1)S(1)} all-gather(bf16[64,768]{1,0:T(8,128)(2,1)S(1)} %convolution_convert_fusion.2), channel_id=1, replica_groups=mesh['section'=4,'z'=16,'y'=4,'core'=2] {'section'}, dimensions={0}, use_global_device_ids=true | all-gather | bytes 491520 | tf_op jit(solution)/shard_map/all_gather | solution.py:221
  176.5 18.4 %all_to_all.15 = bf16[16,16,384]{2,1,0:T(8,128)(2,1)} all-to-all(bf16[16,16,384]{2,1,0:T(8,128)(2,1)S(1)} %broadcast_in_dim.13), channel_id=1, replica_groups=mesh['section'=4,'z'=16,'y'=4,'core'=2] {'z'}, dimensions={0} | all-to-all | bytes 393216 | tf_op jit(solution)/shard_map/all_to_all | solution.py:63
  197.5 27.1 %all-gather.2.cloned.1.call-done = bf16[2048,384]{1,0:T(8,128)(2,1)} async-done(((bf16[256,384]{1,0:T(8,128)(2,1)}), bf16[2048,384]{1,0:T(8,128)(2,1)}) %all-gather.2.cloned.1.call-update) | async-done | bytes 1572880 | tf_op jit(solution)/shard_map/all_gather | solution.py:249
  233.2 4.0 %all-to-all-start.2 = ((f32[4,256,192]{1,2,0:T(8,128)}), f32[4,256,192]{1,2,0:T(8,128)S(1)}, u32[]{:S(2)}, u32[]{:S(2)}) async-start(f32[4,256,192]{1,2,0:T(8,128)} %convolution_bitcast_fusion), calls=%async_computation.2 | async-start | bytes 1572864 | tf_op jit(solution)/shard_map/all_to_all | solution.py:278
  237.4 11.6 %all-to-all-done.2 = f32[4,256,192]{1,2,0:T(8,128)S(1)} async-done(((f32[4,256,192]{1,2,0:T(8,128)}), f32[4,256,192]{1,2,0:T(8,128)S(1)}, u32[]{:S(2)}, u32[]{:S(2)}) %all-to-all-start.2) | async-done | bytes 786464 | tf_op jit(solution)/shard_map/all_to_all | solution.py:278
  (176 shorter events, 47.3 us)
Async XLA Ops:
  6.5 168.2 %copy-start = (bf16[768,576]{0,1:T(8,128)(2,1)S(1)}, bf16[768,576]{0,1:T(8,128)(2,1)}, u32[]{:S(2)}) copy-start(bf16[768,576]{0,1:T(8,128)(2,1)} %param.37) | copy-start | bytes 2654212
  8.9 30.0 %copy-start.28 = (bf16[384]{0:T(512)(128)(2,1)S(1)}, bf16[384]{0:T(512)(128)(2,1)}, u32[]{:S(2)}) copy-start(bf16[384]{0:T(512)(128)(2,1)} %param.26) | copy-start | bytes 2308
  9.0 38.0 %copy-start.3 = (bf16[1,1152,384]{2,1,0:T(8,128)(2,1)}, bf16[1,1152,384]{2,1,0:T(8,128)(2,1)S(1)}, u32[]{:S(2)}) copy-start(bf16[1,1152,384]{2,1,0:T(8,128)(2,1)S(1)} %get-tuple-element.60) | copy-start | bytes 2654212
  9.0 35.2 %copy-start.4 = (bf16[8,8,8,768]{3,2,1,0:T(8,128)(2,1)S(1)}, bf16[8,8,8,768]{3,2,1,0:T(8,128)(2,1)}, u32[]{:S(2)}) copy-start(bf16[8,8,8,768]{3,2,1,0:T(8,128)(2,1)} %param.21) | copy-start | bytes 2359300
  9.0 18.8 %collective-permute-start.5 = (bf16[1152,384]{1,0:T(8,128)(2,1)S(1)}, bf16[1152,384]{1,0:T(8,128)(2,1)S(1)}, u32[]{:S(2)}, u32[]{:S(2)}) collective-permute-start(bf16[1152,384]{1,0:T(8,128)(2,1)S(1)} %get-tuple-element.61), channel_id=1, source_target_pairs={{0,128},{128,256},{256,384},{384,0},{1,129},{129,257},{257,385},{3... | collective-permute-start | bytes 2654216 | tf_op jit(solution)/shard_map/ppermute | solution.py:51
  13.1 21.5 %collective-permute-start.6 = (bf16[1152,384]{1,0:T(8,128)(2,1)S(1)}, bf16[1152,384]{1,0:T(8,128)(2,1)S(1)}, u32[]{:S(2)}, u32[]{:S(2)}) collective-permute-start(bf16[1152,384]{1,0:T(8,128)(2,1)S(1)} %get-tuple-element.61), channel_id=1, source_target_pairs={{0,384},{128,0},{256,128},{384,256},{1,385},{129,1},{257,129},{385... | collective-permute-start | bytes 2654216 | tf_op jit(solution)/shard_map/ppermute | solution.py:51
  27.8 19.2 %copy-start.7 = (bf16[1152,384]{1,0:T(8,128)(2,1)}, bf16[1152,384]{1,0:T(8,128)(2,1)S(1)}, u32[]{:S(2)}) copy-start(bf16[1152,384]{1,0:T(8,128)(2,1)S(1)} %collective-permute-done.5) | copy-start | bytes 2654212
  27.9 17.0 %collective-permute-start.7 = (bf16[576,384]{1,0:T(8,128)(2,1)S(1)}, bf16[576,384]{1,0:T(8,128)(2,1)S(1)}, u32[]{:S(2)}, u32[]{:S(2)}) collective-permute-start(bf16[576,384]{1,0:T(8,128)(2,1)S(1)} %slice.493), channel_id=1, source_target_pairs={{0,128},{128,256},{256,384},{384,0},{1,129},{129,257},{257,385},{3... | collective-permute-start | bytes 1327112 | tf_op jit(solution)/shard_map/ppermute | solution.py:51
  34.6 12.4 %copy-start.6 = (bf16[1152,384]{1,0:T(8,128)(2,1)}, bf16[1152,384]{1,0:T(8,128)(2,1)S(1)}, u32[]{:S(2)}) copy-start(bf16[1152,384]{1,0:T(8,128)(2,1)S(1)} %collective-permute-done.6) | copy-start | bytes 2654212
  34.7 12.2 %collective-permute-start.8 = (bf16[576,384]{1,0:T(8,128)(2,1)S(1)}, bf16[576,384]{1,0:T(8,128)(2,1)S(1)}, u32[]{:S(2)}, u32[]{:S(2)}) collective-permute-start(bf16[576,384]{1,0:T(8,128)(2,1)S(1)} %slice.494), channel_id=1, source_target_pairs={{0,384},{128,0},{256,128},{384,256},{1,385},{129,1},{257,129},{385... | collective-permute-start | bytes 1327112 | tf_op jit(solution)/shard_map/ppermute | solution.py:51
  39.0 31.3 %collective-permute-start.1 = (bf16[400,384]{1,0:T(8,128)(2,1)S(1)}, bf16[400,384]{1,0:T(8,128)(2,1)S(1)}, u32[]{:S(2)}, u32[]{:S(2)}) collective-permute-start(bf16[400,384]{1,0:T(8,128)(2,1)S(1)} %get-tuple-element.69), channel_id=1, source_target_pairs={{0,384},{128,0},{256,128},{384,256},{1,385},{129,1},{257,129},{385... | collective-permute-start | bytes 921608 | tf_op jit(solution)/shard_map/ppermute | solution.py:51
  42.3 33.3 %collective-permute-start = (bf16[400,384]{1,0:T(8,128)(2,1)S(1)}, bf16[400,384]{1,0:T(8,128)(2,1)S(1)}, u32[]{:S(2)}, u32[]{:S(2)}) collective-permute-start(bf16[400,384]{1,0:T(8,128)(2,1)S(1)} %get-tuple-element.69), channel_id=1, source_target_pairs={{0,128},{128,256},{256,384},{384,0},{1,129},{129,257},{257,385},{3... | collective-permute-start | bytes 921608 | tf_op jit(solution)/shard_map/ppermute | solution.py:51
  49.2 50.8 %collective-permute-start.9 = (bf16[4,1152,384]{2,1,0:T(8,128)(2,1)}, bf16[4,1152,384]{2,1,0:T(8,128)(2,1)}, u32[]{:S(2)}, u32[]{:S(2)}) collective-permute-start(bf16[4,1152,384]{2,1,0:T(8,128)(2,1)} %pad_maximum_fusion), channel_id=1, source_target_pairs={{0,1},{1,0},{2,3},{3,2},{4,5},{5,4},{6,7},{7,6},{8,9},{9,8},{10,11... | collective-permute-start | bytes 10616840 | tf_op jit(solution)/shard_map/ppermute | solution.py:51
  70.3 13.7 %copy-start.10 = (bf16[400,384]{1,0:T(8,128)(2,1)}, bf16[400,384]{1,0:T(8,128)(2,1)S(1)}, u32[]{:S(2)}) copy-start(bf16[400,384]{1,0:T(8,128)(2,1)S(1)} %collective-permute-done.1) | copy-start | bytes 921604
  70.3 13.6 %collective-permute-start.3 = (bf16[208,384]{1,0:T(8,128)(2,1)S(1)}, bf16[208,384]{1,0:T(8,128)(2,1)S(1)}, u32[]{:S(2)}, u32[]{:S(2)}) collective-permute-start(bf16[208,384]{1,0:T(8,128)(2,1)S(1)} %slice.491), channel_id=1, source_target_pairs={{0,384},{128,0},{256,128},{384,256},{1,385},{129,1},{257,129},{385... | collective-permute-start | bytes 479240 | tf_op jit(solution)/shard_map/ppermute | solution.py:51
  75.7 8.3 %collective-permute-start.2 = (bf16[192,384]{1,0:T(8,128)(2,1)S(1)}, bf16[192,384]{1,0:T(8,128)(2,1)S(1)}, u32[]{:S(2)}, u32[]{:S(2)}) collective-permute-start(bf16[192,384]{1,0:T(8,128)(2,1)S(1)} %slice.490), channel_id=1, source_target_pairs={{0,128},{128,256},{256,384},{384,0},{1,129},{129,257},{257,385},{3... | collective-permute-start | bytes 442376 | tf_op jit(solution)/shard_map/ppermute | solution.py:51
  84.7 8.9 %collective-permute-start.4 = (bf16[4,384,384]{2,1,0:T(8,128)(2,1)S(1)}, bf16[4,384,384]{2,1,0:T(8,128)(2,1)S(1)}, u32[]{:S(2)}, u32[]{:S(2)}) collective-permute-start(bf16[4,384,384]{2,1,0:T(8,128)(2,1)S(1)} %slice.492.up_a), channel_id=1, source_target_pairs={{0,1},{1,0},{2,3},{3,2},{4,5},{5,4},{6,7},{7,6},{8,9},{9,8},{10,11... | collective-permute-start | bytes 3538952 | tf_op jit(solution)/shard_map/ppermute | solution.py:51
  114.9 21.3 %copy-start.33 = (s32[12]{0:T(128)S(1)}, s32[12]{0:T(128)}, u32[]{:S(2)}) copy-start(s32[12]{0:T(128)} %param.40) | copy-start | bytes 148
  116.4 47.8 %all-to-all-start = ((bf16[128,2,896]{2,1,0:T(2,128)(2,1)}), bf16[128,2,896]{2,1,0:T(2,128)(2,1)S(1)}, u32[]{:S(2)}, u32[]{:S(2)}) async-start(bf16[128,2,896]{2,1,0:T(2,128)(2,1)} %reshape.256), calls=%async_computation | async-start | bytes 917504 | tf_op jit(solution)/shard_map/all_to_all | solution.py:215
  136.0 38.7 %copy-start.32 = (f32[768]{0:T(1024)S(1)}, f32[768]{0:T(1024)}, u32[]{:S(2)}) copy-start(f32[768]{0:T(1024)} %param.36) | copy-start | bytes 9220
  136.0 88.5 %all-gather.2.cloned.1.call-start = ((), (), s32[]{:S(2)}) async-start(), calls=%async_computation.3 | async-start | bytes 1769472 | tf_op jit(solution)/shard_map/all_gather | solution.py:249
  175.3 19.7 %copy-start.15 = (bf16[192,768]{1,0:T(8,128)(2,1)S(1)}, bf16[192,768]{1,0:T(8,128)(2,1)}, u32[]{:S(2)}) copy-start(bf16[192,768]{1,0:T(8,128)(2,1)} %param.41) | copy-start | bytes 884740
  175.6 19.8 %copy-start.30 = (f32[64]{0:T(128)S(1)}, f32[64]{0:T(128)}, u32[]{:S(2)}) copy-start(f32[64]{0:T(128)} %param.38) | copy-start | bytes 772
  233.2 15.8 %all-to-all-start.2 = ((f32[4,256,192]{1,2,0:T(8,128)}), f32[4,256,192]{1,2,0:T(8,128)S(1)}, u32[]{:S(2)}, u32[]{:S(2)}) async-start(f32[4,256,192]{1,2,0:T(8,128)} %convolution_bitcast_fusion), calls=%async_computation.2 | async-start | bytes 1572864 | tf_op jit(solution)/shard_map/all_to_all | solution.py:278
  (23 other events, 104.6 us)
Sparse Core Ops, SparseCore 0:
  195.0 29.4 all-gather.1

commit v2 on v1

v2 whole, which is shorter than its diff:
```python
import math

import jax
import jax.numpy as jnp
from jax import lax
from jax.experimental import pallas as pl
from jax.experimental.pallas import tpu as pltpu
from jax.sharding import Mesh
from jax.sharding import PartitionSpec as P

HS = 64
RB = 16
ROWS = 256
N_SECTION = 4
N_Z, N_Y, N_CORE = 16, 4, 2
SEQ_AXES = ("z", "y", "core")
F32 = jnp.float32
BF16 = jnp.bfloat16


def layer_norm(values, gain_vec):
    row_mean = jnp.mean(values, axis=-1, keepdims=True)
    centered = values - row_mean
    variance = jnp.mean(centered * centered, axis=-1, keepdims=True)
    return centered * lax.rsqrt(variance + 1e-06) * gain_vec


def conv_norm(tile_maps, dw_weight, dw_bias, ln1_gain):
    map_side = tile_maps.shape[1]
    kernel = dw_weight.shape[0]
    half_width = (kernel - 1) // 2
    source = tile_maps.astype(F32)
    padded = jnp.pad(source, ((0, 0), (half_width, half_width), (half_width, half_width), (0, 0)))
    conv_sum = jnp.zeros_like(source) + dw_bias
    for row_off in range(kernel):
        for col_off in range(kernel):
            conv_sum = (
                conv_sum
                + padded[:, row_off : row_off + map_side, col_off : col_off + map_side, :]
                * dw_weight[row_off, col_off]
            )
    channels = source.shape[-1]
    return layer_norm(conv_sum, ln1_gain).astype(BF16).reshape(-1, channels)


def rotate(block, axis, size, step):
    return lax.ppermute(block, axis, [(i, (i + step) % size) for i in range(size)])


def spread(block, axis, size):
    return lax.all_to_all(
        jnp.broadcast_to(block[None], (size,) + block.shape), axis, 0, 0, tiled=True
    )


NT = (((1,), (1,)), ((), ()))


def dot(a, b):
    return jnp.dot(a, b, preferred_element_type=F32)


def gelu_mean(pre, tiles):
    hidden = (0.5 * pre * (1.0 + lax.erf(pre * (1.0 / math.sqrt(2.0))))).astype(BF16).astype(F32)
    return jnp.mean(hidden.reshape(tiles, hidden.shape[0] // tiles, hidden.shape[1]), axis=1)


def lanes(ref, index, width):
    return ref[:, pl.ds(pl.multiple_of(index * width, 128), width)]


def pack_kernel(core_ref, w_up, w_down, w_head, w_in, bias_rows, out, sems):
    n = w_up.shape[0]
    start = pl.multiple_of(core_ref[0] * n, n)
    parts = (
        w_up.at[:, pl.ds(start, n)],
        w_down.at[:, pl.ds(start, n)],
        w_head.at[pl.ds(start, n), :],
        w_in.at[:, pl.ds(start, n)],
    )
    copies = [
        pltpu.make_async_copy(part, out.at[pl.ds(k * n, n), :], sems.at[k])
        for k, part in enumerate(parts)
    ]
    copies.append(pltpu.make_async_copy(bias_rows, out.at[pl.ds(4 * n, 16), :], sems.at[4]))
    for copy in copies:
        copy.start()
    for copy in copies:
        copy.wait()


def pack(core, w_up, w_down, w_head, w_in, bias_rows):
    n = w_up.shape[0]
    return pl.pallas_call(
        pack_kernel,
        in_specs=[pl.BlockSpec(memory_space=pltpu.SMEM)] + [pl.BlockSpec(memory_space=pl.ANY)] * 5,
        out_specs=pl.BlockSpec(memory_space=pltpu.VMEM),
        out_shape=jax.ShapeDtypeStruct((4 * n + 16, n), BF16),
        scratch_shapes=[pltpu.SemaphoreType.DMA((5,))],
        cost_estimate=pl.CostEstimate(flops=0, bytes_accessed=4 * n * n * 4, transcendentals=0),
    )(core.astype(jnp.int32)[None], w_up, w_down, w_head, w_in, bias_rows)


def early_kernel(
    where, maps, up, bias, w_in, prior, left, right, left_swap, right_swap, hid, x_prior
):
    core = where[0]
    n = up.shape[0]
    tiles = hid.shape[1]
    maps_a, maps_b = lanes(maps, core, n), lanes(maps, 1 - core, n)
    pre = lax.dot_general(maps[...], up[...], NT, preferred_element_type=F32)
    hid[0] = gelu_mean(pre + bias[...].astype(F32), tiles)
    own = dot(lanes(prior, where[1], n), w_in[...])
    x_a = jnp.zeros((prior.shape[0], n), F32)
    x_b = x_a
    for slot, (a, b) in enumerate(((left, left_swap), (right, right_swap))):
        pre = lax.dot_general(maps_a, a[0:n, :], NT, preferred_element_type=F32)
        pre += lax.dot_general(maps_b, b[0:n, :], NT, preferred_element_type=F32)
        hid[slot + 1] = gelu_mean(pre + a[4 * n : 4 * n + 1, :].astype(F32), tiles)
        columns = lanes(prior, where[slot + 2], n)
        x_a += dot(columns, a[3 * n : 4 * n, :])
        x_b += dot(columns, b[3 * n : 4 * n, :])
    x_prior[...] = own + natural(core, x_a, x_b)


def natural(core, a, b):
    return jnp.where(core == 0, jnp.concatenate([a, b], 1), jnp.concatenate([b, a], 1))


def late_kernel(
    where, maps, prior, hid, x_prior, feat_mean, layer_scale, b_down, lnf_gain, bucket, row_code,
    w_down, w_head, w_in, left, right, left_swap, right_swap, low, high, low_swap, high_swap,
    payload, slot_x,
):
    core = where[0]
    n = w_down.shape[0]
    tiles = hid.shape[1]
    pre = lax.dot_general(lanes(maps, core, n), low[0:n, :], NT, preferred_element_type=F32)
    pre += lax.dot_general(
        lanes(maps, 1 - core, n), low_swap[0:n, :], NT, preferred_element_type=F32
    )
    hid_far = gelu_mean(pre + high[2 * n : 2 * n + 1, :].astype(F32), tiles)

    def exact(block):
        upper = block.astype(BF16)
        lower = (block - upper.astype(F32)).astype(BF16)
        return jnp.concatenate([upper.astype(F32), lower.astype(F32)], 0).astype(BF16)

    def folded(block):
        return block[0:tiles] + block[tiles : 2 * tiles]

    sides = ((left, left_swap), (right, right_swap))
    own = dot(exact(hid[0]), w_down[...])
    part = exact(hid_far)
    br_a, br_b = dot(part, low[n : 2 * n, :]), dot(part, low_swap[n : 2 * n, :])
    for slot, (a, b) in enumerate(sides):
        part = exact(hid[slot + 1])
        br_a += dot(part, a[n : 2 * n, :])
        br_b += dot(part, b[n : 2 * n, :])
    branch = folded(own + natural(core, br_a, br_b))
    pooled = feat_mean[...] + layer_scale[...] * (branch + b_down[...])
    feature = layer_norm(pooled, lnf_gain[...])
    first, second = feature[:, 0:n], feature[:, n : 2 * n]
    feature_a = jnp.where(core == 0, first, second).astype(BF16)
    feature_b = jnp.where(core == 0, second, first).astype(BF16)
    emb = dot(feature.astype(BF16), w_head[...]).astype(BF16)
    own = dot(emb, w_in[...])
    emb = (dot(feature_a, high[0:n, :]) + dot(feature_b, high_swap[0:n, :])).astype(BF16)
    columns = lanes(prior, where[4], n)
    x_a, x_b = dot(emb, high[n : 2 * n, :]), dot(emb, high_swap[n : 2 * n, :])
    p_a, p_b = dot(columns, high[n : 2 * n, :]), dot(columns, high_swap[n : 2 * n, :])
    for a, b in sides:
        emb = (
            dot(feature_a, a[2 * n : 3 * n, :]) + dot(feature_b, b[2 * n : 3 * n, :])
        ).astype(BF16)
        x_a += dot(emb, a[3 * n : 4 * n, :])
        x_b += dot(emb, b[3 * n : 4 * n, :])
    slot_x[0:tiles, :] = own + natural(core, x_a, x_b)
    slot_x[tiles:, :] = x_prior[...] + natural(core, p_a, p_b)
    places = lax.broadcasted_iota(jnp.int32, (payload.shape[0], bucket.shape[1]), 0)
    select = jnp.where(places == bucket[...], 1.0, 0.0).astype(BF16)
    width = slot_x.shape[1]
    payload[:, 0:width] = dot(select, slot_x[...].astype(BF16)).astype(BF16)
    payload[:, width:] = dot(select, row_code[...]).astype(BF16)


def local_call(body, outs, scratch, flops, size, *operands):
    vmem = pl.BlockSpec(memory_space=pltpu.VMEM)
    return pl.pallas_call(
        body,
        in_specs=[pl.BlockSpec(memory_space=pltpu.SMEM)] + [vmem] * (len(operands) - 1),
        out_specs=jax.tree.map(lambda _: vmem, outs),
        out_shape=outs,
        scratch_shapes=scratch,
        compiler_params=pltpu.CompilerParams(vmem_limit_bytes=48 * 2**20),
        cost_estimate=pl.CostEstimate(flops=flops, bytes_accessed=size, transcendentals=0),
    )(*operands)


def head_lanes(shape, head):
    lane = lax.broadcasted_iota(jnp.int32, shape, len(shape) - 1)
    return (lane >= head * HS) & (lane < (head + 1) * HS)


def dilated(shape, off_lane):
    return lax.rem(lax.broadcasted_iota(jnp.int32, shape, 0), RB) == off_lane


def project_kernel(x, ln_gain, w_q, w_k, w_v, q_gain, k_gain, off_lane, q, k, v, far_q, far_kv):
    rows, width = q.shape
    normed = layer_norm(x[...].astype(F32), ln_gain[...]).astype(BF16)
    chosen = dilated((rows, width), off_lane[...])

    def unit(raw, gain):
        raw = raw.astype(BF16).astype(F32)
        square = raw * raw
        mean = jnp.zeros_like(raw)
        for head in range(width // HS):
            inside = head_lanes(raw.shape, head)
            total = jnp.sum(jnp.where(inside, square, 0.0), axis=1, keepdims=True) * (1.0 / HS)
            mean = jnp.where(inside, total, mean)
        return (raw * lax.rsqrt(mean + 1e-06) * gain).astype(BF16)

    def far_rows(part):
        kept = jnp.where(chosen, part.astype(F32), 0.0)
        return jnp.sum(kept.reshape(rows // RB, RB, width), axis=1)

    q_rows = unit(dot(normed, w_q[...]), q_gain[...])
    k_rows = unit(dot(normed, w_k[...]), k_gain[...])
    v_rows = dot(normed, w_v[...]).astype(BF16)
    q[...], k[...], v[...] = q_rows, k_rows, v_rows
    far_q[...] = far_rows(q_rows)
    far_kv[...] = jnp.concatenate([far_rows(k_rows), far_rows(v_rows)], axis=1).astype(BF16)


def by_head(block):
    heads = block.shape[1] // HS
    wide = block.astype(F32)
    kept = [jnp.where(head_lanes(wide.shape, head), wide, 0.0) for head in range(heads)]
    return jnp.concatenate(kept, axis=0)


def back(block, rows, width):
    out = jnp.zeros((rows, width), F32)
    for head in range(width // HS):
        part = jnp.broadcast_to(block[head * rows : (head + 1) * rows], (rows, width))
        out = jnp.where(head_lanes(out.shape, head), part, out)
    return out


def weigh(queries, keys, values):
    scores = lax.dot_general(queries, keys, NT, preferred_element_type=F32)
    weights = jnp.exp(scores * (1.0 / math.sqrt(HS)))
    return jnp.sum(weights, axis=1, keepdims=True), dot(weights.astype(BF16), values)


def far_part(far_q, kv):
    rows, width = far_q.shape
    spread_q = by_head(far_q[...])
    spread_q = jnp.concatenate([spread_q, jnp.zeros_like(spread_q)], axis=1).astype(BF16)
    den, num = weigh(spread_q, kv[...], kv[...])
    return back(den, rows, width), back(num[:, width:], rows, width)


def near_kernel(q, k, v, far_q, kv, den, num, far_den, far_num):
    rows, width = q.shape
    local_den, local_num = weigh(by_head(q[...]).astype(BF16), k[...], v[...])
    den[...] = back(local_den, rows, width)
    num[...] = back(local_num, rows, width)
    far_den[...], far_num[...] = far_part(far_q, kv)


def far_kernel(far_q, kv, off_lane, den, num, far_den, far_num, w_out, out):
    rows, width = num.shape
    chosen = dilated((rows, width), off_lane[...])
    more_den, more_num = far_part(far_q, kv)

    def placed(block):
        wide = jnp.broadcast_to(block[:, None, :], (rows // RB, RB, width))
        return jnp.where(chosen, wide.reshape(rows, width), 0.0)

    attended = (num[...] + placed(far_num[...] + more_num)) / (
        den[...] + placed(far_den[...] + more_den)
    )
    attended = attended.astype(BF16)
    out[...] = lax.dot_general(w_out[...], attended, NT, preferred_element_type=F32).astype(BF16)


def vmem_call(body, outs, flops, size, exps, *operands):
    vmem = pl.BlockSpec(memory_space=pltpu.VMEM)
    return pl.pallas_call(
        body,
        in_specs=[vmem] * len(operands),
        out_specs=jax.tree.map(lambda _: vmem, outs),
        out_shape=outs,
        compiler_params=pltpu.CompilerParams(vmem_limit_bytes=40 * 2**20),
        cost_estimate=pl.CostEstimate(flops=flops, bytes_accessed=size, transcendentals=exps),
    )(*operands)


def shards(
    feats,
    dw_weight,
    dw_bias,
    ln1_gain,
    w_up,
    b_up,
    w_down,
    b_down,
    layer_scale,
    lnf_gain,
    w_head,
    prior,
    counts,
    positions,
    w_in,
    ln_gain,
    w_qkv,
    qn_gain,
    kn_gain,
    offsets,
    w_out,
):
    n_section = N_SECTION
    n_seq = N_Z * N_Y * N_CORE
    section_idx = lax.axis_index("section")
    core = lax.axis_index("core")
    tiles = feats.shape[0]
    channels = feats.shape[3]
    half = channels // N_CORE
    share = w_up.shape[0]

    bias_rows = jnp.broadcast_to(b_up[None, :], (16, share))
    block = pack(core, w_up, w_down, w_head, w_in, bias_rows)
    left = rotate(block, "section", N_SECTION, 1)
    right = rotate(block, "section", N_SECTION, -1)
    left, right, low_in, high_in = lax.optimization_barrier(
        (left, right, left[: 2 * share], right[2 * share :])
    )
    low = rotate(low_in, "section", N_SECTION, 1)
    high = rotate(high_in, "section", N_SECTION, -1)
    left_swap = rotate(left, "core", N_CORE, 1)
    right_swap = rotate(right, "core", N_CORE, 1)
    low_swap = rotate(low, "core", N_CORE, 1)
    high_swap = rotate(high, "core", N_CORE, 1)

    slot_total = tiles + prior.shape[0]
    q_rows = ROWS // n_section
    capacity = -(-slot_total // n_seq)
    slot_ids = jnp.arange(slot_total)
    live_mask = slot_ids < tiles + counts[0]
    dest_shard = positions // ROWS
    row_in = positions % ROWS - section_idx * q_rows
    earlier = (
        (dest_shard[None, :] == dest_shard[:, None])
        & (slot_ids[None, :] < slot_ids[:, None])
        & live_mask[None, :]
    )
    within = jnp.sum(earlier.astype(jnp.int32), axis=1)
    bucket = jnp.where(live_mask, dest_shard * capacity + within, -1)
    row_code = jnp.broadcast_to((row_in + 1).astype(BF16)[:, None], (slot_total, 128))

    normed_maps = conv_norm(feats, dw_weight, dw_bias, ln1_gain)
    feat_mean = jnp.mean(feats.astype(F32), axis=(1, 2))
    where = jnp.stack(
        [core, section_idx, (section_idx + 3) % 4, (section_idx + 1) % 4, (section_idx + 2) % 4]
    ).astype(jnp.int32)
    row = lambda vec: vec[None, :]
    hid, x_prior = local_call(
        early_kernel,
        (
            jax.ShapeDtypeStruct((3, tiles, share), F32),
            jax.ShapeDtypeStruct((prior.shape[0], channels), F32),
        ),
        [],
        2_000_000_000,
        6_000_000,
        where, normed_maps, w_up, row(b_up), w_in, prior, left, right, left_swap, right_swap,
    )
    payload = local_call(
        late_kernel,
        jax.ShapeDtypeStruct((n_seq * capacity, channels + 128), BF16),
        [pltpu.VMEM((slot_total, channels), F32)],
        2_000_000_000,
        8_000_000,
        where, normed_maps, prior, hid, x_prior, feat_mean, row(layer_scale), row(b_down),
        row(lnf_gain), row(bucket), row_code, w_down, w_head, w_in, left, right, left_swap,
        right_swap, low, high, low_swap, high_swap,
    )

    got = lax.all_to_all(
        payload.reshape(n_seq, capacity, payload.shape[1]), SEQ_AXES, 0, 0, tiled=True
    ).reshape(n_seq * capacity, payload.shape[1])
    code = got[:, channels].astype(F32)
    placer = (jnp.arange(1, q_rows + 1).astype(F32)[:, None] == code[None, :]).astype(BF16)
    x_local = dot(placer, got[:, :channels]).astype(BF16)
    x_rows = spread(x_local, "section", n_section).reshape(ROWS, channels)

    heads_here = w_qkv.shape[1] // (3 * HS)
    width = heads_here * HS
    stride_rows = ROWS // RB
    my_offsets = lax.dynamic_slice_in_dim(offsets, section_idx * heads_here, heads_here)
    off_lane = row(jnp.repeat(my_offsets, HS))
    w_q, w_k, w_v = (w_qkv[:, part * width : (part + 1) * width] for part in range(3))
    small = lambda rows, kind: jax.ShapeDtypeStruct((rows, width), kind)
    q, k, v, far_q, far_kv = vmem_call(
        project_kernel,
        (small(ROWS, BF16),) * 3
        + (small(stride_rows, F32), jax.ShapeDtypeStruct((stride_rows, 2 * width), BF16)),
        300_000_000,
        2_000_000,
        0,
        x_rows, row(ln_gain), w_q, w_k, w_v, row(jnp.tile(qn_gain, heads_here)),
        row(jnp.tile(kn_gain, heads_here)), off_lane,
    )
    z_kv = spread(far_kv, "z", N_Z).reshape(N_Z * stride_rows, 2 * width)
    half_kv = lax.all_gather(z_kv, "y", axis=0, tiled=True)
    other_kv = rotate(half_kv, "core", N_CORE, 1)
    den, num, far_den, far_num = vmem_call(
        near_kernel,
        (small(ROWS, F32),) * 2 + (small(stride_rows, F32),) * 2,
        150_000_000,
        2_000_000,
        250_000,
        q, k, v, far_q, half_kv,
    )
    width_part = channels // n_section
    partial_out = vmem_call(
        far_kernel,
        jax.ShapeDtypeStruct((channels, ROWS), BF16),
        150_000_000,
        2_000_000,
        50_000,
        far_q, other_kv, off_lane, den, num, far_den, far_num,
        jnp.transpose(w_out),
    )
    parts = lax.all_to_all(
        partial_out.reshape(n_section, width_part, ROWS), "section", 0, 0, tiled=True
    )
    residual = lax.dynamic_slice_in_dim(x_rows, section_idx * width_part, width_part, 1)
    total = jnp.transpose(residual).astype(F32) + jnp.sum(parts.astype(F32), axis=0)
    return jnp.transpose(total.astype(BF16))


def solution(mesh):
    fine = Mesh(
        mesh.devices.reshape(N_SECTION, N_Z, N_Y, N_CORE), ("section",) + SEQ_AXES
    )
    both = ("section",) + SEQ_AXES
    placed = (
        P(both, None, None, None),
        P(),
        P(),
        P(),
        P("section", None),
        P("section"),
        P("section", None),
        P(),
        P(),
        P(),
        P(None, "section"),
        P(both, None),
        P(both),
        P(both),
        P("section", None),
        P(),
        P(None, "section"),
        P(),
        P(),
        P(),
        P("section", None),
    )
    return jax.shard_map(
        shards, mesh=fine, in_specs=placed, out_specs=P(SEQ_AXES, "section"), check_vma=False
    )
```

time: 258 us -> 201 us (0.78)
  matrix products: 24.8 us -> 0.24 us
  waiting for transfers between devices: 85 us -> 66.2 us
  between operations: 14.9 us -> 1.29 us
  Pallas kernels: 3.23 us -> 15.4 us
  local copies, waits for them, and re-layouts: 14.6 us -> 7.94 us
  other arithmetic: 21 us -> 15.5 us
  blocking collectives: 28 us -> 31.1 us
  starting transfers between devices: 65 us -> 62.1 us
    all_gather x1 -> x0, waiting for transfers between devices: 27.1 us -> none  [shards(): all_kv = lax.all_gather(z_kv, ('y', 'core'), axis=0, tiled=True)]
    dot_general x18 -> x1, matrix products: 18.3 us -> 0.24 us  [dot(): return jnp.dot(a, b, preferred_element_type=F32)]
    pallas_call x1 -> x6, Pallas kernels: 3.23 us -> 15.4 us  [the longest x2 9.4 us: local_call(): pl.pallas_call(body, in_specs=[pl.BlockSpec(memory_space=pltpu.SMEM)] + [...]
    dot_general x7 -> x0, matrix products: 6.56 us -> none  [the longest x1 1.65 us: shards(): jnp.einsum('ahd,bhd->hab', far_q, piece_k, preferred_element_type=F32)]
    ppermute x10 -> x9, waiting for transfers between devices: 18.5 us -> 24.9 us  [rotate(): lax.ppermute(block, axis, [(i, (i + step) % size) for i in range(size)])]
    ppermute x10 -> x9, starting transfers between devices: 41.2 us -> 35.4 us  [rotate(): lax.ppermute(block, axis, [(i, (i + step) % size) for i in range(size)])]
    dynamic_slice x5 -> x0, local copies, waits for them, and re-layouts: 3.32 us -> none  [the longest x2 2.31 us: mine(): return lax.dynamic_slice_in_dim(matrix, core * half, half, axis)]
    all_to_all x1 -> x2, starting transfers between devices: 3.97 us -> 7.1 us  [the longest x1 3.64 us: spread(): lax.all_to_all(jnp.broadcast_to(block[None], (size,) + block.shape), axis...]
  transfers between devices with their start and end apart: 13 -> 12, of which waited for: 6 -> 7; matrix products, arithmetic and copies ran while one was open for 11% -> 9% of each run, Pallas kernels for 1% -> 2%
where the time goes in v2:
time: 201 us; the launch traced here: 200 us
  waiting for transfers between devices  66.2 us (33%)
  starting transfers between devices  62.1 us (31%)
  blocking collectives  31.1 us (15%)
  other arithmetic  15.5 us (8%)
  Pallas kernels  15.4 us (8%)
  local copies, waits for them, and re-layouts  7.94 us (4%)
    ppermute x9, starting transfers between devices, rotate(): lax.ppermute(block, axis, [(i, (i + step) % size) for i in range(size)])  35.4 us
    all_to_all x1, waiting for transfers between devices, shards(): lax.all_to_all(payload.reshape(n_seq, capacity, payload.shape[1]), SEQ_AX...  28.1 us
    ppermute x9, waiting for transfers between devices, rotate(): lax.ppermute(block, axis, [(i, (i + step) % size) for i in range(size)])  24.9 us
    all_to_all x1, starting transfers between devices, shards(): lax.all_to_all(payload.reshape(n_seq, capacity, payload.shape[1]), SEQ_AX...  19.6 us
    all_to_all x1, blocking collectives, spread(): lax.all_to_all(jnp.broadcast_to(block[None], (size,) + block.shape), axis...  19.4 us
    all_gather x1, blocking collectives, shards(): half_kv = lax.all_gather(z_kv, 'y', axis=0, tiled=True)  11.7 us
    reduce_sum x1, other arithmetic, layer_norm(): row_mean = jnp.mean(values, axis=-1, keepdims=True)  10.2 us
    pallas_call x2, Pallas kernels, local_call(): pl.pallas_call(body, in_specs=[pl.BlockSpec(memory_space=pltpu.SMEM)] + [...  9.4 us
  transfers between devices with their start and end apart: 12, of which 7 were waited for; matrix products, arithmetic and copies ran while one was open for 9% of the time, Pallas kernels for 2%

profile of v2, /device:TPU:1, one launch (start us, length us, event | category | flops | bytes accessed | tf_op | source)
XLA Modules:
  0.0 199.8 jit_solution(10527291909532758533)
XLA Ops:
  1.3 2.4 %shard_map.199 = bf16[1552,384]{1,0:T(8,128)(2,1)} custom-call(s32[1]{0:T(128)} %bitcast.core_ref, bf16[384,768]{1,0:T(8,128)(2,1)} %up.1, bf16[384,768]{1,0:T(8,128)(2,1)} %w_down.3, bf16[768,384]{1,0:T(8,128)(2,1)} %w_head.3, bf16[384,768]{1,0:T(8,128)(2,1)} %w_in.5, bf16[16,384]{1,0:T(8,128)(2,1)} %broadcast_in_dim.25.bias_rows), custom_call_target="tpu_custom_call" | custom-call | bytes 2359296 | tf_op jit(solution)/shard_map/pallas_call | solution.py:94
  3.7 5.2 %collective-permute-start.1 = (bf16[1552,384]{1,0:T(8,128)(2,1)}, bf16[1552,384]{1,0:T(8,128)(2,1)S(1)}, u32[]{:S(2)}, u32[]{:S(2)}) collective-permute-start(bf16[1552,384]{1,0:T(8,128)(2,1)} %shard_map.199), channel_id=1, source_target_pairs={{0,384},{128,0},{256,128},{384,256},{1,385},{129,1},{257,129},{385... | collective-permute-start | bytes 3575816 | tf_op jit(solution)/shard_map/ppermute | solution.py:47
  8.9 1.9 collective-permute-start
  11.5 10.2 %fusion.105 = (f32[8,8,8]{2,1,0:T(8,128)S(1)}, f32[8,8,8,768]{3,2,1,0:T(8,128)}) fusion(f32[768]{0:T(1024)S(1)} %get-tuple-element.82, f32[768]{0:T(1024)S(1)} %get-tuple-element.83, f32[768]{0:T(1024)S(1)} %get-tuple-element.36, f32[768]{0:T(1024)S(1)} %get-tuple-element.37, f32[768]{0:T(1024)S(1)} %get-tuple-element.38, f32[768]{0:T(1024)S(1)} %get-tuple-element.39, ...), kind=kLoop, calls=%fused_computation.225 | loop fusion | flops 38927872 | bytes 3301376 | tf_op jit(solution)/shard_map/reduce_sum | solution.py:22
  24.3 7.2 %collective-permute-done.1.right = bf16[1552,384]{1,0:T(8,128)(2,1)S(1)} collective-permute-done((bf16[1552,384]{1,0:T(8,128)(2,1)}, bf16[1552,384]{1,0:T(8,128)(2,1)S(1)}, u32[]{:S(2)}, u32[]{:S(2)}) %collective-permute-start.1) | collective-permute-done | bytes 1191968 | tf_op jit(solution)/shard_map/ppermute | solution.py:47
  32.4 4.0 %collective-permute-done.left = bf16[1552,384]{1,0:T(8,128)(2,1)S(1)} collective-permute-done((bf16[1552,384]{1,0:T(8,128)(2,1)}, bf16[1552,384]{1,0:T(8,128)(2,1)S(1)}, u32[]{:S(2)}, u32[]{:S(2)}) %collective-permute-start) | collective-permute-done | bytes 1191968 | tf_op jit(solution)/shard_map/ppermute | solution.py:47
  37.3 6.4 %collective-permute-start.2 = (bf16[1552,384]{1,0:T(8,128)(2,1)S(1)}, bf16[1552,384]{1,0:T(8,128)(2,1)}, u32[]{:S(2)}, u32[]{:S(2)}) collective-permute-start(bf16[1552,384]{1,0:T(8,128)(2,1)S(1)} %collective-permute-done.left), channel_id=1, source_target_pairs={{0,1},{1,0},{2,3},{3,2},{4,5},{5,4},{6,7},{7,6},{8,9},{9,8},{10,11... | collective-permute-start | bytes 3575816 | tf_op jit(solution)/shard_map/ppermute | solution.py:47
  43.7 1.9 collective-permute-start.3
  45.8 1.9 collective-permute-start.5
  47.9 3.5 %collective-permute-start.4 = (bf16[768,384]{1,0:T(8,128)(2,1)}, bf16[768,384]{1,0:T(8,128)(2,1)S(1)}, u32[]{:S(2)}, u32[]{:S(2)}) collective-permute-start(bf16[768,384]{1,0:T(8,128)(2,1)} %slice.417), channel_id=1, source_target_pairs={{0,128},{128,256},{256,384},{384,0},{1,129},{129,257},{257,385},{3... | collective-permute-start | bytes 1769480 | tf_op jit(solution)/shard_map/ppermute | solution.py:47
  52.7 13.0 %collective-permute-done.4.low = bf16[768,384]{1,0:T(8,128)(2,1)S(1)} collective-permute-done((bf16[768,384]{1,0:T(8,128)(2,1)}, bf16[768,384]{1,0:T(8,128)(2,1)S(1)}, u32[]{:S(2)}, u32[]{:S(2)}) %collective-permute-start.4) | collective-permute-done | bytes 589856 | tf_op jit(solution)/shard_map/ppermute | solution.py:47
  65.7 3.2 %collective-permute-start.6 = (bf16[768,384]{1,0:T(8,128)(2,1)S(1)}, bf16[768,384]{1,0:T(8,128)(2,1)S(1)}, u32[]{:S(2)}, u32[]{:S(2)}) collective-permute-start(bf16[768,384]{1,0:T(8,128)(2,1)S(1)} %collective-permute-done.4.low), channel_id=1, source_target_pairs={{0,1},{1,0},{2,3},{3,2},{4,5},{5,4},{6,7},{7,6},{8,9},{9,8},{10,11... | collective-permute-start | bytes 1769480 | tf_op jit(solution)/shard_map/ppermute | solution.py:47
  69.0 1.9 collective-permute-start.7
  72.7 4.0 %shard_map.200 = (f32[3,8,384]{2,1,0:T(8,128)S(1)}, f32[152,768]{1,0:T(8,128)S(1)}) custom-call(s32[5]{0:T(128)S(1)} %stack.23.where, bf16[512,768]{1,0:T(8,128)(2,1)S(1)} %bitcast.16, bf16[384,768]{1,0:T(8,128)(2,1)S(1)} %copy-done.6, bf16[1,384]{1,0:T(2,128)(2,1)S(1)} %broadcast_in_dim.24.bias, bf16[384,768]{1,0:T(8,128)(2,1)S(1)} %copy-done.3, ...), custom_call_target="tpu_custom_call" | custom-call | flops 2000000000 | bytes 6000000 | tf_op jit(solution)/shard_map/pallas_call | solution.py:189
  76.9 5.4 %shard_map.201 = bf16[256,896]{1,0:T(8,128)(2,1)S(1)} custom-call(s32[5]{0:T(128)S(1)} %stack.23.where, bf16[512,768]{1,0:T(8,128)(2,1)} %bitcast.17, bf16[152,1536]{1,0:T(8,128)(2,1)S(1)} %copy-done.7, f32[3,8,384]{2,1,0:T(8,128)S(1)} %get-tuple-element.22.hid, f32[152,768]{1,0:T(8,128)S(1)} %get-tuple-element.23.x_prior, ...), custom_call_target="tpu_custom_call" | custom-call | flops 2000000000 | bytes 8000000 | tf_op jit(solution)/shard_map/pallas_call | solution.py:189
  83.2 19.6 %all-to-all-start = ((bf16[128,2,896]{2,1,0:T(2,128)(2,1)}), bf16[128,2,896]{2,1,0:T(2,128)(2,1)S(1)}, u32[]{:S(2)}, u32[]{:S(2)}) async-start(bf16[128,2,896]{2,1,0:T(2,128)(2,1)} %reshape.108), calls=%async_computation | async-start | bytes 917504 | tf_op jit(solution)/shard_map/all_to_all | solution.py:391
  102.8 28.1 %all-to-all-done = bf16[128,2,896]{2,1,0:T(2,128)(2,1)S(1)} async-done(((bf16[128,2,896]{2,1,0:T(2,128)(2,1)}), bf16[128,2,896]{2,1,0:T(2,128)(2,1)S(1)}, u32[]{:S(2)}, u32[]{:S(2)}) %all-to-all-start) | async-done | bytes 458784 | tf_op jit(solution)/shard_map/all_to_all | solution.py:391
  132.2 3.6 %all-to-all-start.1 = ((bf16[4,64,768]{2,1,0:T(8,128)(2,1)}), bf16[4,64,768]{2,1,0:T(8,128)(2,1)S(1)}, u32[]{:S(2)}, u32[]{:S(2)}) async-start(bf16[4,64,768]{2,1,0:T(8,128)(2,1)} %broadcast_in_dim.31), calls=%async_computation.1 | async-start | bytes 786432 | tf_op jit(solution)/shard_map/all_to_all | solution.py:51
  137.0 5.4 %all-to-all-done.1 = bf16[4,64,768]{2,1,0:T(8,128)(2,1)S(1)} async-done(((bf16[4,64,768]{2,1,0:T(8,128)(2,1)}), bf16[4,64,768]{2,1,0:T(8,128)(2,1)S(1)}, u32[]{:S(2)}, u32[]{:S(2)}) %all-to-all-start.1) | async-done | bytes 393248 | tf_op jit(solution)/shard_map/all_to_all | solution.py:51
  143.3 19.4 %all_to_all.20 = bf16[16,16,384]{2,1,0:T(8,128)(2,1)S(1)} all-to-all(bf16[16,16,384]{2,1,0:T(8,128)(2,1)S(1)} %broadcast_in_dim.34), channel_id=1, replica_groups=mesh['section'=4,'z'=16,'y'=4,'core'=2] {'z'}, dimensions={0} | all-to-all | bytes 393216 | tf_op jit(solution)/shard_map/all_to_all | solution.py:51
  162.8 11.7 %all_gather.3.kv = bf16[1024,384]{1,0:T(8,128)(2,1)S(1)} all-gather(bf16[256,384]{1,0:T(8,128)(2,1)S(1)} %bitcast.22), channel_id=1, replica_groups=mesh['section'=4,'z'=16,'y'=4,'core'=2] {'y'}, dimensions={0}, use_global_device_ids=true | all-gather | bytes 983040 | tf_op jit(solution)/shard_map/all_gather | solution.py:417
  174.4 9.4 %collective-permute-start.8 = (bf16[1024,384]{1,0:T(8,128)(2,1)S(1)}, bf16[1024,384]{1,0:T(8,128)(2,1)S(1)}, u32[]{:S(2)}, u32[]{:S(2)}) collective-permute-start(bf16[1024,384]{1,0:T(8,128)(2,1)S(1)} %all_gather.3.kv), channel_id=1, source_target_pairs={{0,1},{1,0},{2,3},{3,2},{4,5},{5,4},{6,7},{7,6},{8,9},{9,8},{10,11... | collective-permute-start | bytes 2359304 | tf_op jit(solution)/shard_map/ppermute | solution.py:47
  187.5 3.5 %all-to-all-start.3 = ((bf16[4,192,256]{2,1,0:T(8,128)(2,1)}), bf16[4,192,256]{2,1,0:T(8,128)(2,1)S(1)}, u32[]{:S(2)}, u32[]{:S(2)}) async-start(bf16[4,192,256]{2,1,0:T(8,128)(2,1)} %bitcast.11), calls=%async_computation.3 | async-start | bytes 786432 | tf_op jit(solution)/shard_map/all_to_all | solution.py:437
  191.0 7.8 %all-to-all-done.3 = bf16[4,192,256]{2,1,0:T(8,128)(2,1)S(1)} async-done(((bf16[4,192,256]{2,1,0:T(8,128)(2,1)}), bf16[4,192,256]{2,1,0:T(8,128)(2,1)S(1)}, u32[]{:S(2)}, u32[]{:S(2)}) %all-to-all-start.3) | async-done | bytes 393248 | tf_op jit(solution)/shard_map/all_to_all | solution.py:437
  (102 shorter events, 17.9 us)
Async XLA Ops:
  3.7 27.7 %collective-permute-start.1 = (bf16[1552,384]{1,0:T(8,128)(2,1)}, bf16[1552,384]{1,0:T(8,128)(2,1)S(1)}, u32[]{:S(2)}, u32[]{:S(2)}) collective-permute-start(bf16[1552,384]{1,0:T(8,128)(2,1)} %shard_map.199), channel_id=1, source_target_pairs={{0,384},{128,0},{256,128},{384,256},{1,385},{129,1},{257,129},{385... | collective-permute-start | bytes 3575816 | tf_op jit(solution)/shard_map/ppermute | solution.py:47
  8.9 27.5 %collective-permute-start = (bf16[1552,384]{1,0:T(8,128)(2,1)}, bf16[1552,384]{1,0:T(8,128)(2,1)S(1)}, u32[]{:S(2)}, u32[]{:S(2)}) collective-permute-start(bf16[1552,384]{1,0:T(8,128)(2,1)} %shard_map.199), channel_id=1, source_target_pairs={{0,128},{128,256},{256,384},{384,0},{1,129},{129,257},{257,385},{3... | collective-permute-start | bytes 3575816 | tf_op jit(solution)/shard_map/ppermute | solution.py:47
  11.5 10.9 %copy-start.14 = (f32[768]{0:T(1024)S(1)}, f32[768]{0:T(1024)}, u32[]{:S(2)}) copy-start(f32[768]{0:T(1024)} %param.29) | copy-start | bytes 9220
  11.5 11.0 %copy-start.15 = (f32[768]{0:T(1024)S(1)}, f32[768]{0:T(1024)}, u32[]{:S(2)}) copy-start(f32[768]{0:T(1024)} %param.28) | copy-start | bytes 9220
  11.5 11.0 %copy-start.16 = (f32[768]{0:T(1024)S(1)}, f32[768]{0:T(1024)}, u32[]{:S(2)}) copy-start(f32[768]{0:T(1024)} %param.30) | copy-start | bytes 9220
  24.3 46.6 %copy-start.13 = (f32[768]{0:T(1024)S(1)}, f32[768]{0:T(1024)}, u32[]{:S(2)}) copy-start(f32[768]{0:T(1024)} %param.24) | copy-start | bytes 9220
  31.4 41.2 %copy-start.1 = (bf16[1552,384]{1,0:T(8,128)(2,1)}, bf16[1552,384]{1,0:T(8,128)(2,1)S(1)}, u32[]{:S(2)}) copy-start(bf16[1552,384]{1,0:T(8,128)(2,1)S(1)} %collective-permute-done.1.right) | copy-start | bytes 3575812
  36.4 36.3 %copy-start.2 = (bf16[1552,384]{1,0:T(8,128)(2,1)}, bf16[1552,384]{1,0:T(8,128)(2,1)S(1)}, u32[]{:S(2)}) copy-start(bf16[1552,384]{1,0:T(8,128)(2,1)S(1)} %collective-permute-done.left) | copy-start | bytes 3575812
  37.3 35.3 %collective-permute-start.2 = (bf16[1552,384]{1,0:T(8,128)(2,1)S(1)}, bf16[1552,384]{1,0:T(8,128)(2,1)}, u32[]{:S(2)}, u32[]{:S(2)}) collective-permute-start(bf16[1552,384]{1,0:T(8,128)(2,1)S(1)} %collective-permute-done.left), channel_id=1, source_target_pairs={{0,1},{1,0},{2,3},{3,2},{4,5},{5,4},{6,7},{7,6},{8,9},{9,8},{10,11... | collective-permute-start | bytes 3575816 | tf_op jit(solution)/shard_map/ppermute | solution.py:47
  43.7 28.9 %collective-permute-start.3 = (bf16[1552,384]{1,0:T(8,128)(2,1)S(1)}, bf16[1552,384]{1,0:T(8,128)(2,1)}, u32[]{:S(2)}, u32[]{:S(2)}) collective-permute-start(bf16[1552,384]{1,0:T(8,128)(2,1)S(1)} %collective-permute-done.1.right), channel_id=1, source_target_pairs={{0,1},{1,0},{2,3},{3,2},{4,5},{5,4},{6,7},{7,6},{8,9},{9,8},{10,11... | collective-permute-start | bytes 3575816 | tf_op jit(solution)/shard_map/ppermute | solution.py:47
  45.8 23.1 %collective-permute-start.5 = (bf16[784,384]{1,0:T(8,128)(2,1)}, bf16[784,384]{1,0:T(8,128)(2,1)S(1)}, u32[]{:S(2)}, u32[]{:S(2)}) collective-permute-start(bf16[784,384]{1,0:T(8,128)(2,1)} %slice.418), channel_id=1, source_target_pairs={{0,384},{128,0},{256,128},{384,256},{1,385},{129,1},{257,129},{385... | collective-permute-start | bytes 1806344 | tf_op jit(solution)/shard_map/ppermute | solution.py:47
  47.9 24.8 %copy-start.3 = (bf16[384,768]{1,0:T(8,128)(2,1)S(1)}, bf16[384,768]{1,0:T(8,128)(2,1)}, u32[]{:S(2)}) copy-start(bf16[384,768]{1,0:T(8,128)(2,1)} %w_in.5) | copy-start | bytes 1769476
  47.9 24.8 %copy-start.6 = (bf16[384,768]{1,0:T(8,128)(2,1)S(1)}, bf16[384,768]{1,0:T(8,128)(2,1)}, u32[]{:S(2)}) copy-start(bf16[384,768]{1,0:T(8,128)(2,1)} %up.1) | copy-start | bytes 1769476
  47.9 24.8 %copy-start.7 = (bf16[152,1536]{1,0:T(8,128)(2,1)S(1)}, bf16[152,1536]{1,0:T(8,128)(2,1)}, u32[]{:S(2)}) copy-start(bf16[152,1536]{1,0:T(8,128)(2,1)} %prior.3) | copy-start | bytes 1400836
  47.9 17.8 %collective-permute-start.4 = (bf16[768,384]{1,0:T(8,128)(2,1)}, bf16[768,384]{1,0:T(8,128)(2,1)S(1)}, u32[]{:S(2)}, u32[]{:S(2)}) collective-permute-start(bf16[768,384]{1,0:T(8,128)(2,1)} %slice.417), channel_id=1, source_target_pairs={{0,128},{128,256},{256,384},{384,0},{1,129},{129,257},{257,385},{3... | collective-permute-start | bytes 1769480 | tf_op jit(solution)/shard_map/ppermute | solution.py:47
  65.7 11.1 %collective-permute-start.6 = (bf16[768,384]{1,0:T(8,128)(2,1)S(1)}, bf16[768,384]{1,0:T(8,128)(2,1)S(1)}, u32[]{:S(2)}, u32[]{:S(2)}) collective-permute-start(bf16[768,384]{1,0:T(8,128)(2,1)S(1)} %collective-permute-done.4.low), channel_id=1, source_target_pairs={{0,1},{1,0},{2,3},{3,2},{4,5},{5,4},{6,7},{7,6},{8,9},{9,8},{10,11... | collective-permute-start | bytes 1769480 | tf_op jit(solution)/shard_map/ppermute | solution.py:47
  69.0 7.8 %collective-permute-start.7 = (bf16[784,384]{1,0:T(8,128)(2,1)S(1)}, bf16[784,384]{1,0:T(8,128)(2,1)S(1)}, u32[]{:S(2)}, u32[]{:S(2)}) collective-permute-start(bf16[784,384]{1,0:T(8,128)(2,1)S(1)} %collective-permute-done.5.high), channel_id=1, source_target_pairs={{0,1},{1,0},{2,3},{3,2},{4,5},{5,4},{6,7},{7,6},{8,9},{9,8},{10,11... | collective-permute-start | bytes 1806344 | tf_op jit(solution)/shard_map/ppermute | solution.py:47
  83.2 47.7 %all-to-all-start = ((bf16[128,2,896]{2,1,0:T(2,128)(2,1)}), bf16[128,2,896]{2,1,0:T(2,128)(2,1)S(1)}, u32[]{:S(2)}, u32[]{:S(2)}) async-start(bf16[128,2,896]{2,1,0:T(2,128)(2,1)} %reshape.108), calls=%async_computation | async-start | bytes 917504 | tf_op jit(solution)/shard_map/all_to_all | solution.py:391
  102.8 33.1 %copy-start.22 = (s32[12]{0:T(128)S(1)}, s32[12]{0:T(128)}, u32[]{:S(2)}) copy-start(s32[12]{0:T(128)} %param.40) | copy-start | bytes 148
  102.8 33.3 %copy-start.9 = (bf16[768,576]{0,1:T(8,128)(2,1)S(1)}, bf16[768,576]{0,1:T(8,128)(2,1)}, u32[]{:S(2)}) copy-start(bf16[768,576]{0,1:T(8,128)(2,1)} %param.37) | copy-start | bytes 2654212
  132.2 10.2 %all-to-all-start.1 = ((bf16[4,64,768]{2,1,0:T(8,128)(2,1)}), bf16[4,64,768]{2,1,0:T(8,128)(2,1)S(1)}, u32[]{:S(2)}, u32[]{:S(2)}) async-start(bf16[4,64,768]{2,1,0:T(8,128)(2,1)} %broadcast_in_dim.31), calls=%async_computation.1 | async-start | bytes 786432 | tf_op jit(solution)/shard_map/all_to_all | solution.py:51
  142.4 41.5 %copy-start.10 = (bf16[192,768]{1,0:T(8,128)(2,1)S(1)}, bf16[192,768]{1,0:T(8,128)(2,1)}, u32[]{:S(2)}) copy-start(bf16[192,768]{1,0:T(8,128)(2,1)} %param.41) | copy-start | bytes 884740
  174.4 11.3 %collective-permute-start.8 = (bf16[1024,384]{1,0:T(8,128)(2,1)S(1)}, bf16[1024,384]{1,0:T(8,128)(2,1)S(1)}, u32[]{:S(2)}, u32[]{:S(2)}) collective-permute-start(bf16[1024,384]{1,0:T(8,128)(2,1)S(1)} %all_gather.3.kv), channel_id=1, source_target_pairs={{0,1},{1,0},{2,3},{3,2},{4,5},{5,4},{6,7},{7,6},{8,9},{9,8},{10,11... | collective-permute-start | bytes 2359304 | tf_op jit(solution)/shard_map/ppermute | solution.py:47
  187.5 11.3 %all-to-all-start.3 = ((bf16[4,192,256]{2,1,0:T(8,128)(2,1)}), bf16[4,192,256]{2,1,0:T(8,128)(2,1)S(1)}, u32[]{:S(2)}, u32[]{:S(2)}) async-start(bf16[4,192,256]{2,1,0:T(8,128)(2,1)} %bitcast.11), calls=%async_computation.3 | async-start | bytes 786432 | tf_op jit(solution)/shard_map/all_to_all | solution.py:437
  (11 other events, 54.8 us)

commit v3 on v2

--- a/solution.py
+++ b/solution.py
@@ -69,40 +69,46 @@
     return ref[:, pl.ds(pl.multiple_of(index * width, 128), width)]
 
 
-def pack_kernel(core_ref, w_up, w_down, w_head, w_in, bias_rows, out, sems):
+def pack_kernel(core_ref, w_up, w_down, w_head, w_in, bias, first, second, sems):
     n = w_up.shape[0]
     start = pl.multiple_of(core_ref[0] * n, n)
-    parts = (
-        w_up.at[:, pl.ds(start, n)],
-        w_down.at[:, pl.ds(start, n)],
-        w_head.at[pl.ds(start, n), :],
-        w_in.at[:, pl.ds(start, n)],
-    )
     copies = [
-        pltpu.make_async_copy(part, out.at[pl.ds(k * n, n), :], sems.at[k])
-        for k, part in enumerate(parts)
+        pltpu.make_async_copy(part, out.at[pl.ds(k * n, n), :], sems.at[k, slot])
+        for out, slot, k, part in (
+            (first, 0, 0, w_up.at[:, pl.ds(start, n)]),
+            (first, 0, 1, w_down.at[:, pl.ds(start, n)]),
+            (second, 1, 0, w_head.at[pl.ds(start, n), :]),
+            (second, 1, 1, w_in.at[:, pl.ds(start, n)]),
+        )
     ]
-    copies.append(pltpu.make_async_copy(bias_rows, out.at[pl.ds(4 * n, 16), :], sems.at[4]))
     for copy in copies:
         copy.start()
+    second[2 * n :, :] = jnp.broadcast_to(bias[...][None, :], (16, n))
     for copy in copies:
         copy.wait()
 
 
-def pack(core, w_up, w_down, w_head, w_in, bias_rows):
+def pack(core, w_up, w_down, w_head, w_in, bias):
     n = w_up.shape[0]
+    vmem = pl.BlockSpec(memory_space=pltpu.VMEM)
     return pl.pallas_call(
         pack_kernel,
-        in_specs=[pl.BlockSpec(memory_space=pltpu.SMEM)] + [pl.BlockSpec(memory_space=pl.ANY)] * 5,
-        out_specs=pl.BlockSpec(memory_space=pltpu.VMEM),
-        out_shape=jax.ShapeDtypeStruct((4 * n + 16, n), BF16),
-        scratch_shapes=[pltpu.SemaphoreType.DMA((5,))],
+        in_specs=[pl.BlockSpec(memory_space=pltpu.SMEM)]
+        + [pl.BlockSpec(memory_space=pl.ANY)] * 4
+        + [vmem],
+        out_specs=(vmem, vmem),
+        out_shape=(
+            jax.ShapeDtypeStruct((2 * n, n), BF16),
+            jax.ShapeDtypeStruct((2 * n + 16, n), BF16),
+        ),
+        scratch_shapes=[pltpu.SemaphoreType.DMA((2, 2))],
         cost_estimate=pl.CostEstimate(flops=0, bytes_accessed=4 * n * n * 4, transcendentals=0),
-    )(core.astype(jnp.int32)[None], w_up, w_down, w_head, w_in, bias_rows)
+    )(core.astype(jnp.int32)[None], w_up, w_down, w_head, w_in, bias)
 
 
 def early_kernel(
-    where, maps, up, bias, w_in, prior, left, right, left_swap, right_swap, hid, x_prior
+    where, maps, up, bias, w_in, prior,
+    left, right, left_swap, right_swap, left2, right2, left2_swap, right2_swap, hid, x_prior,
 ):
     core = where[0]
     n = up.shape[0]
@@ -113,13 +119,14 @@
     own = dot(lanes(prior, where[1], n), w_in[...])
     x_a = jnp.zeros((prior.shape[0], n), F32)
     x_b = x_a
-    for slot, (a, b) in enumerate(((left, left_swap), (right, right_swap))):
+    sides = ((left, left_swap, left2, left2_swap), (right, right_swap, right2, right2_swap))
+    for slot, (a, b, a2, b2) in enumerate(sides):
         pre = lax.dot_general(maps_a, a[0:n, :], NT, preferred_element_type=F32)
         pre += lax.dot_general(maps_b, b[0:n, :], NT, preferred_element_type=F32)
-        hid[slot + 1] = gelu_mean(pre + a[4 * n : 4 * n + 1, :].astype(F32), tiles)
+        hid[slot + 1] = gelu_mean(pre + a2[2 * n : 2 * n + 1, :].astype(F32), tiles)
         columns = lanes(prior, where[slot + 2], n)
-        x_a += dot(columns, a[3 * n : 4 * n, :])
-        x_b += dot(columns, b[3 * n : 4 * n, :])
+        x_a += dot(columns, a2[n : 2 * n, :])
+        x_b += dot(columns, b2[n : 2 * n, :])
     x_prior[...] = own + natural(core, x_a, x_b)
 
 
@@ -129,8 +136,9 @@
 
 def late_kernel(
     where, maps, prior, hid, x_prior, feat_mean, layer_scale, b_down, lnf_gain, bucket, row_code,
-    w_down, w_head, w_in, left, right, left_swap, right_swap, low, high, low_swap, high_swap,
-    payload, slot_x,
+    w_down, w_head, w_in,
+    left, right, left_swap, right_swap, left2, right2, left2_swap, right2_swap,
+    low, high, low_swap, high_swap, payload, slot_x,
 ):
     core = where[0]
     n = w_down.shape[0]
@@ -169,12 +177,10 @@
     columns = lanes(prior, where[4], n)
     x_a, x_b = dot(emb, high[n : 2 * n, :]), dot(emb, high_swap[n : 2 * n, :])
     p_a, p_b = dot(columns, high[n : 2 * n, :]), dot(columns, high_swap[n : 2 * n, :])
-    for a, b in sides:
-        emb = (
-            dot(feature_a, a[2 * n : 3 * n, :]) + dot(feature_b, b[2 * n : 3 * n, :])
-        ).astype(BF16)
-        x_a += dot(emb, a[3 * n : 4 * n, :])
-        x_b += dot(emb, b[3 * n : 4 * n, :])
+    for a, b in ((left2, left2_swap), (right2, right2_swap)):
+        emb = (dot(feature_a, a[0:n, :]) + dot(feature_b, b[0:n, :])).astype(BF16)
+        x_a += dot(emb, a[n : 2 * n, :])
+        x_b += dot(emb, b[n : 2 * n, :])
     slot_x[0:tiles, :] = own + natural(core, x_a, x_b)
     slot_x[tiles:, :] = x_prior[...] + natural(core, p_a, p_b)
     places = lax.broadcasted_iota(jnp.int32, (payload.shape[0], bucket.shape[1]), 0)
@@ -262,7 +268,11 @@
     return back(den, rows, width), back(num[:, width:], rows, width)
 
 
-def near_kernel(q, k, v, far_q, kv, den, num, far_den, far_num):
+def near_kernel(where, q, k, v, far_q, kv, x, den, num, far_den, far_num, residual):
+    wanted = lax.broadcasted_iota(jnp.int32, (residual.shape[0], x.shape[1]), 0)
+    column = lax.broadcasted_iota(jnp.int32, (residual.shape[0], x.shape[1]), 1)
+    pick = jnp.where(column == wanted + where[1] * residual.shape[0], 1.0, 0.0).astype(BF16)
+    residual[...] = lax.dot_general(pick, x[...], NT, preferred_element_type=F32)
     rows, width = q.shape
     local_den, local_num = weigh(by_head(q[...]).astype(BF16), k[...], v[...])
     den[...] = back(local_den, rows, width)
@@ -284,6 +294,13 @@
     )
     attended = attended.astype(BF16)
     out[...] = lax.dot_general(w_out[...], attended, NT, preferred_element_type=F32).astype(BF16)
+
+
+def sum_kernel(residual, parts, out):
+    total = residual[...]
+    for part in range(parts.shape[0]):
+        total += parts[part].astype(F32)
+    out[...] = total.astype(BF16)
 
 
 def vmem_call(body, outs, flops, size, exps, *operands):
@@ -330,17 +347,20 @@
     half = channels // N_CORE
     share = w_up.shape[0]
 
-    bias_rows = jnp.broadcast_to(b_up[None, :], (16, share))
-    block = pack(core, w_up, w_down, w_head, w_in, bias_rows)
-    left = rotate(block, "section", N_SECTION, 1)
-    right = rotate(block, "section", N_SECTION, -1)
-    left, right, low_in, high_in = lax.optimization_barrier(
-        (left, right, left[: 2 * share], right[2 * share :])
-    )
-    low = rotate(low_in, "section", N_SECTION, 1)
-    high = rotate(high_in, "section", N_SECTION, -1)
+    first, second = pack(core, w_up, w_down, w_head, w_in, b_up)
+    left = rotate(first, "section", N_SECTION, 1)
+    right2 = rotate(second, "section", N_SECTION, -1)
+    left2 = rotate(second, "section", N_SECTION, 1)
+    right = rotate(first, "section", N_SECTION, -1)
+    normed_maps = conv_norm(feats, dw_weight, dw_bias, ln1_gain)
+    left, right2, normed_maps = lax.optimization_barrier((left, right2, normed_maps))
+    low = rotate(left, "section", N_SECTION, 1)
+    high = rotate(right2, "section", N_SECTION, -1)
+    left, right2, left2, right = lax.optimization_barrier((left, right2, left2, right))
     left_swap = rotate(left, "core", N_CORE, 1)
     right_swap = rotate(right, "core", N_CORE, 1)
+    left2_swap = rotate(left2, "core", N_CORE, 1)
+    right2_swap = rotate(right2, "core", N_CORE, 1)
     low_swap = rotate(low, "core", N_CORE, 1)
     high_swap = rotate(high, "core", N_CORE, 1)
 
@@ -360,7 +380,6 @@
     bucket = jnp.where(live_mask, dest_shard * capacity + within, -1)
     row_code = jnp.broadcast_to((row_in + 1).astype(BF16)[:, None], (slot_total, 128))
 
-    normed_maps = conv_norm(feats, dw_weight, dw_bias, ln1_gain)
     feat_mean = jnp.mean(feats.astype(F32), axis=(1, 2))
     where = jnp.stack(
         [core, section_idx, (section_idx + 3) % 4, (section_idx + 1) % 4, (section_idx + 2) % 4]
@@ -376,6 +395,7 @@
         2_000_000_000,
         6_000_000,
         where, normed_maps, w_up, row(b_up), w_in, prior, left, right, left_swap, right_swap,
+        left2, right2, left2_swap, right2_swap,
     )
     payload = local_call(
         late_kernel,
@@ -385,7 +405,7 @@
         8_000_000,
         where, normed_maps, prior, hid, x_prior, feat_mean, row(layer_scale), row(b_down),
         row(lnf_gain), row(bucket), row_code, w_down, w_head, w_in, left, right, left_swap,
-        right_swap, low, high, low_swap, high_swap,
+        right_swap, left2, right2, left2_swap, right2_swap, low, high, low_swap, high_swap,
     )
 
     got = lax.all_to_all(
@@ -416,15 +436,17 @@
     z_kv = spread(far_kv, "z", N_Z).reshape(N_Z * stride_rows, 2 * width)
     half_kv = lax.all_gather(z_kv, "y", axis=0, tiled=True)
     other_kv = rotate(half_kv, "core", N_CORE, 1)
-    den, num, far_den, far_num = vmem_call(
+    width_part = channels // n_section
+    den, num, far_den, far_num, residual = local_call(
         near_kernel,
-        (small(ROWS, F32),) * 2 + (small(stride_rows, F32),) * 2,
-        150_000_000,
+        (small(ROWS, F32),) * 2
+        + (small(stride_rows, F32),) * 2
+        + (jax.ShapeDtypeStruct((width_part, ROWS), F32),),
+        [],
+        2_000_000_000,
         2_000_000,
-        250_000,
-        q, k, v, far_q, half_kv,
-    )
-    width_part = channels // n_section
+        where, q, k, v, far_q, half_kv, x_rows,
+    )
     partial_out = vmem_call(
         far_kernel,
         jax.ShapeDtypeStruct((channels, ROWS), BF16),
@@ -437,9 +459,15 @@
     parts = lax.all_to_all(
         partial_out.reshape(n_section, width_part, ROWS), "section", 0, 0, tiled=True
     )
-    residual = lax.dynamic_slice_in_dim(x_rows, section_idx * width_part, width_part, 1)
-    total = jnp.transpose(residual).astype(F32) + jnp.sum(parts.astype(F32), axis=0)
-    return jnp.transpose(total.astype(BF16))
+    total = vmem_call(
+        sum_kernel,
+        jax.ShapeDtypeStruct((width_part, ROWS), BF16),
+        1_000_000,
+        1_000_000,
+        0,
+        residual, parts,
+    )
+    return jnp.transpose(total)
 
 
 def solution(mesh):

time: 201 us -> 198 us (0.985)
  waiting for transfers between devices: 66.2 us -> 47.6 us
  blocking collectives: 31.1 us -> 41.4 us
  starting transfers between devices: 62.1 us -> 69.3 us
  other arithmetic: 15.5 us -> 12.9 us
    ppermute x9 -> x13, waiting for transfers between devices: 24.9 us -> 14.1 us  [rotate(): lax.ppermute(block, axis, [(i, (i + step) % size) for i in range(size)])]
    ppermute x9 -> x13, starting transfers between devices: 35.4 us -> 46.2 us  [rotate(): lax.ppermute(block, axis, [(i, (i + step) % size) for i in range(size)])]
    all_to_all x0 -> x1, blocking collectives: none -> 10.3 us  [shards(): lax.all_to_all(partial_out.reshape(n_section, width_part, ROWS), 'section...]
    all_to_all x1 -> x0, waiting for transfers between devices: 7.79 us -> none  [shards(): lax.all_to_all(partial_out.reshape(n_section, width_part, ROWS), 'section...]
    all_to_all x1 -> x0, starting transfers between devices: 3.46 us -> none  [shards(): lax.all_to_all(partial_out.reshape(n_section, width_part, ROWS), 'section...]
    unnamed x50 -> x48, local copies, waits for them, and re-layouts: 0.88 us -> 4.29 us
    pallas_call x2 -> x3, Pallas kernels: 9.4 us -> 11.1 us  [local_call(): pl.pallas_call(body, in_specs=[pl.BlockSpec(memory_space=pltpu.SMEM)] + [...]
  transfers between devices with their start and end apart: 12 -> 15, of which waited for: 7 -> 4; matrix products, arithmetic and copies ran while one was open for 9% -> 8% of each run, Pallas kernels for 2% -> 3%
where the time goes in v3:
time: 198 us; the launch traced here: 197 us
  starting transfers between devices  69.3 us (35%)
  waiting for transfers between devices  47.6 us (24%)
  blocking collectives  41.4 us (21%)
  Pallas kernels  16.9 us (9%)
  other arithmetic  12.9 us (7%)
  local copies, waits for them, and re-layouts  7.27 us (4%)
    ppermute x13, starting transfers between devices, rotate(): lax.ppermute(block, axis, [(i, (i + step) % size) for i in range(size)])  46.2 us
    all_to_all x1, waiting for transfers between devices, shards(): lax.all_to_all(payload.reshape(n_seq, capacity, payload.shape[1]), SEQ_AX...  28.1 us
    all_to_all x1, starting transfers between devices, shards(): lax.all_to_all(payload.reshape(n_seq, capacity, payload.shape[1]), SEQ_AX...  19.6 us
    all_to_all x1, blocking collectives, spread(): lax.all_to_all(jnp.broadcast_to(block[None], (size,) + block.shape), axis...  19.4 us
    ppermute x13, waiting for transfers between devices, rotate(): lax.ppermute(block, axis, [(i, (i + step) % size) for i in range(size)])  14.1 us
    all_gather x1, blocking collectives, shards(): half_kv = lax.all_gather(z_kv, 'y', axis=0, tiled=True)  11.7 us
    pallas_call x3, Pallas kernels, local_call(): pl.pallas_call(body, in_specs=[pl.BlockSpec(memory_space=pltpu.SMEM)] + [...  11.1 us
    all_to_all x1, blocking collectives, shards(): lax.all_to_all(partial_out.reshape(n_section, width_part, ROWS), 'section...  10.3 us
  transfers between devices with their start and end apart: 15, of which 4 were waited for; matrix products, arithmetic and copies ran while one was open for 8% of the time, Pallas kernels for 3%

profile of v3, /device:TPU:1, one launch (start us, length us, event | category | flops | bytes accessed | tf_op | source)
XLA Modules:
  0.0 196.9 jit_solution(11340883575515390690)
XLA Ops:
  0.0 3.1 %shard_map.199 = (bf16[768,384]{1,0:T(8,128)(2,1)}, bf16[784,384]{1,0:T(8,128)(2,1)}) custom-call(s32[1]{0:T(128)} %bitcast.core_ref, bf16[384,768]{1,0:T(8,128)(2,1)} %up.1, bf16[384,768]{1,0:T(8,128)(2,1)} %w_down.3, bf16[768,384]{1,0:T(8,128)(2,1)} %w_head.3, bf16[384,768]{1,0:T(8,128)(2,1)} %w_in.5, bf16[384]{0:T(512)(128)(2,1)} %bias.1), custom_call_target="tpu_custom_call" | custom-call | bytes 2359296 | tf_op jit(solution)/shard_map/pallas_call | solution.py:94
  3.1 5.2 %collective-permute-start.1 = (bf16[784,384]{1,0:T(8,128)(2,1)}, bf16[784,384]{1,0:T(8,128)(2,1)S(1)}, u32[]{:S(2)}, u32[]{:S(2)}) collective-permute-start(bf16[784,384]{1,0:T(8,128)(2,1)} %get-tuple-element.27), channel_id=1, source_target_pairs={{0,384},{128,0},{256,128},{384,256},{1,385},{129,1},{257,129},{385... | collective-permute-start | bytes 1806344 | tf_op jit(solution)/shard_map/ppermute | solution.py:47
  10.3 2.1 %collective-permute-start = (bf16[768,384]{1,0:T(8,128)(2,1)}, bf16[768,384]{1,0:T(8,128)(2,1)S(1)}, u32[]{:S(2)}, u32[]{:S(2)}) collective-permute-start(bf16[768,384]{1,0:T(8,128)(2,1)} %get-tuple-element.26), channel_id=1, source_target_pairs={{0,128},{128,256},{256,384},{384,0},{1,129},{129,257},{257,385},{3... | collective-permute-start | bytes 1769480 | tf_op jit(solution)/shard_map/ppermute | solution.py:47
  12.4 4.4 %collective-permute-start.3 = (bf16[768,384]{1,0:T(8,128)(2,1)}, bf16[768,384]{1,0:T(8,128)(2,1)S(1)}, u32[]{:S(2)}, u32[]{:S(2)}) collective-permute-start(bf16[768,384]{1,0:T(8,128)(2,1)} %get-tuple-element.26), channel_id=1, source_target_pairs={{0,384},{128,0},{256,128},{384,256},{1,385},{129,1},{257,129},{385... | collective-permute-start | bytes 1769480 | tf_op jit(solution)/shard_map/ppermute | solution.py:47
  17.4 9.6 %fusion.104 = (f32[8,8,8]{2,1,0:T(8,128)S(1)}, f32[8,8,8,768]{3,2,1,0:T(8,128)S(1)}) fusion(f32[768]{0:T(1024)S(1)} %get-tuple-element.94, f32[768]{0:T(1024)S(1)} %get-tuple-element.95, f32[768]{0:T(1024)S(1)} %get-tuple-element.48, f32[768]{0:T(1024)S(1)} %get-tuple-element.49, f32[768]{0:T(1024)S(1)} %get-tuple-element.50, ...), kind=kLoop, calls=%fused_computation.222 | loop fusion | flops 38927872 | bytes 3301376 | tf_op jit(solution)/shard_map/reduce_sum | solution.py:22
  28.8 7.0 %collective-permute-done.left = bf16[768,384]{1,0:T(8,128)(2,1)S(1)} collective-permute-done((bf16[768,384]{1,0:T(8,128)(2,1)}, bf16[768,384]{1,0:T(8,128)(2,1)S(1)}, u32[]{:S(2)}, u32[]{:S(2)}) %collective-permute-start) | collective-permute-done | bytes 589856 | tf_op jit(solution)/shard_map/ppermute | solution.py:47
  35.8 3.9 %collective-permute-start.9 = (bf16[784,384]{1,0:T(8,128)(2,1)S(1)}, bf16[784,384]{1,0:T(8,128)(2,1)}, u32[]{:S(2)}, u32[]{:S(2)}) collective-permute-start(bf16[784,384]{1,0:T(8,128)(2,1)S(1)} %collective-permute-done.1.right2), channel_id=1, source_target_pairs={{0,384},{128,0},{256,128},{384,256},{1,385},{129,1},{257,129},{385... | collective-permute-start | bytes 1806344 | tf_op jit(solution)/shard_map/ppermute | solution.py:47
  39.7 4.4 %collective-permute-start.4 = (bf16[768,384]{1,0:T(8,128)(2,1)S(1)}, bf16[768,384]{1,0:T(8,128)(2,1)}, u32[]{:S(2)}, u32[]{:S(2)}) collective-permute-start(bf16[768,384]{1,0:T(8,128)(2,1)S(1)} %collective-permute-done.left), channel_id=1, source_target_pairs={{0,1},{1,0},{2,3},{3,2},{4,5},{5,4},{6,7},{7,6},{8,9},{9,8},{10,11... | collective-permute-start | bytes 1769480 | tf_op jit(solution)/shard_map/ppermute | solution.py:47
  44.2 3.6 %collective-permute-start.8 = (bf16[768,384]{1,0:T(8,128)(2,1)S(1)}, bf16[768,384]{1,0:T(8,128)(2,1)}, u32[]{:S(2)}, u32[]{:S(2)}) collective-permute-start(bf16[768,384]{1,0:T(8,128)(2,1)S(1)} %collective-permute-done.left), channel_id=1, source_target_pairs={{0,128},{128,256},{256,384},{384,0},{1,129},{129,257},{257,385},{3... | collective-permute-start | bytes 1769480 | tf_op jit(solution)/shard_map/ppermute | solution.py:47
  48.7 2.2 %collective-permute-start.6 = (bf16[784,384]{1,0:T(8,128)(2,1)S(1)}, bf16[784,384]{1,0:T(8,128)(2,1)}, u32[]{:S(2)}, u32[]{:S(2)}) collective-permute-start(bf16[784,384]{1,0:T(8,128)(2,1)S(1)} %collective-permute-done.2.left2), channel_id=1, source_target_pairs={{0,1},{1,0},{2,3},{3,2},{4,5},{5,4},{6,7},{7,6},{8,9},{9,8},{10,11... | collective-permute-start | bytes 1806344 | tf_op jit(solution)/shard_map/ppermute | solution.py:47
  50.9 2.1 %collective-permute-start.7 = (bf16[784,384]{1,0:T(8,128)(2,1)S(1)}, bf16[784,384]{1,0:T(8,128)(2,1)}, u32[]{:S(2)}, u32[]{:S(2)}) collective-permute-start(bf16[784,384]{1,0:T(8,128)(2,1)S(1)} %collective-permute-done.1.right2), channel_id=1, source_target_pairs={{0,1},{1,0},{2,3},{3,2},{4,5},{5,4},{6,7},{7,6},{8,9},{9,8},{10,11... | collective-permute-start | bytes 1806344 | tf_op jit(solution)/shard_map/ppermute | solution.py:47
  53.1 2.2 %collective-permute-start.5 = (bf16[768,384]{1,0:T(8,128)(2,1)S(1)}, bf16[768,384]{1,0:T(8,128)(2,1)}, u32[]{:S(2)}, u32[]{:S(2)}) collective-permute-start(bf16[768,384]{1,0:T(8,128)(2,1)S(1)} %collective-permute-done.3.right), channel_id=1, source_target_pairs={{0,1},{1,0},{2,3},{3,2},{4,5},{5,4},{6,7},{7,6},{8,9},{9,8},{10,11... | collective-permute-start | bytes 1769480 | tf_op jit(solution)/shard_map/ppermute | solution.py:47
  55.3 7.1 %collective-permute-done.8.low = bf16[768,384]{1,0:T(8,128)(2,1)} collective-permute-done((bf16[768,384]{1,0:T(8,128)(2,1)S(1)}, bf16[768,384]{1,0:T(8,128)(2,1)}, u32[]{:S(2)}, u32[]{:S(2)}) %collective-permute-start.8) | collective-permute-done | bytes 589856 | tf_op jit(solution)/shard_map/ppermute | solution.py:47
  62.3 2.7 %collective-permute-start.10 = (bf16[768,384]{1,0:T(8,128)(2,1)}, bf16[768,384]{1,0:T(8,128)(2,1)}, u32[]{:S(2)}, u32[]{:S(2)}) collective-permute-start(bf16[768,384]{1,0:T(8,128)(2,1)} %collective-permute-done.8.low), channel_id=1, source_target_pairs={{0,1},{1,0},{2,3},{3,2},{4,5},{5,4},{6,7},{7,6},{8,9},{9,8},{10,11... | collective-permute-start | bytes 1769480 | tf_op jit(solution)/shard_map/ppermute | solution.py:47
  70.8 4.0 %shard_map.200 = (f32[3,8,384]{2,1,0:T(8,128)S(1)}, f32[152,768]{1,0:T(8,128)S(1)}) custom-call(s32[5]{0:T(128)S(1)} %stack.23.where, bf16[512,768]{1,0:T(8,128)(2,1)} %bitcast.18, bf16[384,768]{1,0:T(8,128)(2,1)S(1)} %copy-done.5, bf16[1,384]{1,0:T(2,128)(2,1)S(1)} %broadcast_in_dim.22.bias, bf16[384,768]{1,0:T(8,128)(2,1)S(1)} %copy-done, ...), custom_call_target="tpu_custom_call" | custom-call | flops 2000000000 | bytes 6000000 | tf_op jit(solution)/shard_map/pallas_call | solution.py:195
  75.0 5.7 %shard_map.201 = bf16[256,896]{1,0:T(8,128)(2,1)S(1)} custom-call(s32[5]{0:T(128)S(1)} %stack.23.where, bf16[512,768]{1,0:T(8,128)(2,1)} %bitcast.19, bf16[152,1536]{1,0:T(8,128)(2,1)S(1)} %copy-done.7, f32[3,8,384]{2,1,0:T(8,128)S(1)} %get-tuple-element.35.hid, f32[152,768]{1,0:T(8,128)S(1)} %get-tuple-element.36.x_prior, ...), custom_call_target="tpu_custom_call" | custom-call | flops 2000000000 | bytes 8000000 | tf_op jit(solution)/shard_map/pallas_call | solution.py:195
  81.6 19.6 %all-to-all-start = ((bf16[128,2,896]{2,1,0:T(2,128)(2,1)}), bf16[128,2,896]{2,1,0:T(2,128)(2,1)S(1)}, u32[]{:S(2)}, u32[]{:S(2)}) async-start(bf16[128,2,896]{2,1,0:T(2,128)(2,1)} %reshape.107), calls=%async_computation | async-start | bytes 917504 | tf_op jit(solution)/shard_map/all_to_all | solution.py:411
  101.2 28.1 %all-to-all-done = bf16[128,2,896]{2,1,0:T(2,128)(2,1)S(1)} async-done(((bf16[128,2,896]{2,1,0:T(2,128)(2,1)}), bf16[128,2,896]{2,1,0:T(2,128)(2,1)S(1)}, u32[]{:S(2)}, u32[]{:S(2)}) %all-to-all-start) | async-done | bytes 458784 | tf_op jit(solution)/shard_map/all_to_all | solution.py:411
  130.6 3.6 %all-to-all-start.1 = ((bf16[4,64,768]{2,1,0:T(8,128)(2,1)}), bf16[4,64,768]{2,1,0:T(8,128)(2,1)S(1)}, u32[]{:S(2)}, u32[]{:S(2)}) async-start(bf16[4,64,768]{2,1,0:T(8,128)(2,1)} %broadcast_in_dim.28), calls=%async_computation.1 | async-start | bytes 786432 | tf_op jit(solution)/shard_map/all_to_all | solution.py:51
  135.4 5.4 %all-to-all-done.1 = bf16[4,64,768]{2,1,0:T(8,128)(2,1)S(1)} async-done(((bf16[4,64,768]{2,1,0:T(8,128)(2,1)}), bf16[4,64,768]{2,1,0:T(8,128)(2,1)S(1)}, u32[]{:S(2)}, u32[]{:S(2)}) %all-to-all-start.1) | async-done | bytes 393248 | tf_op jit(solution)/shard_map/all_to_all | solution.py:51
  141.7 19.4 %all_to_all.20 = bf16[16,16,384]{2,1,0:T(8,128)(2,1)S(1)} all-to-all(bf16[16,16,384]{2,1,0:T(8,128)(2,1)S(1)} %broadcast_in_dim.31), channel_id=1, replica_groups=mesh['section'=4,'z'=16,'y'=4,'core'=2] {'z'}, dimensions={0} | all-to-all | bytes 393216 | tf_op jit(solution)/shard_map/all_to_all | solution.py:51
  161.1 11.7 %all_gather.3.kv = bf16[1024,384]{1,0:T(8,128)(2,1)S(1)} all-gather(bf16[256,384]{1,0:T(8,128)(2,1)S(1)} %bitcast.20), channel_id=1, replica_groups=mesh['section'=4,'z'=16,'y'=4,'core'=2] {'y'}, dimensions={0}, use_global_device_ids=true | all-gather | bytes 983040 | tf_op jit(solution)/shard_map/all_gather | solution.py:437
  172.8 9.4 %collective-permute-start.12 = (bf16[1024,384]{1,0:T(8,128)(2,1)S(1)}, bf16[1024,384]{1,0:T(8,128)(2,1)S(1)}, u32[]{:S(2)}, u32[]{:S(2)}) collective-permute-start(bf16[1024,384]{1,0:T(8,128)(2,1)S(1)} %all_gather.3.kv), channel_id=1, source_target_pairs={{0,1},{1,0},{2,3},{3,2},{4,5},{5,4},{6,7},{7,6},{8,9},{9,8},{10,11... | collective-permute-start | bytes 2359304 | tf_op jit(solution)/shard_map/ppermute | solution.py:47
  185.9 10.3 %all_to_all.21.parts = bf16[4,192,256]{2,1,0:T(8,128)(2,1)S(1)} all-to-all(bf16[4,192,256]{2,1,0:T(8,128)(2,1)S(1)} %bitcast.15), channel_id=1, replica_groups=mesh['section'=4,'z'=16,'y'=4,'core'=2] {'section'}, dimensions={0} | all-to-all | bytes 786432 | tf_op jit(solution)/shard_map/all_to_all | solution.py:459
  (101 shorter events, 18.8 us)
Async XLA Ops:
  3.1 32.7 %collective-permute-start.1 = (bf16[784,384]{1,0:T(8,128)(2,1)}, bf16[784,384]{1,0:T(8,128)(2,1)S(1)}, u32[]{:S(2)}, u32[]{:S(2)}) collective-permute-start(bf16[784,384]{1,0:T(8,128)(2,1)} %get-tuple-element.27), channel_id=1, source_target_pairs={{0,384},{128,0},{256,128},{384,256},{1,385},{129,1},{257,129},{385... | collective-permute-start | bytes 1806344 | tf_op jit(solution)/shard_map/ppermute | solution.py:47
  8.3 31.4 %collective-permute-start.2 = (bf16[784,384]{1,0:T(8,128)(2,1)}, bf16[784,384]{1,0:T(8,128)(2,1)S(1)}, u32[]{:S(2)}, u32[]{:S(2)}) collective-permute-start(bf16[784,384]{1,0:T(8,128)(2,1)} %get-tuple-element.27), channel_id=1, source_target_pairs={{0,128},{128,256},{256,384},{384,0},{1,129},{129,257},{257,385},{3... | collective-permute-start | bytes 1806344 | tf_op jit(solution)/shard_map/ppermute | solution.py:47
  10.3 25.5 %collective-permute-start = (bf16[768,384]{1,0:T(8,128)(2,1)}, bf16[768,384]{1,0:T(8,128)(2,1)S(1)}, u32[]{:S(2)}, u32[]{:S(2)}) collective-permute-start(bf16[768,384]{1,0:T(8,128)(2,1)} %get-tuple-element.26), channel_id=1, source_target_pairs={{0,128},{128,256},{256,384},{384,0},{1,129},{129,257},{257,385},{3... | collective-permute-start | bytes 1769480 | tf_op jit(solution)/shard_map/ppermute | solution.py:47
  12.4 27.3 %collective-permute-start.3 = (bf16[768,384]{1,0:T(8,128)(2,1)}, bf16[768,384]{1,0:T(8,128)(2,1)S(1)}, u32[]{:S(2)}, u32[]{:S(2)}) collective-permute-start(bf16[768,384]{1,0:T(8,128)(2,1)} %get-tuple-element.26), channel_id=1, source_target_pairs={{0,384},{128,0},{256,128},{384,256},{1,385},{129,1},{257,129},{385... | collective-permute-start | bytes 1769480 | tf_op jit(solution)/shard_map/ppermute | solution.py:47
  27.3 39.7 %copy-start.13 = (bf16[384]{0:T(512)(128)(2,1)S(1)}, bf16[384]{0:T(512)(128)(2,1)}, u32[]{:S(2)}) copy-start(bf16[384]{0:T(512)(128)(2,1)} %bias.1) | copy-start | bytes 2308
  27.3 39.7 %copy-start.14 = (f32[768]{0:T(1024)S(1)}, f32[768]{0:T(1024)}, u32[]{:S(2)}) copy-start(f32[768]{0:T(1024)} %param.29) | copy-start | bytes 9220
  27.3 39.7 %copy-start.15 = (f32[768]{0:T(1024)S(1)}, f32[768]{0:T(1024)}, u32[]{:S(2)}) copy-start(f32[768]{0:T(1024)} %param.28) | copy-start | bytes 9220
  27.3 39.7 %copy-start.16 = (f32[768]{0:T(1024)S(1)}, f32[768]{0:T(1024)}, u32[]{:S(2)}) copy-start(f32[768]{0:T(1024)} %param.30) | copy-start | bytes 9220
  27.7 41.0 %copy-start = (bf16[384,768]{1,0:T(8,128)(2,1)S(1)}, bf16[384,768]{1,0:T(8,128)(2,1)}, u32[]{:S(2)}) copy-start(bf16[384,768]{1,0:T(8,128)(2,1)} %w_in.5) | copy-start | bytes 1769476
  35.8 39.0 %copy-start.3 = (bf16[784,384]{1,0:T(8,128)(2,1)}, bf16[784,384]{1,0:T(8,128)(2,1)S(1)}, u32[]{:S(2)}) copy-start(bf16[784,384]{1,0:T(8,128)(2,1)S(1)} %collective-permute-done.1.right2) | copy-start | bytes 1806340
  35.8 29.2 %collective-permute-start.9 = (bf16[784,384]{1,0:T(8,128)(2,1)S(1)}, bf16[784,384]{1,0:T(8,128)(2,1)}, u32[]{:S(2)}, u32[]{:S(2)}) collective-permute-start(bf16[784,384]{1,0:T(8,128)(2,1)S(1)} %collective-permute-done.1.right2), channel_id=1, source_target_pairs={{0,384},{128,0},{256,128},{384,256},{1,385},{129,1},{257,129},{385... | collective-permute-start | bytes 1806344 | tf_op jit(solution)/shard_map/ppermute | solution.py:47
  39.7 35.1 %copy-start.4 = (bf16[784,384]{1,0:T(8,128)(2,1)}, bf16[784,384]{1,0:T(8,128)(2,1)S(1)}, u32[]{:S(2)}) copy-start(bf16[784,384]{1,0:T(8,128)(2,1)S(1)} %collective-permute-done.2.left2) | copy-start | bytes 1806340
  39.7 13.3 %collective-permute-start.4 = (bf16[768,384]{1,0:T(8,128)(2,1)S(1)}, bf16[768,384]{1,0:T(8,128)(2,1)}, u32[]{:S(2)}, u32[]{:S(2)}) collective-permute-start(bf16[768,384]{1,0:T(8,128)(2,1)S(1)} %collective-permute-done.left), channel_id=1, source_target_pairs={{0,1},{1,0},{2,3},{3,2},{4,5},{5,4},{6,7},{7,6},{8,9},{9,8},{10,11... | collective-permute-start | bytes 1769480 | tf_op jit(solution)/shard_map/ppermute | solution.py:47
  44.2 18.2 %collective-permute-start.8 = (bf16[768,384]{1,0:T(8,128)(2,1)S(1)}, bf16[768,384]{1,0:T(8,128)(2,1)}, u32[]{:S(2)}, u32[]{:S(2)}) collective-permute-start(bf16[768,384]{1,0:T(8,128)(2,1)S(1)} %collective-permute-done.left), channel_id=1, source_target_pairs={{0,128},{128,256},{256,384},{384,0},{1,129},{129,257},{257,385},{3... | collective-permute-start | bytes 1769480 | tf_op jit(solution)/shard_map/ppermute | solution.py:47
  48.7 19.9 %collective-permute-start.6 = (bf16[784,384]{1,0:T(8,128)(2,1)S(1)}, bf16[784,384]{1,0:T(8,128)(2,1)}, u32[]{:S(2)}, u32[]{:S(2)}) collective-permute-start(bf16[784,384]{1,0:T(8,128)(2,1)S(1)} %collective-permute-done.2.left2), channel_id=1, source_target_pairs={{0,1},{1,0},{2,3},{3,2},{4,5},{5,4},{6,7},{7,6},{8,9},{9,8},{10,11... | collective-permute-start | bytes 1806344 | tf_op jit(solution)/shard_map/ppermute | solution.py:47
  50.9 17.7 %collective-permute-start.7 = (bf16[784,384]{1,0:T(8,128)(2,1)S(1)}, bf16[784,384]{1,0:T(8,128)(2,1)}, u32[]{:S(2)}, u32[]{:S(2)}) collective-permute-start(bf16[784,384]{1,0:T(8,128)(2,1)S(1)} %collective-permute-done.1.right2), channel_id=1, source_target_pairs={{0,1},{1,0},{2,3},{3,2},{4,5},{5,4},{6,7},{7,6},{8,9},{9,8},{10,11... | collective-permute-start | bytes 1806344 | tf_op jit(solution)/shard_map/ppermute | solution.py:47
  53.1 15.5 %collective-permute-start.5 = (bf16[768,384]{1,0:T(8,128)(2,1)S(1)}, bf16[768,384]{1,0:T(8,128)(2,1)}, u32[]{:S(2)}, u32[]{:S(2)}) collective-permute-start(bf16[768,384]{1,0:T(8,128)(2,1)S(1)} %collective-permute-done.3.right), channel_id=1, source_target_pairs={{0,1},{1,0},{2,3},{3,2},{4,5},{5,4},{6,7},{7,6},{8,9},{9,8},{10,11... | collective-permute-start | bytes 1769480 | tf_op jit(solution)/shard_map/ppermute | solution.py:47
  62.3 12.5 %collective-permute-start.10 = (bf16[768,384]{1,0:T(8,128)(2,1)}, bf16[768,384]{1,0:T(8,128)(2,1)}, u32[]{:S(2)}, u32[]{:S(2)}) collective-permute-start(bf16[768,384]{1,0:T(8,128)(2,1)} %collective-permute-done.8.low), channel_id=1, source_target_pairs={{0,1},{1,0},{2,3},{3,2},{4,5},{5,4},{6,7},{7,6},{8,9},{9,8},{10,11... | collective-permute-start | bytes 1769480 | tf_op jit(solution)/shard_map/ppermute | solution.py:47
  65.0 9.8 %collective-permute-start.11 = (bf16[784,384]{1,0:T(8,128)(2,1)}, bf16[784,384]{1,0:T(8,128)(2,1)}, u32[]{:S(2)}, u32[]{:S(2)}) collective-permute-start(bf16[784,384]{1,0:T(8,128)(2,1)} %collective-permute-done.9.high), channel_id=1, source_target_pairs={{0,1},{1,0},{2,3},{3,2},{4,5},{5,4},{6,7},{7,6},{8,9},{9,8},{10,11... | collective-permute-start | bytes 1806344 | tf_op jit(solution)/shard_map/ppermute | solution.py:47
  81.6 47.7 %all-to-all-start = ((bf16[128,2,896]{2,1,0:T(2,128)(2,1)}), bf16[128,2,896]{2,1,0:T(2,128)(2,1)S(1)}, u32[]{:S(2)}, u32[]{:S(2)}) async-start(bf16[128,2,896]{2,1,0:T(2,128)(2,1)} %reshape.107), calls=%async_computation | async-start | bytes 917504 | tf_op jit(solution)/shard_map/all_to_all | solution.py:411
  101.2 33.1 %copy-start.21 = (s32[12]{0:T(128)S(1)}, s32[12]{0:T(128)}, u32[]{:S(2)}) copy-start(s32[12]{0:T(128)} %param.40) | copy-start | bytes 148
  101.2 33.3 %copy-start.9 = (bf16[768,576]{0,1:T(8,128)(2,1)S(1)}, bf16[768,576]{0,1:T(8,128)(2,1)}, u32[]{:S(2)}) copy-start(bf16[768,576]{0,1:T(8,128)(2,1)} %param.37) | copy-start | bytes 2654212
  130.6 10.2 %all-to-all-start.1 = ((bf16[4,64,768]{2,1,0:T(8,128)(2,1)}), bf16[4,64,768]{2,1,0:T(8,128)(2,1)S(1)}, u32[]{:S(2)}, u32[]{:S(2)}) async-start(bf16[4,64,768]{2,1,0:T(8,128)(2,1)} %broadcast_in_dim.28), calls=%async_computation.1 | async-start | bytes 786432 | tf_op jit(solution)/shard_map/all_to_all | solution.py:51
  172.8 12.0 %collective-permute-start.12 = (bf16[1024,384]{1,0:T(8,128)(2,1)S(1)}, bf16[1024,384]{1,0:T(8,128)(2,1)S(1)}, u32[]{:S(2)}, u32[]{:S(2)}) collective-permute-start(bf16[1024,384]{1,0:T(8,128)(2,1)S(1)} %all_gather.3.kv), channel_id=1, source_target_pairs={{0,1},{1,0},{2,3},{3,2},{4,5},{5,4},{6,7},{7,6},{8,9},{9,8},{10,11... | collective-permute-start | bytes 2359304 | tf_op jit(solution)/shard_map/ppermute | solution.py:47
  (13 other events, 95.0 us)

commit v4 on v3

--- a/solution.py
+++ b/solution.py
@@ -25,24 +25,6 @@
     return centered * lax.rsqrt(variance + 1e-06) * gain_vec
 
 
-def conv_norm(tile_maps, dw_weight, dw_bias, ln1_gain):
-    map_side = tile_maps.shape[1]
-    kernel = dw_weight.shape[0]
-    half_width = (kernel - 1) // 2
-    source = tile_maps.astype(F32)
-    padded = jnp.pad(source, ((0, 0), (half_width, half_width), (half_width, half_width), (0, 0)))
-    conv_sum = jnp.zeros_like(source) + dw_bias
-    for row_off in range(kernel):
-        for col_off in range(kernel):
-            conv_sum = (
-                conv_sum
-                + padded[:, row_off : row_off + map_side, col_off : col_off + map_side, :]
-                * dw_weight[row_off, col_off]
-            )
-    channels = source.shape[-1]
-    return layer_norm(conv_sum, ln1_gain).astype(BF16).reshape(-1, channels)
-
-
 def rotate(block, axis, size, step):
     return lax.ppermute(block, axis, [(i, (i + step) % size) for i in range(size)])
 
@@ -69,21 +51,22 @@
     return ref[:, pl.ds(pl.multiple_of(index * width, 128), width)]
 
 
-def pack_kernel(core_ref, w_up, w_down, w_head, w_in, bias, first, second, sems):
+def pack_kernel(core_ref, w_up, w_down, w_head, w_in, bias, out, sems):
     n = w_up.shape[0]
     start = pl.multiple_of(core_ref[0] * n, n)
+    parts = (
+        w_up.at[:, pl.ds(start, n)],
+        w_down.at[:, pl.ds(start, n)],
+        w_head.at[pl.ds(start, n), :],
+        w_in.at[:, pl.ds(start, n)],
+    )
     copies = [
-        pltpu.make_async_copy(part, out.at[pl.ds(k * n, n), :], sems.at[k, slot])
-        for out, slot, k, part in (
-            (first, 0, 0, w_up.at[:, pl.ds(start, n)]),
-            (first, 0, 1, w_down.at[:, pl.ds(start, n)]),
-            (second, 1, 0, w_head.at[pl.ds(start, n), :]),
-            (second, 1, 1, w_in.at[:, pl.ds(start, n)]),
-        )
+        pltpu.make_async_copy(part, out.at[pl.ds(k * n, n), :], sems.at[k])
+        for k, part in enumerate(parts)
     ]
     for copy in copies:
         copy.start()
-    second[2 * n :, :] = jnp.broadcast_to(bias[...][None, :], (16, n))
+    out[4 * n :, :] = jnp.broadcast_to(bias[...][None, :], (16, n))
     for copy in copies:
         copy.wait()
 
@@ -96,49 +79,72 @@
         in_specs=[pl.BlockSpec(memory_space=pltpu.SMEM)]
         + [pl.BlockSpec(memory_space=pl.ANY)] * 4
         + [vmem],
-        out_specs=(vmem, vmem),
-        out_shape=(
-            jax.ShapeDtypeStruct((2 * n, n), BF16),
-            jax.ShapeDtypeStruct((2 * n + 16, n), BF16),
-        ),
-        scratch_shapes=[pltpu.SemaphoreType.DMA((2, 2))],
+        out_specs=vmem,
+        out_shape=jax.ShapeDtypeStruct((4 * n + 16, n), BF16),
+        scratch_shapes=[pltpu.SemaphoreType.DMA((4,))],
         cost_estimate=pl.CostEstimate(flops=0, bytes_accessed=4 * n * n * 4, transcendentals=0),
     )(core.astype(jnp.int32)[None], w_up, w_down, w_head, w_in, bias)
 
 
-def early_kernel(
-    where, maps, up, bias, w_in, prior,
-    left, right, left_swap, right_swap, left2, right2, left2_swap, right2_swap, hid, x_prior,
-):
+def natural(core, a, b):
+    return jnp.where(core == 0, jnp.concatenate([a, b], 1), jnp.concatenate([b, a], 1))
+
+
+def conv_kernel(feats, dw_weight, dw_bias, gain, out, mean, conv):
+    tiles, side, _, channels = feats.shape
+    taps = math.isqrt(dw_weight.shape[0])
+    reach = (taps - 1) // 2
+    column = lax.broadcasted_iota(jnp.int32, (side, side, 128), 1)
+    tile_row = lax.broadcasted_iota(jnp.int32, (tiles, 128), 0)
+    mean[...] = jnp.zeros_like(mean)
+
+    def one_tile(tile, carry):
+        for chunk in range(channels // 128):
+            cols = pl.ds(chunk * 128, 128)
+            source = feats[tile, :, :, cols].astype(F32)
+            total = jnp.sum(jnp.sum(source, axis=0), axis=0, keepdims=True)
+            total = jnp.broadcast_to(total * (1.0 / (side * side)), (tiles, 128))
+            mean[:, cols] = jnp.where(tile_row == tile, total, mean[:, cols])
+            bias = jnp.broadcast_to(dw_bias[0:1, cols], (side, 128))
+            sums = [bias] * side
+            for b in range(taps):
+                move = b - reach
+                moved = source
+                if move:
+                    moved = pltpu.roll(source, (-move) % side, 1)
+                    inside = (column + move >= 0) & (column + move < side)
+                    moved = jnp.where(inside, moved, 0.0)
+                for a in range(taps):
+                    tap = dw_weight[a * taps + b : a * taps + b + 1, cols]
+                    tap = jnp.broadcast_to(tap, (side, 128))
+                    for i in range(side):
+                        if 0 <= i + a - reach < side:
+                            sums[i] = sums[i] + moved[i + a - reach] * tap
+            for i in range(side):
+                conv[i * side : (i + 1) * side, cols] = sums[i]
+        start = pl.multiple_of(tile * side * side, side * side)
+        out[pl.ds(start, side * side), :] = layer_norm(conv[...], gain[...]).astype(BF16)
+        return carry
+
+    lax.fori_loop(0, tiles, one_tile, 0)
+
+
+def early_kernel(where, maps, up, bias, left, right, left_swap, right_swap, hid):
     core = where[0]
     n = up.shape[0]
     tiles = hid.shape[1]
     maps_a, maps_b = lanes(maps, core, n), lanes(maps, 1 - core, n)
     pre = lax.dot_general(maps[...], up[...], NT, preferred_element_type=F32)
     hid[0] = gelu_mean(pre + bias[...].astype(F32), tiles)
-    own = dot(lanes(prior, where[1], n), w_in[...])
-    x_a = jnp.zeros((prior.shape[0], n), F32)
-    x_b = x_a
-    sides = ((left, left_swap, left2, left2_swap), (right, right_swap, right2, right2_swap))
-    for slot, (a, b, a2, b2) in enumerate(sides):
+    for slot, (a, b) in enumerate(((left, left_swap), (right, right_swap))):
         pre = lax.dot_general(maps_a, a[0:n, :], NT, preferred_element_type=F32)
         pre += lax.dot_general(maps_b, b[0:n, :], NT, preferred_element_type=F32)
-        hid[slot + 1] = gelu_mean(pre + a2[2 * n : 2 * n + 1, :].astype(F32), tiles)
-        columns = lanes(prior, where[slot + 2], n)
-        x_a += dot(columns, a2[n : 2 * n, :])
-        x_b += dot(columns, b2[n : 2 * n, :])
-    x_prior[...] = own + natural(core, x_a, x_b)
-
-
-def natural(core, a, b):
-    return jnp.where(core == 0, jnp.concatenate([a, b], 1), jnp.concatenate([b, a], 1))
+        hid[slot + 1] = gelu_mean(pre + a[4 * n : 4 * n + 1, :].astype(F32), tiles)
 
 
 def late_kernel(
-    where, maps, prior, hid, x_prior, feat_mean, layer_scale, b_down, lnf_gain, bucket, row_code,
-    w_down, w_head, w_in,
-    left, right, left_swap, right_swap, left2, right2, left2_swap, right2_swap,
-    low, high, low_swap, high_swap, payload, slot_x,
+    where, maps, hid, feat_mean, layer_scale, b_down, lnf_gain, code, w_down, w_head, w_in,
+    left, right, left_swap, right_swap, low, high, low_swap, high_swap, out,
 ):
     core = where[0]
     n = w_down.shape[0]
@@ -153,9 +159,6 @@
         upper = block.astype(BF16)
         lower = (block - upper.astype(F32)).astype(BF16)
         return jnp.concatenate([upper.astype(F32), lower.astype(F32)], 0).astype(BF16)
-
-    def folded(block):
-        return block[0:tiles] + block[tiles : 2 * tiles]
 
     sides = ((left, left_swap), (right, right_swap))
     own = dot(exact(hid[0]), w_down[...])
@@ -165,7 +168,8 @@
         part = exact(hid[slot + 1])
         br_a += dot(part, a[n : 2 * n, :])
         br_b += dot(part, b[n : 2 * n, :])
-    branch = folded(own + natural(core, br_a, br_b))
+    branch = own + natural(core, br_a, br_b)
+    branch = branch[0:tiles] + branch[tiles : 2 * tiles]
     pooled = feat_mean[...] + layer_scale[...] * (branch + b_down[...])
     feature = layer_norm(pooled, lnf_gain[...])
     first, second = feature[:, 0:n], feature[:, n : 2 * n]
@@ -174,20 +178,73 @@
     emb = dot(feature.astype(BF16), w_head[...]).astype(BF16)
     own = dot(emb, w_in[...])
     emb = (dot(feature_a, high[0:n, :]) + dot(feature_b, high_swap[0:n, :])).astype(BF16)
-    columns = lanes(prior, where[4], n)
     x_a, x_b = dot(emb, high[n : 2 * n, :]), dot(emb, high_swap[n : 2 * n, :])
-    p_a, p_b = dot(columns, high[n : 2 * n, :]), dot(columns, high_swap[n : 2 * n, :])
-    for a, b in ((left2, left2_swap), (right2, right2_swap)):
-        emb = (dot(feature_a, a[0:n, :]) + dot(feature_b, b[0:n, :])).astype(BF16)
-        x_a += dot(emb, a[n : 2 * n, :])
-        x_b += dot(emb, b[n : 2 * n, :])
-    slot_x[0:tiles, :] = own + natural(core, x_a, x_b)
-    slot_x[tiles:, :] = x_prior[...] + natural(core, p_a, p_b)
-    places = lax.broadcasted_iota(jnp.int32, (payload.shape[0], bucket.shape[1]), 0)
+    for a, b in sides:
+        emb = dot(feature_a, a[2 * n : 3 * n, :]) + dot(feature_b, b[2 * n : 3 * n, :])
+        emb = emb.astype(BF16)
+        x_a += dot(emb, a[3 * n : 4 * n, :])
+        x_b += dot(emb, b[3 * n : 4 * n, :])
+    x_fresh = own + natural(core, x_a, x_b)
+    out[...] = jnp.concatenate([x_fresh, code[...]], axis=1).astype(BF16)
+
+
+def select_kernel(bucket, rows, code, out):
+    places = lax.broadcasted_iota(jnp.int32, (out.shape[0], bucket.shape[1]), 0)
     select = jnp.where(places == bucket[...], 1.0, 0.0).astype(BF16)
-    width = slot_x.shape[1]
-    payload[:, 0:width] = dot(select, slot_x[...].astype(BF16)).astype(BF16)
-    payload[:, width:] = dot(select, row_code[...]).astype(BF16)
+    width = rows.shape[1]
+    out[:, 0:width] = dot(select, rows[...]).astype(BF16)
+    out[:, width:] = dot(select, code[...]).astype(BF16)
+
+
+def column_as_row(ref, column):
+    lane = lax.broadcasted_iota(jnp.int32, (8, 128), 1)
+    unit_row = jnp.where(lane == column, 1.0, 0.0).astype(BF16)
+    tail = ref[:, ref.shape[1] - 128 :]
+    return lax.dot_general(unit_row, tail, NT, preferred_element_type=F32)[0:1, :]
+
+
+def place_rows(got, q_rows):
+    code = column_as_row(got, 0)
+    places = lax.broadcasted_iota(jnp.int32, (q_rows, got.shape[0]), 0).astype(F32) + 1.0
+    placer = jnp.where(places == code, 1.0, 0.0).astype(BF16)
+    return dot(placer, got[:, 0 : got.shape[1] - 128])
+
+
+def earlier_kernel(
+    where, got, w_in, left, right, left_swap, right_swap, high, high_swap, out, rows
+):
+    n = w_in.shape[0]
+    rows[...] = place_rows(got, out.shape[0]).astype(BF16)
+    own = dot(lanes(rows, where[1], n), w_in[...])
+    columns = lanes(rows, where[4], n)
+    x_a, x_b = dot(columns, high[n : 2 * n, :]), dot(columns, high_swap[n : 2 * n, :])
+    for slot, (a, b) in enumerate(((left, left_swap), (right, right_swap))):
+        columns = lanes(rows, where[slot + 2], n)
+        x_a += dot(columns, a[3 * n : 4 * n, :])
+        x_b += dot(columns, b[3 * n : 4 * n, :])
+    out[...] = own + natural(where[0], x_a, x_b)
+
+
+def scatter_kernel(where, rows, out):
+    count = rows.shape[0]
+    dest_row = column_as_row(rows, 1)
+    dest = rows[:, rows.shape[1] - 128 :].astype(F32)[:, 1:2]
+    index_a = lax.broadcasted_iota(jnp.int32, (count, count), 0)
+    index_b = lax.broadcasted_iota(jnp.int32, (count, count), 1)
+    before = jnp.where((dest == dest_row) & (index_a < index_b), 1.0, 0.0)
+    rank = jnp.sum(before, axis=0, keepdims=True).astype(jnp.int32)
+    shard = dest_row.astype(jnp.int32)
+    plane = N_Y * N_CORE
+    room = out.shape[0] // plane
+    inside = shard - where[5] * plane
+    bucket = jnp.where((inside >= 0) & (inside < plane), inside * room + rank, -1)
+    places = lax.broadcasted_iota(jnp.int32, (out.shape[0], count), 0)
+    select = jnp.where(places == bucket, 1.0, 0.0).astype(BF16)
+    out[...] = dot(select, rows[...]).astype(BF16)
+
+
+def arrive_kernel(got, earlier, out):
+    out[...] = (place_rows(got, out.shape[0]) + earlier[...]).astype(BF16)
 
 
 def local_call(body, outs, scratch, flops, size, *operands):
@@ -303,13 +360,14 @@
     out[...] = total.astype(BF16)
 
 
-def vmem_call(body, outs, flops, size, exps, *operands):
+def vmem_call(body, outs, flops, size, exps, *operands, scratch=()):
     vmem = pl.BlockSpec(memory_space=pltpu.VMEM)
     return pl.pallas_call(
         body,
         in_specs=[vmem] * len(operands),
         out_specs=jax.tree.map(lambda _: vmem, outs),
         out_shape=outs,
+        scratch_shapes=list(scratch),
         compiler_params=pltpu.CompilerParams(vmem_limit_bytes=40 * 2**20),
         cost_estimate=pl.CostEstimate(flops=flops, bytes_accessed=size, transcendentals=exps),
     )(*operands)
@@ -347,73 +405,122 @@
     half = channels // N_CORE
     share = w_up.shape[0]
 
-    first, second = pack(core, w_up, w_down, w_head, w_in, b_up)
-    left = rotate(first, "section", N_SECTION, 1)
-    right2 = rotate(second, "section", N_SECTION, -1)
-    left2 = rotate(second, "section", N_SECTION, 1)
-    right = rotate(first, "section", N_SECTION, -1)
-    normed_maps = conv_norm(feats, dw_weight, dw_bias, ln1_gain)
-    left, right2, normed_maps = lax.optimization_barrier((left, right2, normed_maps))
-    low = rotate(left, "section", N_SECTION, 1)
-    high = rotate(right2, "section", N_SECTION, -1)
-    left, right2, left2, right = lax.optimization_barrier((left, right2, left2, right))
+    row = lambda vec: vec[None, :]
+    others = [(section_idx + step) % N_SECTION for step in (3, 1, 2)]
+    where = jnp.stack([core, section_idx] + others + [lax.axis_index("z")]).astype(jnp.int32)
+
+    block = pack(core, w_up, w_down, w_head, w_in, b_up)
+    block, prior = lax.optimization_barrier((block, prior))
+    left = rotate(block, "section", N_SECTION, 1)
+    right = rotate(block, "section", N_SECTION, -1)
+
+    q_rows = ROWS // n_section
+    capacity = -(-(tiles + prior.shape[0]) // n_seq)
+    slot_ids = jnp.arange(prior.shape[0])
+    live_mask = slot_ids < counts[0]
+    dest_shard = positions // ROWS
+    row_code = (positions % ROWS - section_idx * q_rows + 1).astype(BF16)
+    dest_prior = dest_shard[tiles:]
+    earlier = (
+        (dest_prior[None, :] == dest_prior[:, None])
+        & (slot_ids[None, :] < slot_ids[:, None])
+        & live_mask[None, :]
+    )
+    within = jnp.sum(earlier.astype(jnp.int32), axis=1)
+    bucket = jnp.where(live_mask, dest_prior * capacity + within, -1)
+    code_prior = jnp.broadcast_to(row_code[tiles:, None], (prior.shape[0], 128))
+    send = vmem_call(
+        select_kernel,
+        jax.ShapeDtypeStruct((n_seq * capacity, prior.shape[1] + 128), BF16),
+        200_000_000,
+        2_000_000,
+        0,
+        row(bucket), prior, code_prior,
+    )
+
+    got_prior = lax.all_to_all(
+        send.reshape(n_seq, capacity, send.shape[1]), SEQ_AXES, 0, 0, tiled=True
+    ).reshape(send.shape)
+    left, right, low_in, high_in, feats = lax.optimization_barrier(
+        (left, right, left[: 2 * share], right[2 * share :], feats)
+    )
+    low = rotate(low_in, "section", N_SECTION, 1)
+    high = rotate(high_in, "section", N_SECTION, -1)
     left_swap = rotate(left, "core", N_CORE, 1)
     right_swap = rotate(right, "core", N_CORE, 1)
-    left2_swap = rotate(left2, "core", N_CORE, 1)
-    right2_swap = rotate(right2, "core", N_CORE, 1)
+    pixels = feats.shape[1] * feats.shape[2]
+    normed_maps, feat_mean = vmem_call(
+        conv_kernel,
+        (
+            jax.ShapeDtypeStruct((tiles * pixels, channels), BF16),
+            jax.ShapeDtypeStruct((tiles, channels), F32),
+        ),
+        30_000_000_000,
+        8_000_000,
+        0,
+        feats, dw_weight.reshape(-1, channels), row(dw_bias), row(ln1_gain),
+        scratch=[pltpu.VMEM((pixels, channels), F32)],
+    )
+    low, high, normed_maps, feat_mean = lax.optimization_barrier(
+        (low, high, normed_maps, feat_mean)
+    )
     low_swap = rotate(low, "core", N_CORE, 1)
     high_swap = rotate(high, "core", N_CORE, 1)
-
-    slot_total = tiles + prior.shape[0]
-    q_rows = ROWS // n_section
-    capacity = -(-slot_total // n_seq)
-    slot_ids = jnp.arange(slot_total)
-    live_mask = slot_ids < tiles + counts[0]
-    dest_shard = positions // ROWS
-    row_in = positions % ROWS - section_idx * q_rows
-    earlier = (
-        (dest_shard[None, :] == dest_shard[:, None])
-        & (slot_ids[None, :] < slot_ids[:, None])
-        & live_mask[None, :]
-    )
-    within = jnp.sum(earlier.astype(jnp.int32), axis=1)
-    bucket = jnp.where(live_mask, dest_shard * capacity + within, -1)
-    row_code = jnp.broadcast_to((row_in + 1).astype(BF16)[:, None], (slot_total, 128))
-
-    feat_mean = jnp.mean(feats.astype(F32), axis=(1, 2))
-    where = jnp.stack(
-        [core, section_idx, (section_idx + 3) % 4, (section_idx + 1) % 4, (section_idx + 2) % 4]
-    ).astype(jnp.int32)
-    row = lambda vec: vec[None, :]
-    hid, x_prior = local_call(
+    code_fresh = jnp.where(
+        jnp.arange(128)[None, :] == 0,
+        row_code[:tiles, None].astype(F32),
+        dest_shard[:tiles, None].astype(F32),
+    )
+    hid = local_call(
         early_kernel,
-        (
-            jax.ShapeDtypeStruct((3, tiles, share), F32),
-            jax.ShapeDtypeStruct((prior.shape[0], channels), F32),
-        ),
+        jax.ShapeDtypeStruct((3, tiles, share), F32),
         [],
         2_000_000_000,
         6_000_000,
-        where, normed_maps, w_up, row(b_up), w_in, prior, left, right, left_swap, right_swap,
-        left2, right2, left2_swap, right2_swap,
-    )
-    payload = local_call(
+        where, normed_maps, w_up, row(b_up), left, right, left_swap, right_swap,
+    )
+    got_prior, hid = lax.optimization_barrier((got_prior, hid))
+    fresh = local_call(
         late_kernel,
-        jax.ShapeDtypeStruct((n_seq * capacity, channels + 128), BF16),
-        [pltpu.VMEM((slot_total, channels), F32)],
+        jax.ShapeDtypeStruct((tiles, channels + 128), BF16),
+        [],
         2_000_000_000,
         8_000_000,
-        where, normed_maps, prior, hid, x_prior, feat_mean, row(layer_scale), row(b_down),
-        row(lnf_gain), row(bucket), row_code, w_down, w_head, w_in, left, right, left_swap,
-        right_swap, left2, right2, left2_swap, right2_swap, low, high, low_swap, high_swap,
-    )
-
+        where, normed_maps, hid, feat_mean, row(layer_scale), row(b_down), row(lnf_gain),
+        code_fresh, w_down, w_head, w_in, left, right, left_swap, right_swap, low, high, low_swap,
+        high_swap,
+    )
+    x_earlier = local_call(
+        earlier_kernel,
+        jax.ShapeDtypeStruct((q_rows, channels), F32),
+        [pltpu.VMEM((q_rows, prior.shape[1]), BF16)],
+        500_000_000,
+        4_000_000,
+        where, got_prior, w_in, left, right, left_swap, right_swap, high, high_swap,
+    )
+
+    fresh_z = spread(fresh, "z", N_Z).reshape(N_Z * tiles, channels + 128)
+    plane = N_Y * N_CORE
+    room = N_Z * capacity
+    to_plane = local_call(
+        scatter_kernel,
+        jax.ShapeDtypeStruct((plane * room, channels + 128), BF16),
+        [],
+        60_000_000,
+        1_000_000,
+        where, fresh_z,
+    )
     got = lax.all_to_all(
-        payload.reshape(n_seq, capacity, payload.shape[1]), SEQ_AXES, 0, 0, tiled=True
-    ).reshape(n_seq * capacity, payload.shape[1])
-    code = got[:, channels].astype(F32)
-    placer = (jnp.arange(1, q_rows + 1).astype(F32)[:, None] == code[None, :]).astype(BF16)
-    x_local = dot(placer, got[:, :channels]).astype(BF16)
+        to_plane.reshape(plane, room, channels + 128), ("y", "core"), 0, 0, tiled=True
+    ).reshape(plane * room, channels + 128)
+    x_local = vmem_call(
+        arrive_kernel,
+        jax.ShapeDtypeStruct((q_rows, channels), BF16),
+        30_000_000,
+        1_000_000,
+        0,
+        got, x_earlier,
+    )
     x_rows = spread(x_local, "section", n_section).reshape(ROWS, channels)
 
     heads_here = w_qkv.shape[1] // (3 * HS)

time: 198 us -> 195 us (0.985)
  waiting for transfers between devices: 47.6 us -> 20.6 us
  blocking collectives: 41.4 us -> 58.5 us
  other arithmetic: 12.9 us -> 0.37 us
  Pallas kernels: 16.9 us -> 28.3 us
  local copies, waits for them, and re-layouts: 7.27 us -> 15.7 us
    all_to_all x1 -> x2, blocking collectives: 19.4 us -> 36.7 us  [spread(): lax.all_to_all(jnp.broadcast_to(block[None], (size,) + block.shape), axis...]
    all_to_all x1 -> x2, waiting for transfers between devices: 28.1 us -> 14.5 us  [the longest x1 10.4 us: shards(): lax.all_to_all(send.reshape(n_seq, capacity, send.shape[1]), SEQ_AXES, 0,...]
    ppermute x13 -> x9, waiting for transfers between devices: 14.1 us -> 0.63 us  [rotate(): lax.ppermute(block, axis, [(i, (i + step) % size) for i in range(size)])]
    reduce_sum x3 -> x0, other arithmetic: 11.2 us -> none  [the longest x1 9.59 us: layer_norm(): row_mean = jnp.mean(values, axis=-1, keepdims=True)]
    ppermute x13 -> x9, starting transfers between devices: 46.2 us -> 35.5 us  [rotate(): lax.ppermute(block, axis, [(i, (i + step) % size) for i in range(size)])]
    all_to_all x1 -> x2, starting transfers between devices: 19.6 us -> 29.7 us  [the longest x1 20.6 us: shards(): lax.all_to_all(send.reshape(n_seq, capacity, send.shape[1]), SEQ_AXES, 0,...]
    pallas_call x3 -> x6, Pallas kernels: 2.66 us -> 12.3 us  [vmem_call(): pl.pallas_call(body, in_specs=[vmem] * len(operands), out_specs=jax.tree....]
    unnamed x48 -> x62, local copies, waits for them, and re-layouts: 4.29 us -> 9.56 us
  transfers between devices with their start and end apart: 15 -> 12, of which waited for: 4 -> 4; matrix products, arithmetic and copies ran while one was open for 8% -> 4% of each run, Pallas kernels for 3% -> 8%
where the time goes in v4:
time: 195 us; the launch traced here: 194 us
  starting transfers between devices  69.4 us (36%)
  blocking collectives  58.5 us (30%)
  Pallas kernels  28.3 us (15%)
  waiting for transfers between devices  20.6 us (11%)
  local copies, waits for them, and re-layouts  15.7 us (8%)
    all_to_all x2, blocking collectives, spread(): lax.all_to_all(jnp.broadcast_to(block[None], (size,) + block.shape), axis...  36.7 us
    ppermute x9, starting transfers between devices, rotate(): lax.ppermute(block, axis, [(i, (i + step) % size) for i in range(size)])  35.5 us
    all_to_all x1, starting transfers between devices, shards(): lax.all_to_all(send.reshape(n_seq, capacity, send.shape[1]), SEQ_AXES, 0,...  20.6 us
    pallas_call x5, Pallas kernels, local_call(): pl.pallas_call(body, in_specs=[pl.BlockSpec(memory_space=pltpu.SMEM)] + [...  13 us
    pallas_call x6, Pallas kernels, vmem_call(): pl.pallas_call(body, in_specs=[vmem] * len(operands), out_specs=jax.tree....  12.3 us
    all_gather x1, blocking collectives, shards(): half_kv = lax.all_gather(z_kv, 'y', axis=0, tiled=True)  11.4 us
    all_to_all x1, waiting for transfers between devices, shards(): lax.all_to_all(send.reshape(n_seq, capacity, send.shape[1]), SEQ_AXES, 0,...  10.4 us
    all_to_all x1, blocking collectives, shards(): lax.all_to_all(partial_out.reshape(n_section, width_part, ROWS), 'section...  10.3 us
  transfers between devices with their start and end apart: 12, of which 4 were waited for; matrix products, arithmetic and copies ran while one was open for 4% of the time, Pallas kernels for 8%

profile of v4, /device:TPU:1, one launch (start us, length us, event | category | flops | bytes accessed | tf_op | source)
XLA Modules:
  0.0 194.2 jit_solution(11194577248774927399)
XLA Ops:
  0.0 3.0 %shard_map.199 = bf16[1552,384]{1,0:T(8,128)(2,1)} custom-call(s32[1]{0:T(128)} %bitcast.core_ref, bf16[384,768]{1,0:T(8,128)(2,1)} %up.1, bf16[384,768]{1,0:T(8,128)(2,1)} %w_down.3, bf16[768,384]{1,0:T(8,128)(2,1)} %w_head.3, bf16[384,768]{1,0:T(8,128)(2,1)} %w_in.5, bf16[384]{0:T(512)(128)(2,1)} %bias.1), custom_call_target="tpu_custom_call" | custom-call | bytes 2359296 | tf_op jit(solution)/shard_map/pallas_call | solution.py:77
  3.0 5.2 %collective-permute-start.1 = (bf16[1552,384]{1,0:T(8,128)(2,1)}, bf16[1552,384]{1,0:T(8,128)(2,1)S(1)}, u32[]{:S(2)}, u32[]{:S(2)}) collective-permute-start(bf16[1552,384]{1,0:T(8,128)(2,1)} %shard_map.199), channel_id=1, source_target_pairs={{0,384},{128,0},{256,128},{384,256},{1,385},{129,1},{257,129},{385... | collective-permute-start | bytes 3575816 | tf_op jit(solution)/shard_map/ppermute | solution.py:29
  14.1 20.6 %all-to-all-start = ((bf16[128,2,1664]{2,1,0:T(2,128)(2,1)}), bf16[128,2,1664]{2,1,0:T(2,128)(2,1)}, u32[]{:S(2)}, u32[]{:S(2)}) async-start(bf16[128,2,1664]{2,1,0:T(2,128)(2,1)} %reshape.49), calls=%async_computation | async-start | bytes 1703936 | tf_op jit(solution)/shard_map/all_to_all | solution.py:441
  35.8 4.5 %collective-permute-start.3 = (bf16[784,384]{1,0:T(8,128)(2,1)S(1)}, bf16[784,384]{1,0:T(8,128)(2,1)}, u32[]{:S(2)}, u32[]{:S(2)}) collective-permute-start(bf16[784,384]{1,0:T(8,128)(2,1)S(1)} %slice.37), channel_id=1, source_target_pairs={{0,384},{128,0},{256,128},{384,256},{1,385},{129,1},{257,129},{385... | collective-permute-start | bytes 1806344 | tf_op jit(solution)/shard_map/ppermute | solution.py:29
  40.3 1.9 collective-permute-start.2
  42.2 5.9 %collective-permute-start.4 = (bf16[1552,384]{1,0:T(8,128)(2,1)S(1)}, bf16[1552,384]{1,0:T(8,128)(2,1)S(1)}, u32[]{:S(2)}, u32[]{:S(2)}) collective-permute-start(bf16[1552,384]{1,0:T(8,128)(2,1)S(1)} %collective-permute-done.left), channel_id=1, source_target_pairs={{0,1},{1,0},{2,3},{3,2},{4,5},{5,4},{6,7},{7,6},{8,9},{9,8},{10,11... | collective-permute-start | bytes 3575816 | tf_op jit(solution)/shard_map/ppermute | solution.py:29
  48.2 1.9 collective-permute-start.5
  50.1 9.0 %shard_map.200 = (bf16[512,768]{1,0:T(8,128)(2,1)S(1)}, f32[8,768]{1,0:T(8,128)S(1)}) custom-call(bf16[8,8,8,768]{3,2,1,0:T(8,128)(2,1)S(1)} %copy-done.15, f32[49,768]{1,0:T(8,128)S(1)} %reshape.48.dw_weight, f32[1,768]{1,0:T(1,128)S(1)} %broadcast_in_dim.88.dw_bias, f32[1,768]{1,0:T(1,128)S(1)} %broadcast_in_dim.89.gain), custom_call_target="tpu_custom_call" | custom-call | flops 30000001024 | bytes 8000000 | tf_op jit(solution)/shard_map/pallas_call | solution.py:365
  59.1 2.4 %collective-permute-start.7 = (bf16[784,384]{1,0:T(8,128)(2,1)}, bf16[784,384]{1,0:T(8,128)(2,1)}, u32[]{:S(2)}, u32[]{:S(2)}) collective-permute-start(bf16[784,384]{1,0:T(8,128)(2,1)} %collective-permute-done.3.high), channel_id=1, source_target_pairs={{0,1},{1,0},{2,3},{3,2},{4,5},{5,4},{6,7},{7,6},{8,9},{9,8},{10,11... | collective-permute-start | bytes 1806344 | tf_op jit(solution)/shard_map/ppermute | solution.py:29
  61.5 1.9 collective-permute-start.6
  63.6 2.3 %shard_map.202.hid = f32[3,8,384]{2,1,0:T(8,128)S(1)} custom-call(s32[6]{0:T(128)S(1)} %stack.27.where, bf16[512,768]{1,0:T(8,128)(2,1)S(1)} %get-tuple-element.36.maps, bf16[384,768]{1,0:T(8,128)(2,1)S(1)} %copy-done.13, bf16[1,384]{1,0:T(2,128)(2,1)S(1)} %broadcast_in_dim.93.bias, bf16[1552,384]{1,0:T(8,128)(2,1)S(1)} %collective-permute-done.left, ...), custom_call_target="tpu_custom_call" | custom-call | flops 2000000000 | bytes 6000000 | tf_op jit(solution)/shard_map/pallas_call | solution.py:252
  67.9 10.4 %all-to-all-done = bf16[128,2,1664]{2,1,0:T(2,128)(2,1)} async-done(((bf16[128,2,1664]{2,1,0:T(2,128)(2,1)}), bf16[128,2,1664]{2,1,0:T(2,128)(2,1)}, u32[]{:S(2)}, u32[]{:S(2)}) %all-to-all-start) | async-done | bytes 852000 | tf_op jit(solution)/shard_map/all_to_all | solution.py:441
  78.3 3.1 %reshape.50.got = bf16[256,1664]{1,0:T(8,128)(2,1)} reshape(bf16[128,2,1664]{2,1,0:T(2,128)(2,1)} %all-to-all-done) | data formatting | bytes 1703936 | tf_op jit(solution)/shard_map/reshape | solution.py:443
  82.5 5.5 %shard_map.203 = bf16[8,896]{1,0:T(8,128)(2,1)S(1)} custom-call(s32[6]{0:T(128)S(1)} %stack.27.where, bf16[512,768]{1,0:T(8,128)(2,1)S(1)} %get-tuple-element.36.maps, f32[3,8,384]{2,1,0:T(8,128)S(1)} %shard_map.202.hid, f32[8,768]{1,0:T(8,128)S(1)} %get-tuple-element.41.feat_mean, f32[1,768]{1,0:T(1,128)S(1)} %broadcast_in_dim.94.layer_scale, ...), custom_call_target="tpu_custom_call" | custom-call | flops 2000000000 | bytes 8000000 | tf_op jit(solution)/shard_map/pallas_call | solution.py:252
  88.0 19.6 %all_to_all.30 = bf16[16,8,896]{2,1,0:T(8,128)(2,1)S(1)} all-to-all(bf16[16,8,896]{2,1,0:T(8,128)(2,1)S(1)} %broadcast_in_dim.100), channel_id=1, replica_groups=mesh['section'=4,'z'=16,'y'=4,'core'=2] {'z'}, dimensions={0} | all-to-all | bytes 458752 | tf_op jit(solution)/shard_map/all_to_all | solution.py:33
  109.4 9.1 %all-to-all-start.2 = ((bf16[8,32,896]{2,1,0:T(8,128)(2,1)}), bf16[8,32,896]{2,1,0:T(8,128)(2,1)S(1)}, u32[]{:S(2)}, u32[]{:S(2)}) async-start(bf16[8,32,896]{2,1,0:T(8,128)(2,1)} %bitcast.19), calls=%async_computation.2 | async-start | bytes 917504 | tf_op jit(solution)/shard_map/all_to_all | solution.py:513
  119.7 2.8 %shard_map.205.earlier = f32[64,768]{1,0:T(8,128)S(1)} custom-call(s32[6]{0:T(128)S(1)} %stack.27.where, bf16[256,1664]{1,0:T(8,128)(2,1)S(1)} %copy-done.7, bf16[384,768]{1,0:T(8,128)(2,1)S(1)} %copy-done.4, bf16[1552,384]{1,0:T(8,128)(2,1)S(1)} %copy-done.3, bf16[1552,384]{1,0:T(8,128)(2,1)S(1)} %copy-done.1, bf16[1552,384]{1,0:T(8,128)(2,1)} %copy-done.5, ...), custom_call_target="tpu_custom_call" | custom-call | flops 500000000 | bytes 4000000 | tf_op jit(solution)/shard_map/pallas_call | solution.py:252
  123.2 4.1 %all-to-all-done.2 = bf16[8,32,896]{2,1,0:T(8,128)(2,1)S(1)} async-done(((bf16[8,32,896]{2,1,0:T(8,128)(2,1)}), bf16[8,32,896]{2,1,0:T(8,128)(2,1)S(1)}, u32[]{:S(2)}, u32[]{:S(2)}) %all-to-all-start.2) | async-done | bytes 458784 | tf_op jit(solution)/shard_map/all_to_all | solution.py:513
  129.4 4.2 %all-to-all-start.3 = ((bf16[4,64,768]{2,1,0:T(8,128)(2,1)}), bf16[4,64,768]{2,1,0:T(8,128)(2,1)S(1)}, u32[]{:S(2)}, u32[]{:S(2)}) async-start(bf16[4,64,768]{2,1,0:T(8,128)(2,1)} %broadcast_in_dim.101), calls=%async_computation.3 | async-start | bytes 786432 | tf_op jit(solution)/shard_map/all_to_all | solution.py:33
  134.8 5.5 %all-to-all-done.3 = bf16[4,64,768]{2,1,0:T(8,128)(2,1)S(1)} async-done(((bf16[4,64,768]{2,1,0:T(8,128)(2,1)}), bf16[4,64,768]{2,1,0:T(8,128)(2,1)S(1)}, u32[]{:S(2)}, u32[]{:S(2)}) %all-to-all-start.3) | async-done | bytes 393248 | tf_op jit(solution)/shard_map/all_to_all | solution.py:33
  141.2 17.1 %all_to_all.31 = bf16[16,16,384]{2,1,0:T(8,128)(2,1)S(1)} all-to-all(bf16[16,16,384]{2,1,0:T(8,128)(2,1)S(1)} %broadcast_in_dim.104), channel_id=1, replica_groups=mesh['section'=4,'z'=16,'y'=4,'core'=2] {'z'}, dimensions={0} | all-to-all | bytes 393216 | tf_op jit(solution)/shard_map/all_to_all | solution.py:33
  158.3 11.4 %all_gather.3.kv = bf16[1024,384]{1,0:T(8,128)(2,1)S(1)} all-gather(bf16[256,384]{1,0:T(8,128)(2,1)S(1)} %bitcast.26), channel_id=1, replica_groups=mesh['section'=4,'z'=16,'y'=4,'core'=2] {'y'}, dimensions={0}, use_global_device_ids=true | all-gather | bytes 983040 | tf_op jit(solution)/shard_map/all_gather | solution.py:544
  169.7 9.7 %collective-permute-start.8 = (bf16[1024,384]{1,0:T(8,128)(2,1)S(1)}, bf16[1024,384]{1,0:T(8,128)(2,1)S(1)}, u32[]{:S(2)}, u32[]{:S(2)}) collective-permute-start(bf16[1024,384]{1,0:T(8,128)(2,1)S(1)} %all_gather.3.kv), channel_id=1, source_target_pairs={{0,1},{1,0},{2,3},{3,2},{4,5},{5,4},{6,7},{7,6},{8,9},{9,8},{10,11... | collective-permute-start | bytes 2359304 | tf_op jit(solution)/shard_map/ppermute | solution.py:29
  183.1 10.3 %all_to_all.32.parts = bf16[4,192,256]{2,1,0:T(8,128)(2,1)S(1)} all-to-all(bf16[4,192,256]{2,1,0:T(8,128)(2,1)S(1)} %bitcast.22), channel_id=1, replica_groups=mesh['section'=4,'z'=16,'y'=4,'core'=2] {'section'}, dimensions={0} | all-to-all | bytes 786432 | tf_op jit(solution)/shard_map/all_to_all | solution.py:566
  (113 shorter events, 21.3 us)
Async XLA Ops:
  3.0 32.0 %collective-permute-start.1 = (bf16[1552,384]{1,0:T(8,128)(2,1)}, bf16[1552,384]{1,0:T(8,128)(2,1)S(1)}, u32[]{:S(2)}, u32[]{:S(2)}) collective-permute-start(bf16[1552,384]{1,0:T(8,128)(2,1)} %shard_map.199), channel_id=1, source_target_pairs={{0,384},{128,0},{256,128},{384,256},{1,385},{129,1},{257,129},{385... | collective-permute-start | bytes 3575816 | tf_op jit(solution)/shard_map/ppermute | solution.py:29
  8.2 27.5 %collective-permute-start = (bf16[1552,384]{1,0:T(8,128)(2,1)}, bf16[1552,384]{1,0:T(8,128)(2,1)S(1)}, u32[]{:S(2)}, u32[]{:S(2)}) collective-permute-start(bf16[1552,384]{1,0:T(8,128)(2,1)} %shard_map.199), channel_id=1, source_target_pairs={{0,128},{128,256},{256,384},{384,0},{1,129},{129,257},{257,385},{3... | collective-permute-start | bytes 3575816 | tf_op jit(solution)/shard_map/ppermute | solution.py:29
  14.0 20.6 %copy-start.18 = (bf16[384]{0:T(512)(128)(2,1)S(1)}, bf16[384]{0:T(512)(128)(2,1)}, u32[]{:S(2)}) copy-start(bf16[384]{0:T(512)(128)(2,1)} %bias.1) | copy-start | bytes 2308
  14.0 20.7 %copy-start.17 = (f32[7,7,768]{2,1,0:T(8,128)S(1)}, f32[7,7,768]{2,1,0:T(8,128)}, u32[]{:S(2)}) copy-start(f32[7,7,768]{2,1,0:T(8,128)} %param.22) | copy-start | bytes 451588
  14.0 20.7 %copy-start.19 = (f32[768]{0:T(1024)S(1)}, f32[768]{0:T(1024)}, u32[]{:S(2)}) copy-start(f32[768]{0:T(1024)} %param.23) | copy-start | bytes 9220
  14.0 20.7 %copy-start.20 = (f32[768]{0:T(1024)S(1)}, f32[768]{0:T(1024)}, u32[]{:S(2)}) copy-start(f32[768]{0:T(1024)} %param.24) | copy-start | bytes 9220
  14.1 20.7 %copy-start.21 = (f32[768]{0:T(1024)S(1)}, f32[768]{0:T(1024)}, u32[]{:S(2)}) copy-start(f32[768]{0:T(1024)} %param.29) | copy-start | bytes 9220
  14.1 20.8 %copy-start.22 = (f32[768]{0:T(1024)S(1)}, f32[768]{0:T(1024)}, u32[]{:S(2)}) copy-start(f32[768]{0:T(1024)} %param.28) | copy-start | bytes 9220
  14.1 20.8 %copy-start.23 = (f32[768]{0:T(1024)S(1)}, f32[768]{0:T(1024)}, u32[]{:S(2)}) copy-start(f32[768]{0:T(1024)} %param.30) | copy-start | bytes 9220
  14.1 64.2 %all-to-all-start = ((bf16[128,2,1664]{2,1,0:T(2,128)(2,1)}), bf16[128,2,1664]{2,1,0:T(2,128)(2,1)}, u32[]{:S(2)}, u32[]{:S(2)}) async-start(bf16[128,2,1664]{2,1,0:T(2,128)(2,1)} %reshape.49), calls=%async_computation | async-start | bytes 1703936 | tf_op jit(solution)/shard_map/all_to_all | solution.py:441
  35.0 28.5 %copy-start = (bf16[1552,384]{1,0:T(8,128)(2,1)}, bf16[1552,384]{1,0:T(8,128)(2,1)S(1)}, u32[]{:S(2)}) copy-start(bf16[1552,384]{1,0:T(8,128)(2,1)S(1)} %collective-permute-done.1.right) | copy-start | bytes 3575812
  35.7 27.9 %copy-start.2 = (bf16[1552,384]{1,0:T(8,128)(2,1)}, bf16[1552,384]{1,0:T(8,128)(2,1)S(1)}, u32[]{:S(2)}) copy-start(bf16[1552,384]{1,0:T(8,128)(2,1)S(1)} %collective-permute-done.left) | copy-start | bytes 3575812
  35.8 27.8 %copy-start.13 = (bf16[384,768]{1,0:T(8,128)(2,1)S(1)}, bf16[384,768]{1,0:T(8,128)(2,1)}, u32[]{:S(2)}) copy-start(bf16[384,768]{1,0:T(8,128)(2,1)} %up.1) | copy-start | bytes 1769476
  35.8 23.3 %collective-permute-start.3 = (bf16[784,384]{1,0:T(8,128)(2,1)S(1)}, bf16[784,384]{1,0:T(8,128)(2,1)}, u32[]{:S(2)}, u32[]{:S(2)}) collective-permute-start(bf16[784,384]{1,0:T(8,128)(2,1)S(1)} %slice.37), channel_id=1, source_target_pairs={{0,384},{128,0},{256,128},{384,256},{1,385},{129,1},{257,129},{385... | collective-permute-start | bytes 1806344 | tf_op jit(solution)/shard_map/ppermute | solution.py:29
  40.3 18.8 %collective-permute-start.2 = (bf16[768,384]{1,0:T(8,128)(2,1)S(1)}, bf16[768,384]{1,0:T(8,128)(2,1)}, u32[]{:S(2)}, u32[]{:S(2)}) collective-permute-start(bf16[768,384]{1,0:T(8,128)(2,1)S(1)} %slice.36), channel_id=1, source_target_pairs={{0,128},{128,256},{256,384},{384,0},{1,129},{129,257},{257,385},{3... | collective-permute-start | bytes 1769480 | tf_op jit(solution)/shard_map/ppermute | solution.py:29
  42.2 21.3 %collective-permute-start.4 = (bf16[1552,384]{1,0:T(8,128)(2,1)S(1)}, bf16[1552,384]{1,0:T(8,128)(2,1)S(1)}, u32[]{:S(2)}, u32[]{:S(2)}) collective-permute-start(bf16[1552,384]{1,0:T(8,128)(2,1)S(1)} %collective-permute-done.left), channel_id=1, source_target_pairs={{0,1},{1,0},{2,3},{3,2},{4,5},{5,4},{6,7},{7,6},{8,9},{9,8},{10,11... | collective-permute-start | bytes 3575816 | tf_op jit(solution)/shard_map/ppermute | solution.py:29
  48.2 15.4 %collective-permute-start.5 = (bf16[1552,384]{1,0:T(8,128)(2,1)S(1)}, bf16[1552,384]{1,0:T(8,128)(2,1)S(1)}, u32[]{:S(2)}, u32[]{:S(2)}) collective-permute-start(bf16[1552,384]{1,0:T(8,128)(2,1)S(1)} %collective-permute-done.1.right), channel_id=1, source_target_pairs={{0,1},{1,0},{2,3},{3,2},{4,5},{5,4},{6,7},{7,6},{8,9},{9,8},{10,11... | collective-permute-start | bytes 3575816 | tf_op jit(solution)/shard_map/ppermute | solution.py:29
  59.1 22.3 %collective-permute-start.7 = (bf16[784,384]{1,0:T(8,128)(2,1)}, bf16[784,384]{1,0:T(8,128)(2,1)}, u32[]{:S(2)}, u32[]{:S(2)}) collective-permute-start(bf16[784,384]{1,0:T(8,128)(2,1)} %collective-permute-done.3.high), channel_id=1, source_target_pairs={{0,1},{1,0},{2,3},{3,2},{4,5},{5,4},{6,7},{7,6},{8,9},{9,8},{10,11... | collective-permute-start | bytes 1806344 | tf_op jit(solution)/shard_map/ppermute | solution.py:29
  61.5 19.9 %collective-permute-start.6 = (bf16[768,384]{1,0:T(8,128)(2,1)}, bf16[768,384]{1,0:T(8,128)(2,1)}, u32[]{:S(2)}, u32[]{:S(2)}) collective-permute-start(bf16[768,384]{1,0:T(8,128)(2,1)} %collective-permute-done.2.low), channel_id=1, source_target_pairs={{0,1},{1,0},{2,3},{3,2},{4,5},{5,4},{6,7},{7,6},{8,9},{9,8},{10,11... | collective-permute-start | bytes 1769480 | tf_op jit(solution)/shard_map/ppermute | solution.py:29
  82.5 36.1 %copy-start.3 = (bf16[1552,384]{1,0:T(8,128)(2,1)S(1)}, bf16[1552,384]{1,0:T(8,128)(2,1)}, u32[]{:S(2)}) copy-start(bf16[1552,384]{1,0:T(8,128)(2,1)} %copy-done.2) | copy-start | bytes 3575812
  88.0 30.6 %copy-start.1 = (bf16[1552,384]{1,0:T(8,128)(2,1)S(1)}, bf16[1552,384]{1,0:T(8,128)(2,1)}, u32[]{:S(2)}) copy-start(bf16[1552,384]{1,0:T(8,128)(2,1)} %copy-done) | copy-start | bytes 3575812
  109.4 17.9 %all-to-all-start.2 = ((bf16[8,32,896]{2,1,0:T(8,128)(2,1)}), bf16[8,32,896]{2,1,0:T(8,128)(2,1)S(1)}, u32[]{:S(2)}, u32[]{:S(2)}) async-start(bf16[8,32,896]{2,1,0:T(8,128)(2,1)} %bitcast.19), calls=%async_computation.2 | async-start | bytes 917504 | tf_op jit(solution)/shard_map/all_to_all | solution.py:513
  129.4 10.9 %all-to-all-start.3 = ((bf16[4,64,768]{2,1,0:T(8,128)(2,1)}), bf16[4,64,768]{2,1,0:T(8,128)(2,1)S(1)}, u32[]{:S(2)}, u32[]{:S(2)}) async-start(bf16[4,64,768]{2,1,0:T(8,128)(2,1)} %broadcast_in_dim.101), calls=%async_computation.3 | async-start | bytes 786432 | tf_op jit(solution)/shard_map/all_to_all | solution.py:33
  169.7 12.3 %collective-permute-start.8 = (bf16[1024,384]{1,0:T(8,128)(2,1)S(1)}, bf16[1024,384]{1,0:T(8,128)(2,1)S(1)}, u32[]{:S(2)}, u32[]{:S(2)}) collective-permute-start(bf16[1024,384]{1,0:T(8,128)(2,1)S(1)} %all_gather.3.kv), channel_id=1, source_target_pairs={{0,1},{1,0},{2,3},{3,2},{4,5},{5,4},{6,7},{7,6},{8,9},{9,8},{10,11... | collective-permute-start | bytes 2359304 | tf_op jit(solution)/shard_map/ppermute | solution.py:29
  (17 other events, 77.8 us)

commit v5 on v4

--- a/solution.py
+++ b/solution.py
@@ -255,7 +255,7 @@
         out_specs=jax.tree.map(lambda _: vmem, outs),
         out_shape=outs,
         scratch_shapes=scratch,
-        compiler_params=pltpu.CompilerParams(vmem_limit_bytes=48 * 2**20),
+        compiler_params=pltpu.CompilerParams(vmem_limit_bytes=24 * 2**20),
         cost_estimate=pl.CostEstimate(flops=flops, bytes_accessed=size, transcendentals=0),
     )(*operands)
 
@@ -368,7 +368,7 @@
         out_specs=jax.tree.map(lambda _: vmem, outs),
         out_shape=outs,
         scratch_shapes=list(scratch),
-        compiler_params=pltpu.CompilerParams(vmem_limit_bytes=40 * 2**20),
+        compiler_params=pltpu.CompilerParams(vmem_limit_bytes=16 * 2**20),
         cost_estimate=pl.CostEstimate(flops=flops, bytes_accessed=size, transcendentals=exps),
     )(*operands)
 
@@ -479,7 +479,6 @@
         6_000_000,
         where, normed_maps, w_up, row(b_up), left, right, left_swap, right_swap,
     )
-    got_prior, hid = lax.optimization_barrier((got_prior, hid))
     fresh = local_call(
         late_kernel,
         jax.ShapeDtypeStruct((tiles, channels + 128), BF16),
@@ -490,6 +489,7 @@
         code_fresh, w_down, w_head, w_in, left, right, left_swap, right_swap, low, high, low_swap,
         high_swap,
     )
+    got_prior, fresh = lax.optimization_barrier((got_prior, fresh))
     x_earlier = local_call(
         earlier_kernel,
         jax.ShapeDtypeStruct((q_rows, channels), F32),

time: 195 us -> 189 us (0.969)
  waiting for transfers between devices: 20.6 us -> 16.1 us
  Pallas kernels: 28.3 us -> 25.3 us
    pallas_call x5, Pallas kernels: 13 us -> 8.98 us  [local_call(): pl.pallas_call(body, in_specs=[pl.BlockSpec(memory_space=pltpu.SMEM)] + [...]
    all_to_all x1, waiting for transfers between devices: 4.12 us -> 0.87 us  [shards(): lax.all_to_all(to_plane.reshape(plane, room, channels + 128), ('y', 'core...]
    unnamed x62 -> x68, local copies, waits for them, and re-layouts: 9.56 us -> 11 us
  transfers between devices with their start and end apart: 12 -> 12, of which waited for: 4 -> 5; matrix products, arithmetic and copies ran while one was open for 4% -> 2% of each run, Pallas kernels for 8% -> 9%
where the time goes in v5:
time: 189 us; the launch traced here: 188 us
  starting transfers between devices  69.2 us (37%)
  blocking collectives  58.7 us (31%)
  Pallas kernels  25.3 us (13%)
  local copies, waits for them, and re-layouts  17.1 us (9%)
  waiting for transfers between devices  16.1 us (9%)
    all_to_all x2, blocking collectives, spread(): lax.all_to_all(jnp.broadcast_to(block[None], (size,) + block.shape), axis...  36.6 us
    ppermute x9, starting transfers between devices, rotate(): lax.ppermute(block, axis, [(i, (i + step) % size) for i in range(size)])  35.3 us
    all_to_all x1, starting transfers between devices, shards(): lax.all_to_all(send.reshape(n_seq, capacity, send.shape[1]), SEQ_AXES, 0,...  20.6 us
    pallas_call x6, Pallas kernels, vmem_call(): pl.pallas_call(body, in_specs=[vmem] * len(operands), out_specs=jax.tree....  13.3 us
    all_gather x1, blocking collectives, shards(): half_kv = lax.all_gather(z_kv, 'y', axis=0, tiled=True)  11.9 us
    unnamed x68, local copies, waits for them, and re-layouts  11 us
    all_to_all x1, blocking collectives, shards(): lax.all_to_all(partial_out.reshape(n_section, width_part, ROWS), 'section...  10.2 us
    all_to_all x1, starting transfers between devices, shards(): lax.all_to_all(to_plane.reshape(plane, room, channels + 128), ('y', 'core...  9.16 us
  transfers between devices with their start and end apart: 12, of which 5 were waited for; matrix products, arithmetic and copies ran while one was open for 2% of the time, Pallas kernels for 9%

profile of v5, /device:TPU:1, one launch (start us, length us, event | category | flops | bytes accessed | tf_op | source)
XLA Modules:
  0.0 188.1 jit_solution(9940956486113741766)
XLA Ops:
  0.0 3.0 %shard_map.199 = bf16[1552,384]{1,0:T(8,128)(2,1)} custom-call(s32[1]{0:T(128)} %bitcast.core_ref, bf16[384,768]{1,0:T(8,128)(2,1)} %up.1, bf16[384,768]{1,0:T(8,128)(2,1)} %w_down.3, bf16[768,384]{1,0:T(8,128)(2,1)} %w_head.3, bf16[384,768]{1,0:T(8,128)(2,1)} %w_in.5, bf16[384]{0:T(512)(128)(2,1)} %bias.1), custom_call_target="tpu_custom_call" | custom-call | bytes 2359296 | tf_op jit(solution)/shard_map/pallas_call | solution.py:77
  3.0 5.2 %collective-permute-start.1 = (bf16[1552,384]{1,0:T(8,128)(2,1)}, bf16[1552,384]{1,0:T(8,128)(2,1)S(1)}, u32[]{:S(2)}, u32[]{:S(2)}) collective-permute-start(bf16[1552,384]{1,0:T(8,128)(2,1)} %shard_map.199), channel_id=1, source_target_pairs={{0,384},{128,0},{256,128},{384,256},{1,385},{129,1},{257,129},{385... | collective-permute-start | bytes 3575816 | tf_op jit(solution)/shard_map/ppermute | solution.py:29
  8.3 1.9 %collective-permute-start = (bf16[1552,384]{1,0:T(8,128)(2,1)}, bf16[1552,384]{1,0:T(8,128)(2,1)S(1)}, u32[]{:S(2)}, u32[]{:S(2)}) collective-permute-start(bf16[1552,384]{1,0:T(8,128)(2,1)} %shard_map.199), channel_id=1, source_target_pairs={{0,128},{128,256},{256,384},{384,0},{1,129},{129,257},{257,385},{3... | collective-permute-start | bytes 3575816 | tf_op jit(solution)/shard_map/ppermute | solution.py:29
  14.1 20.6 %all-to-all-start = ((bf16[128,2,1664]{2,1,0:T(2,128)(2,1)}), bf16[128,2,1664]{2,1,0:T(2,128)(2,1)}, u32[]{:S(2)}, u32[]{:S(2)}) async-start(bf16[128,2,1664]{2,1,0:T(2,128)(2,1)} %reshape.48), calls=%async_computation | async-start | bytes 1703936 | tf_op jit(solution)/shard_map/all_to_all | solution.py:441
  35.8 4.4 %collective-permute-start.3 = (bf16[784,384]{1,0:T(8,128)(2,1)S(1)}, bf16[784,384]{1,0:T(8,128)(2,1)S(1)}, u32[]{:S(2)}, u32[]{:S(2)}) collective-permute-start(bf16[784,384]{1,0:T(8,128)(2,1)S(1)} %slice.37), channel_id=1, source_target_pairs={{0,384},{128,0},{256,128},{384,256},{1,385},{129,1},{257,129},{385... | collective-permute-start | bytes 1806344 | tf_op jit(solution)/shard_map/ppermute | solution.py:29
  40.2 1.9 %collective-permute-start.2 = (bf16[768,384]{1,0:T(8,128)(2,1)S(1)}, bf16[768,384]{1,0:T(8,128)(2,1)S(1)}, u32[]{:S(2)}, u32[]{:S(2)}) collective-permute-start(bf16[768,384]{1,0:T(8,128)(2,1)S(1)} %slice.36), channel_id=1, source_target_pairs={{0,128},{128,256},{256,384},{384,0},{1,129},{129,257},{257,385},{3... | collective-permute-start | bytes 1769480 | tf_op jit(solution)/shard_map/ppermute | solution.py:29
  42.1 6.1 %collective-permute-start.4 = (bf16[1552,384]{1,0:T(8,128)(2,1)S(1)}, bf16[1552,384]{1,0:T(8,128)(2,1)S(1)}, u32[]{:S(2)}, u32[]{:S(2)}) collective-permute-start(bf16[1552,384]{1,0:T(8,128)(2,1)S(1)} %collective-permute-done.left), channel_id=1, source_target_pairs={{0,1},{1,0},{2,3},{3,2},{4,5},{5,4},{6,7},{7,6},{8,9},{9,8},{10,11... | collective-permute-start | bytes 3575816 | tf_op jit(solution)/shard_map/ppermute | solution.py:29
  48.2 1.9 %collective-permute-start.5 = (bf16[1552,384]{1,0:T(8,128)(2,1)S(1)}, bf16[1552,384]{1,0:T(8,128)(2,1)S(1)}, u32[]{:S(2)}, u32[]{:S(2)}) collective-permute-start(bf16[1552,384]{1,0:T(8,128)(2,1)S(1)} %collective-permute-done.1.right), channel_id=1, source_target_pairs={{0,1},{1,0},{2,3},{3,2},{4,5},{5,4},{6,7},{7,6},{8,9},{9,8},{10,11... | collective-permute-start | bytes 3575816 | tf_op jit(solution)/shard_map/ppermute | solution.py:29
  50.1 8.8 %shard_map.201 = (bf16[512,768]{1,0:T(8,128)(2,1)S(1)}, f32[8,768]{1,0:T(8,128)S(1)}) custom-call(bf16[8,8,8,768]{3,2,1,0:T(8,128)(2,1)S(1)} %copy-done.17, f32[49,768]{1,0:T(8,128)S(1)} %reshape.50.dw_weight, f32[1,768]{1,0:T(1,128)S(1)} %broadcast_in_dim.91.dw_bias, f32[1,768]{1,0:T(1,128)S(1)} %broadcast_in_dim.92.gain), custom_call_target="tpu_custom_call" | custom-call | flops 30000001024 | bytes 8000000 | tf_op jit(solution)/shard_map/pallas_call | solution.py:365
  59.0 2.4 %collective-permute-start.7 = (bf16[784,384]{1,0:T(8,128)(2,1)S(1)}, bf16[784,384]{1,0:T(8,128)(2,1)S(1)}, u32[]{:S(2)}, u32[]{:S(2)}) collective-permute-start(bf16[784,384]{1,0:T(8,128)(2,1)S(1)} %collective-permute-done.3.high), channel_id=1, source_target_pairs={{0,1},{1,0},{2,3},{3,2},{4,5},{5,4},{6,7},{7,6},{8,9},{9,8},{10,11... | collective-permute-start | bytes 1806344 | tf_op jit(solution)/shard_map/ppermute | solution.py:29
  61.4 1.9 %collective-permute-start.6 = (bf16[768,384]{1,0:T(8,128)(2,1)S(1)}, bf16[768,384]{1,0:T(8,128)(2,1)S(1)}, u32[]{:S(2)}, u32[]{:S(2)}) collective-permute-start(bf16[768,384]{1,0:T(8,128)(2,1)S(1)} %collective-permute-done.2.low), channel_id=1, source_target_pairs={{0,1},{1,0},{2,3},{3,2},{4,5},{5,4},{6,7},{7,6},{8,9},{9,8},{10,11... | collective-permute-start | bytes 1769480 | tf_op jit(solution)/shard_map/ppermute | solution.py:29
  63.5 2.3 %shard_map.202.hid = f32[3,8,384]{2,1,0:T(8,128)S(1)} custom-call(s32[6]{0:T(128)S(1)} %stack.27.where, bf16[512,768]{1,0:T(8,128)(2,1)S(1)} %get-tuple-element.37.maps, bf16[384,768]{1,0:T(8,128)(2,1)S(1)} %copy-done.15, bf16[1,384]{1,0:T(2,128)(2,1)S(1)} %broadcast_in_dim.93.bias, bf16[1552,384]{1,0:T(8,128)(2,1)S(1)} %collective-permute-done.left, ...), custom_call_target="tpu_custom_call" | custom-call | flops 2000000000 | bytes 6000000 | tf_op jit(solution)/shard_map/pallas_call | solution.py:252
  65.8 2.9 %shard_map.203 = bf16[8,896]{1,0:T(8,128)(2,1)S(1)} custom-call(s32[6]{0:T(128)S(1)} %stack.27.where, bf16[512,768]{1,0:T(8,128)(2,1)S(1)} %get-tuple-element.37.maps, f32[3,8,384]{2,1,0:T(8,128)S(1)} %shard_map.202.hid, f32[8,768]{1,0:T(8,128)S(1)} %get-tuple-element.40.feat_mean, f32[1,768]{1,0:T(1,128)S(1)} %broadcast_in_dim.94.layer_scale, ...), custom_call_target="tpu_custom_call" | custom-call | flops 2000000000 | bytes 8000000 | tf_op jit(solution)/shard_map/pallas_call | solution.py:252
  69.6 8.8 %all-to-all-done = bf16[128,2,1664]{2,1,0:T(2,128)(2,1)} async-done(((bf16[128,2,1664]{2,1,0:T(2,128)(2,1)}), bf16[128,2,1664]{2,1,0:T(2,128)(2,1)}, u32[]{:S(2)}, u32[]{:S(2)}) %all-to-all-start) | async-done | bytes 852000 | tf_op jit(solution)/shard_map/all_to_all | solution.py:441
  78.3 3.1 %reshape.49.got = bf16[256,1664]{1,0:T(8,128)(2,1)} reshape(bf16[128,2,1664]{2,1,0:T(2,128)(2,1)} %all-to-all-done) | data formatting | bytes 1703936 | tf_op jit(solution)/shard_map/reshape | solution.py:443
  81.4 19.5 %all_to_all.30 = bf16[16,8,896]{2,1,0:T(8,128)(2,1)S(1)} all-to-all(bf16[16,8,896]{2,1,0:T(8,128)(2,1)S(1)} %broadcast_in_dim.100), channel_id=1, replica_groups=mesh['section'=4,'z'=16,'y'=4,'core'=2] {'z'}, dimensions={0} | all-to-all | bytes 458752 | tf_op jit(solution)/shard_map/all_to_all | solution.py:33
  102.7 9.2 %all-to-all-start.2 = ((bf16[8,32,896]{2,1,0:T(8,128)(2,1)}), bf16[8,32,896]{2,1,0:T(8,128)(2,1)S(1)}, u32[]{:S(2)}, u32[]{:S(2)}) async-start(bf16[8,32,896]{2,1,0:T(8,128)(2,1)} %bitcast.19), calls=%async_computation.2 | async-start | bytes 917504 | tf_op jit(solution)/shard_map/all_to_all | solution.py:513
  122.7 4.2 %all-to-all-start.3 = ((bf16[4,64,768]{2,1,0:T(8,128)(2,1)}), bf16[4,64,768]{2,1,0:T(8,128)(2,1)S(1)}, u32[]{:S(2)}, u32[]{:S(2)}) async-start(bf16[4,64,768]{2,1,0:T(8,128)(2,1)} %broadcast_in_dim.101), calls=%async_computation.3 | async-start | bytes 786432 | tf_op jit(solution)/shard_map/all_to_all | solution.py:33
  128.1 5.5 %all-to-all-done.3 = bf16[4,64,768]{2,1,0:T(8,128)(2,1)S(1)} async-done(((bf16[4,64,768]{2,1,0:T(8,128)(2,1)}), bf16[4,64,768]{2,1,0:T(8,128)(2,1)S(1)}, u32[]{:S(2)}, u32[]{:S(2)}) %all-to-all-start.3) | async-done | bytes 393248 | tf_op jit(solution)/shard_map/all_to_all | solution.py:33
  134.5 17.1 %all_to_all.31 = bf16[16,16,384]{2,1,0:T(8,128)(2,1)S(1)} all-to-all(bf16[16,16,384]{2,1,0:T(8,128)(2,1)S(1)} %broadcast_in_dim.104), channel_id=1, replica_groups=mesh['section'=4,'z'=16,'y'=4,'core'=2] {'z'}, dimensions={0} | all-to-all | bytes 393216 | tf_op jit(solution)/shard_map/all_to_all | solution.py:33
  151.5 11.9 %all_gather.3.kv = bf16[1024,384]{1,0:T(8,128)(2,1)S(1)} all-gather(bf16[256,384]{1,0:T(8,128)(2,1)S(1)} %bitcast.26), channel_id=1, replica_groups=mesh['section'=4,'z'=16,'y'=4,'core'=2] {'y'}, dimensions={0}, use_global_device_ids=true | all-gather | bytes 983040 | tf_op jit(solution)/shard_map/all_gather | solution.py:544
  163.4 9.5 %collective-permute-start.8 = (bf16[1024,384]{1,0:T(8,128)(2,1)S(1)}, bf16[1024,384]{1,0:T(8,128)(2,1)}, u32[]{:S(2)}, u32[]{:S(2)}) collective-permute-start(bf16[1024,384]{1,0:T(8,128)(2,1)S(1)} %all_gather.3.kv), channel_id=1, source_target_pairs={{0,1},{1,0},{2,3},{3,2},{4,5},{5,4},{6,7},{7,6},{8,9},{9,8},{10,11... | collective-permute-start | bytes 2359304 | tf_op jit(solution)/shard_map/ppermute | solution.py:29
  174.9 2.2 %shard_map.209 = bf16[768,256]{1,0:T(8,128)(2,1)S(1)} custom-call(f32[16,192]{1,0:T(8,128)S(1)} %get-tuple-element.48.far_q, bf16[1024,384]{1,0:T(8,128)(2,1)} %collective-permute-done.8.kv, s32[1,192]{1,0:T(1,128)S(1)} %broadcast_in_dim_reshape.3.off_lane, f32[256,192]{1,0:T(8,128)S(1)} %get-tuple-element.51.den, f32[256,192]{1,0:T(8,128)S(1)} %get-tuple-element.52.num, ...), custom_call_target="tpu_custom_call" | custom-call | flops 150000000 | bytes 2000000 | tf_op jit(solution)/shard_map/pallas_call | solution.py:365
  177.2 10.2 %all_to_all.32.parts = bf16[4,192,256]{2,1,0:T(8,128)(2,1)S(1)} all-to-all(bf16[4,192,256]{2,1,0:T(8,128)(2,1)S(1)} %bitcast.22), channel_id=1, replica_groups=mesh['section'=4,'z'=16,'y'=4,'core'=2] {'section'}, dimensions={0} | all-to-all | bytes 786432 | tf_op jit(solution)/shard_map/all_to_all | solution.py:566
  (119 shorter events, 22.4 us)
Async XLA Ops:
  0.0 10.2 %copy-start.28 = (s32[160]{0:T(256)S(1)}, s32[160]{0:T(256)}, u32[]{:S(2)}) copy-start(s32[160]{0:T(256)} %param.34) | copy-start | bytes 1924
  3.0 32.0 %collective-permute-start.1 = (bf16[1552,384]{1,0:T(8,128)(2,1)}, bf16[1552,384]{1,0:T(8,128)(2,1)S(1)}, u32[]{:S(2)}, u32[]{:S(2)}) collective-permute-start(bf16[1552,384]{1,0:T(8,128)(2,1)} %shard_map.199), channel_id=1, source_target_pairs={{0,384},{128,0},{256,128},{384,256},{1,385},{129,1},{257,129},{385... | collective-permute-start | bytes 3575816 | tf_op jit(solution)/shard_map/ppermute | solution.py:29
  8.3 27.5 %collective-permute-start = (bf16[1552,384]{1,0:T(8,128)(2,1)}, bf16[1552,384]{1,0:T(8,128)(2,1)S(1)}, u32[]{:S(2)}, u32[]{:S(2)}) collective-permute-start(bf16[1552,384]{1,0:T(8,128)(2,1)} %shard_map.199), channel_id=1, source_target_pairs={{0,128},{128,256},{256,384},{384,0},{1,129},{129,257},{257,385},{3... | collective-permute-start | bytes 3575816 | tf_op jit(solution)/shard_map/ppermute | solution.py:29
  14.0 20.6 %copy-start.21 = (bf16[384]{0:T(512)(128)(2,1)S(1)}, bf16[384]{0:T(512)(128)(2,1)}, u32[]{:S(2)}) copy-start(bf16[384]{0:T(512)(128)(2,1)} %bias.1) | copy-start | bytes 2308
  14.0 20.7 %copy-start.20 = (f32[7,7,768]{2,1,0:T(8,128)S(1)}, f32[7,7,768]{2,1,0:T(8,128)}, u32[]{:S(2)}) copy-start(f32[7,7,768]{2,1,0:T(8,128)} %param.22) | copy-start | bytes 451588
  14.1 20.7 %copy-start.22 = (f32[768]{0:T(1024)S(1)}, f32[768]{0:T(1024)}, u32[]{:S(2)}) copy-start(f32[768]{0:T(1024)} %param.23) | copy-start | bytes 9220
  14.1 20.7 %copy-start.23 = (f32[768]{0:T(1024)S(1)}, f32[768]{0:T(1024)}, u32[]{:S(2)}) copy-start(f32[768]{0:T(1024)} %param.24) | copy-start | bytes 9220
  14.1 20.7 %copy-start.24 = (f32[768]{0:T(1024)S(1)}, f32[768]{0:T(1024)}, u32[]{:S(2)}) copy-start(f32[768]{0:T(1024)} %param.29) | copy-start | bytes 9220
  14.1 20.8 %copy-start.25 = (f32[768]{0:T(1024)S(1)}, f32[768]{0:T(1024)}, u32[]{:S(2)}) copy-start(f32[768]{0:T(1024)} %param.28) | copy-start | bytes 9220
  14.1 20.8 %copy-start.26 = (f32[768]{0:T(1024)S(1)}, f32[768]{0:T(1024)}, u32[]{:S(2)}) copy-start(f32[768]{0:T(1024)} %param.30) | copy-start | bytes 9220
  14.1 64.2 %all-to-all-start = ((bf16[128,2,1664]{2,1,0:T(2,128)(2,1)}), bf16[128,2,1664]{2,1,0:T(2,128)(2,1)}, u32[]{:S(2)}, u32[]{:S(2)}) async-start(bf16[128,2,1664]{2,1,0:T(2,128)(2,1)} %reshape.48), calls=%async_computation | async-start | bytes 1703936 | tf_op jit(solution)/shard_map/all_to_all | solution.py:441
  35.0 15.1 %copy-start.17 = (bf16[8,8,8,768]{3,2,1,0:T(8,128)(2,1)S(1)}, bf16[8,8,8,768]{3,2,1,0:T(8,128)(2,1)}, u32[]{:S(2)}) copy-start(bf16[8,8,8,768]{3,2,1,0:T(8,128)(2,1)} %feats) | copy-start | bytes 2359300
  35.8 27.7 %copy-start.15 = (bf16[384,768]{1,0:T(8,128)(2,1)S(1)}, bf16[384,768]{1,0:T(8,128)(2,1)}, u32[]{:S(2)}) copy-start(bf16[384,768]{1,0:T(8,128)(2,1)} %up.1) | copy-start | bytes 1769476
  35.8 23.2 %collective-permute-start.3 = (bf16[784,384]{1,0:T(8,128)(2,1)S(1)}, bf16[784,384]{1,0:T(8,128)(2,1)S(1)}, u32[]{:S(2)}, u32[]{:S(2)}) collective-permute-start(bf16[784,384]{1,0:T(8,128)(2,1)S(1)} %slice.37), channel_id=1, source_target_pairs={{0,384},{128,0},{256,128},{384,256},{1,385},{129,1},{257,129},{385... | collective-permute-start | bytes 1806344 | tf_op jit(solution)/shard_map/ppermute | solution.py:29
  40.2 18.8 %collective-permute-start.2 = (bf16[768,384]{1,0:T(8,128)(2,1)S(1)}, bf16[768,384]{1,0:T(8,128)(2,1)S(1)}, u32[]{:S(2)}, u32[]{:S(2)}) collective-permute-start(bf16[768,384]{1,0:T(8,128)(2,1)S(1)} %slice.36), channel_id=1, source_target_pairs={{0,128},{128,256},{256,384},{384,0},{1,129},{129,257},{257,385},{3... | collective-permute-start | bytes 1769480 | tf_op jit(solution)/shard_map/ppermute | solution.py:29
  42.1 21.3 %collective-permute-start.4 = (bf16[1552,384]{1,0:T(8,128)(2,1)S(1)}, bf16[1552,384]{1,0:T(8,128)(2,1)S(1)}, u32[]{:S(2)}, u32[]{:S(2)}) collective-permute-start(bf16[1552,384]{1,0:T(8,128)(2,1)S(1)} %collective-permute-done.left), channel_id=1, source_target_pairs={{0,1},{1,0},{2,3},{3,2},{4,5},{5,4},{6,7},{7,6},{8,9},{9,8},{10,11... | collective-permute-start | bytes 3575816 | tf_op jit(solution)/shard_map/ppermute | solution.py:29
  48.2 15.2 %collective-permute-start.5 = (bf16[1552,384]{1,0:T(8,128)(2,1)S(1)}, bf16[1552,384]{1,0:T(8,128)(2,1)S(1)}, u32[]{:S(2)}, u32[]{:S(2)}) collective-permute-start(bf16[1552,384]{1,0:T(8,128)(2,1)S(1)} %collective-permute-done.1.right), channel_id=1, source_target_pairs={{0,1},{1,0},{2,3},{3,2},{4,5},{5,4},{6,7},{7,6},{8,9},{9,8},{10,11... | collective-permute-start | bytes 3575816 | tf_op jit(solution)/shard_map/ppermute | solution.py:29
  59.0 6.8 %collective-permute-start.7 = (bf16[784,384]{1,0:T(8,128)(2,1)S(1)}, bf16[784,384]{1,0:T(8,128)(2,1)S(1)}, u32[]{:S(2)}, u32[]{:S(2)}) collective-permute-start(bf16[784,384]{1,0:T(8,128)(2,1)S(1)} %collective-permute-done.3.high), channel_id=1, source_target_pairs={{0,1},{1,0},{2,3},{3,2},{4,5},{5,4},{6,7},{7,6},{8,9},{9,8},{10,11... | collective-permute-start | bytes 1806344 | tf_op jit(solution)/shard_map/ppermute | solution.py:29
  61.4 4.3 %collective-permute-start.6 = (bf16[768,384]{1,0:T(8,128)(2,1)S(1)}, bf16[768,384]{1,0:T(8,128)(2,1)S(1)}, u32[]{:S(2)}, u32[]{:S(2)}) collective-permute-start(bf16[768,384]{1,0:T(8,128)(2,1)S(1)} %collective-permute-done.2.low), channel_id=1, source_target_pairs={{0,1},{1,0},{2,3},{3,2},{4,5},{5,4},{6,7},{7,6},{8,9},{9,8},{10,11... | collective-permute-start | bytes 1769480 | tf_op jit(solution)/shard_map/ppermute | solution.py:29
  102.7 18.0 %all-to-all-start.2 = ((bf16[8,32,896]{2,1,0:T(8,128)(2,1)}), bf16[8,32,896]{2,1,0:T(8,128)(2,1)S(1)}, u32[]{:S(2)}, u32[]{:S(2)}) async-start(bf16[8,32,896]{2,1,0:T(8,128)(2,1)} %bitcast.19), calls=%async_computation.2 | async-start | bytes 917504 | tf_op jit(solution)/shard_map/all_to_all | solution.py:513
  119.8 7.1 %copy-start.31 = (s32[12]{0:T(128)S(1)}, s32[12]{0:T(128)}, u32[]{:S(2)}) copy-start(s32[12]{0:T(128)} %param.40) | copy-start | bytes 148
  122.7 10.9 %all-to-all-start.3 = ((bf16[4,64,768]{2,1,0:T(8,128)(2,1)}), bf16[4,64,768]{2,1,0:T(8,128)(2,1)S(1)}, u32[]{:S(2)}, u32[]{:S(2)}) async-start(bf16[4,64,768]{2,1,0:T(8,128)(2,1)} %broadcast_in_dim.101), calls=%async_computation.3 | async-start | bytes 786432 | tf_op jit(solution)/shard_map/all_to_all | solution.py:33
  133.6 39.4 %copy-start.19 = (bf16[192,768]{1,0:T(8,128)(2,1)S(1)}, bf16[192,768]{1,0:T(8,128)(2,1)}, u32[]{:S(2)}) copy-start(bf16[192,768]{1,0:T(8,128)(2,1)} %param.41) | copy-start | bytes 884740
  163.4 11.5 %collective-permute-start.8 = (bf16[1024,384]{1,0:T(8,128)(2,1)S(1)}, bf16[1024,384]{1,0:T(8,128)(2,1)}, u32[]{:S(2)}, u32[]{:S(2)}) collective-permute-start(bf16[1024,384]{1,0:T(8,128)(2,1)S(1)} %all_gather.3.kv), channel_id=1, source_target_pairs={{0,1},{1,0},{2,3},{3,2},{4,5},{5,4},{6,7},{7,6},{8,9},{9,8},{10,11... | collective-permute-start | bytes 2359304 | tf_op jit(solution)/shard_map/ppermute | solution.py:29
  (20 other events, 36.1 us)

commit v6 on v5

--- a/solution.py
+++ b/solution.py
@@ -129,13 +129,13 @@
     lax.fori_loop(0, tiles, one_tile, 0)
 
 
-def early_kernel(where, maps, up, bias, left, right, left_swap, right_swap, hid):
+def early_kernel(where, maps, up, block, left, right, left_swap, right_swap, hid):
     core = where[0]
     n = up.shape[0]
     tiles = hid.shape[1]
     maps_a, maps_b = lanes(maps, core, n), lanes(maps, 1 - core, n)
     pre = lax.dot_general(maps[...], up[...], NT, preferred_element_type=F32)
-    hid[0] = gelu_mean(pre + bias[...].astype(F32), tiles)
+    hid[0] = gelu_mean(pre + block[4 * n : 4 * n + 1, :].astype(F32), tiles)
     for slot, (a, b) in enumerate(((left, left_swap), (right, right_swap))):
         pre = lax.dot_general(maps_a, a[0:n, :], NT, preferred_element_type=F32)
         pre += lax.dot_general(maps_b, b[0:n, :], NT, preferred_element_type=F32)
@@ -255,7 +255,7 @@
         out_specs=jax.tree.map(lambda _: vmem, outs),
         out_shape=outs,
         scratch_shapes=scratch,
-        compiler_params=pltpu.CompilerParams(vmem_limit_bytes=24 * 2**20),
+        compiler_params=pltpu.CompilerParams(vmem_limit_bytes=16 * 2**20),
         cost_estimate=pl.CostEstimate(flops=flops, bytes_accessed=size, transcendentals=0),
     )(*operands)
 
@@ -440,7 +440,7 @@
 
     got_prior = lax.all_to_all(
         send.reshape(n_seq, capacity, send.shape[1]), SEQ_AXES, 0, 0, tiled=True
-    ).reshape(send.shape)
+    )
     left, right, low_in, high_in, feats = lax.optimization_barrier(
         (left, right, left[: 2 * share], right[2 * share :], feats)
     )
@@ -477,7 +477,7 @@
         [],
         2_000_000_000,
         6_000_000,
-        where, normed_maps, w_up, row(b_up), left, right, left_swap, right_swap,
+        where, normed_maps, w_up, block, left, right, left_swap, right_swap,
     )
     fresh = local_call(
         late_kernel,
@@ -490,16 +490,16 @@
         high_swap,
     )
     got_prior, fresh = lax.optimization_barrier((got_prior, fresh))
+    fresh_z = spread(fresh, "z", N_Z).reshape(N_Z * tiles, channels + 128)
     x_earlier = local_call(
         earlier_kernel,
         jax.ShapeDtypeStruct((q_rows, channels), F32),
         [pltpu.VMEM((q_rows, prior.shape[1]), BF16)],
         500_000_000,
         4_000_000,
-        where, got_prior, w_in, left, right, left_swap, right_swap, high, high_swap,
-    )
-
-    fresh_z = spread(fresh, "z", N_Z).reshape(N_Z * tiles, channels + 128)
+        where, got_prior.reshape(send.shape), w_in, left, right, left_swap, right_swap, high, high_swap,
+    )
+    fresh_z, x_earlier = lax.optimization_barrier((fresh_z, x_earlier))
     plane = N_Y * N_CORE
     room = N_Z * capacity
     to_plane = local_call(

time: 189 us -> 186 us (0.984)
  starting transfers between devices: 69.2 us -> 66.9 us
    all_to_all x2 -> x1, blocking collectives: 36.6 us -> 17.6 us  [spread(): lax.all_to_all(jnp.broadcast_to(block[None], (size,) + block.shape), axis...]
    all_to_all x0 -> x1, blocking collectives: none -> 17.7 us  [shards(): lax.all_to_all(to_plane.reshape(plane, room, channels + 128), ('y', 'core...]
    all_to_all x1 -> x0, starting transfers between devices: 9.16 us -> none  [shards(): lax.all_to_all(to_plane.reshape(plane, room, channels + 128), ('y', 'core...]
    all_to_all x1 -> x2, starting transfers between devices: 4.21 us -> 10.6 us  [spread(): lax.all_to_all(jnp.broadcast_to(block[None], (size,) + block.shape), axis...]
    unnamed x68 -> x64, local copies, waits for them, and re-layouts: 11 us -> 9.54 us
    all_to_all x1 -> x2, waiting for transfers between devices: 5.49 us -> 6.45 us  [spread(): lax.all_to_all(jnp.broadcast_to(block[None], (size,) + block.shape), axis...]
  transfers between devices with their start and end apart: 12 -> 12, of which waited for: 5 -> 4; matrix products, arithmetic and copies ran while one was open for 2% -> 4% of each run, Pallas kernels for 9% -> 10%
where the time goes in v6:
time: 186 us; the launch traced here: 185 us
  starting transfers between devices  66.9 us (36%)
  blocking collectives  58.1 us (31%)
  Pallas kernels  24.9 us (13%)
  local copies, waits for them, and re-layouts  17.5 us (9%)
  waiting for transfers between devices  15.7 us (8%)
    ppermute x9, starting transfers between devices, rotate(): lax.ppermute(block, axis, [(i, (i + step) % size) for i in range(size)])  35.7 us
    all_to_all x1, starting transfers between devices, shards(): lax.all_to_all(send.reshape(n_seq, capacity, send.shape[1]), SEQ_AXES, 0,...  20.6 us
    all_to_all x1, blocking collectives, shards(): lax.all_to_all(to_plane.reshape(plane, room, channels + 128), ('y', 'core...  17.7 us
    all_to_all x1, blocking collectives, spread(): lax.all_to_all(jnp.broadcast_to(block[None], (size,) + block.shape), axis...  17.6 us
    all_gather x1, blocking collectives, shards(): half_kv = lax.all_gather(z_kv, 'y', axis=0, tiled=True)  12.5 us
    pallas_call x6, Pallas kernels, vmem_call(): pl.pallas_call(body, in_specs=[vmem] * len(operands), out_specs=jax.tree....  12.3 us
    all_to_all x2, starting transfers between devices, spread(): lax.all_to_all(jnp.broadcast_to(block[None], (size,) + block.shape), axis...  10.6 us
    all_to_all x1, blocking collectives, shards(): lax.all_to_all(partial_out.reshape(n_section, width_part, ROWS), 'section...  10.3 us
  transfers between devices with their start and end apart: 12, of which 4 were waited for; matrix products, arithmetic and copies ran while one was open for 4% of the time, Pallas kernels for 10%

profile of v6, /device:TPU:1, one launch (start us, length us, event | category | flops | bytes accessed | tf_op | source)
XLA Modules:
  0.0 184.8 jit_solution(16298190821657853577)
XLA Ops:
  0.0 3.0 %shard_map.199.block = bf16[1552,384]{1,0:T(8,128)(2,1)} custom-call(s32[1]{0:T(128)} %bitcast.core_ref, bf16[384,768]{1,0:T(8,128)(2,1)} %up.1, bf16[384,768]{1,0:T(8,128)(2,1)} %w_down.3, bf16[768,384]{1,0:T(8,128)(2,1)} %w_head.3, bf16[384,768]{1,0:T(8,128)(2,1)} %w_in.5, bf16[384]{0:T(512)(128)(2,1)} %bias.1), custom_call_target="tpu_custom_call" | custom-call | bytes 2359296 | tf_op jit(solution)/shard_map/pallas_call | solution.py:77
  3.0 5.2 %collective-permute-start.1 = (bf16[1552,384]{1,0:T(8,128)(2,1)}, bf16[1552,384]{1,0:T(8,128)(2,1)S(1)}, u32[]{:S(2)}, u32[]{:S(2)}) collective-permute-start(bf16[1552,384]{1,0:T(8,128)(2,1)} %shard_map.199.block), channel_id=1, source_target_pairs={{0,384},{128,0},{256,128},{384,256},{1,385},{129,1},{257,129},{385... | collective-permute-start | bytes 3575816 | tf_op jit(solution)/shard_map/ppermute | solution.py:29
  14.1 20.6 %all-to-all-start = ((bf16[128,2,1664]{2,1,0:T(2,128)(2,1)}), bf16[128,2,1664]{2,1,0:T(2,128)(2,1)}, u32[]{:S(2)}, u32[]{:S(2)}) async-start(bf16[128,2,1664]{2,1,0:T(2,128)(2,1)} %reshape.48), calls=%async_computation | async-start | bytes 1703936 | tf_op jit(solution)/shard_map/all_to_all | solution.py:441
  35.8 4.4 %collective-permute-start.3 = (bf16[784,384]{1,0:T(8,128)(2,1)S(1)}, bf16[784,384]{1,0:T(8,128)(2,1)S(1)}, u32[]{:S(2)}, u32[]{:S(2)}) collective-permute-start(bf16[784,384]{1,0:T(8,128)(2,1)S(1)} %slice.37), channel_id=1, source_target_pairs={{0,384},{128,0},{256,128},{384,256},{1,385},{129,1},{257,129},{385... | collective-permute-start | bytes 1806344 | tf_op jit(solution)/shard_map/ppermute | solution.py:29
  40.1 1.9 %collective-permute-start.2 = (bf16[768,384]{1,0:T(8,128)(2,1)S(1)}, bf16[768,384]{1,0:T(8,128)(2,1)S(1)}, u32[]{:S(2)}, u32[]{:S(2)}) collective-permute-start(bf16[768,384]{1,0:T(8,128)(2,1)S(1)} %slice.36), channel_id=1, source_target_pairs={{0,128},{128,256},{256,384},{384,0},{1,129},{129,257},{257,385},{3... | collective-permute-start | bytes 1769480 | tf_op jit(solution)/shard_map/ppermute | solution.py:29
  42.1 6.1 %collective-permute-start.4 = (bf16[1552,384]{1,0:T(8,128)(2,1)S(1)}, bf16[1552,384]{1,0:T(8,128)(2,1)S(1)}, u32[]{:S(2)}, u32[]{:S(2)}) collective-permute-start(bf16[1552,384]{1,0:T(8,128)(2,1)S(1)} %collective-permute-done.left), channel_id=1, source_target_pairs={{0,1},{1,0},{2,3},{3,2},{4,5},{5,4},{6,7},{7,6},{8,9},{9,8},{10,11... | collective-permute-start | bytes 3575816 | tf_op jit(solution)/shard_map/ppermute | solution.py:29
  48.2 1.9 %collective-permute-start.5 = (bf16[1552,384]{1,0:T(8,128)(2,1)S(1)}, bf16[1552,384]{1,0:T(8,128)(2,1)S(1)}, u32[]{:S(2)}, u32[]{:S(2)}) collective-permute-start(bf16[1552,384]{1,0:T(8,128)(2,1)S(1)} %collective-permute-done.1.right), channel_id=1, source_target_pairs={{0,1},{1,0},{2,3},{3,2},{4,5},{5,4},{6,7},{7,6},{8,9},{9,8},{10,11... | collective-permute-start | bytes 3575816 | tf_op jit(solution)/shard_map/ppermute | solution.py:29
  50.1 9.0 %shard_map.201 = (bf16[512,768]{1,0:T(8,128)(2,1)S(1)}, f32[8,768]{1,0:T(8,128)S(1)}) custom-call(bf16[8,8,8,768]{3,2,1,0:T(8,128)(2,1)S(1)} %copy-done.15, f32[49,768]{1,0:T(8,128)S(1)} %reshape.49.dw_weight, f32[1,768]{1,0:T(1,128)S(1)} %broadcast_in_dim.88.dw_bias, f32[1,768]{1,0:T(1,128)S(1)} %broadcast_in_dim.89.gain), custom_call_target="tpu_custom_call" | custom-call | flops 30000001024 | bytes 8000000 | tf_op jit(solution)/shard_map/pallas_call | solution.py:365
  59.1 2.4 %collective-permute-start.7 = (bf16[784,384]{1,0:T(8,128)(2,1)S(1)}, bf16[784,384]{1,0:T(8,128)(2,1)S(1)}, u32[]{:S(2)}, u32[]{:S(2)}) collective-permute-start(bf16[784,384]{1,0:T(8,128)(2,1)S(1)} %collective-permute-done.3.high), channel_id=1, source_target_pairs={{0,1},{1,0},{2,3},{3,2},{4,5},{5,4},{6,7},{7,6},{8,9},{9,8},{10,11... | collective-permute-start | bytes 1806344 | tf_op jit(solution)/shard_map/ppermute | solution.py:29
  61.5 1.9 %collective-permute-start.6 = (bf16[768,384]{1,0:T(8,128)(2,1)S(1)}, bf16[768,384]{1,0:T(8,128)(2,1)S(1)}, u32[]{:S(2)}, u32[]{:S(2)}) collective-permute-start(bf16[768,384]{1,0:T(8,128)(2,1)S(1)} %collective-permute-done.2.low), channel_id=1, source_target_pairs={{0,1},{1,0},{2,3},{3,2},{4,5},{5,4},{6,7},{7,6},{8,9},{9,8},{10,11... | collective-permute-start | bytes 1769480 | tf_op jit(solution)/shard_map/ppermute | solution.py:29
  63.6 2.3 %shard_map.202.hid = f32[3,8,384]{2,1,0:T(8,128)S(1)} custom-call(s32[6]{0:T(128)S(1)} %stack.27.where, bf16[512,768]{1,0:T(8,128)(2,1)S(1)} %get-tuple-element.39.maps, bf16[384,768]{1,0:T(8,128)(2,1)S(1)} %copy-done.13, bf16[1552,384]{1,0:T(8,128)(2,1)S(1)} %copy-done.12, bf16[1552,384]{1,0:T(8,128)(2,1)S(1)} %collective-permute-done.left, ...), custom_call_target="tpu_custom_call" | custom-call | flops 2000000000 | bytes 6000000 | tf_op jit(solution)/shard_map/pallas_call | solution.py:252
  66.0 2.9 %shard_map.203 = bf16[8,896]{1,0:T(8,128)(2,1)S(1)} custom-call(s32[6]{0:T(128)S(1)} %stack.27.where, bf16[512,768]{1,0:T(8,128)(2,1)S(1)} %get-tuple-element.39.maps, f32[3,8,384]{2,1,0:T(8,128)S(1)} %shard_map.202.hid, f32[8,768]{1,0:T(8,128)S(1)} %get-tuple-element.42.feat_mean, f32[1,768]{1,0:T(1,128)S(1)} %broadcast_in_dim.90.layer_scale, ...), custom_call_target="tpu_custom_call" | custom-call | flops 2000000000 | bytes 8000000 | tf_op jit(solution)/shard_map/pallas_call | solution.py:252
  69.8 8.6 %all-to-all-done = bf16[128,2,1664]{2,1,0:T(2,128)(2,1)} async-done(((bf16[128,2,1664]{2,1,0:T(2,128)(2,1)}), bf16[128,2,1664]{2,1,0:T(2,128)(2,1)}, u32[]{:S(2)}, u32[]{:S(2)}) %all-to-all-start) | async-done | bytes 852000 | tf_op jit(solution)/shard_map/all_to_all | solution.py:441
  79.0 7.0 %all-to-all-start.1 = ((bf16[16,8,896]{2,1,0:T(8,128)(2,1)}), bf16[16,8,896]{2,1,0:T(8,128)(2,1)S(1)}, u32[]{:S(2)}, u32[]{:S(2)}) async-start(bf16[16,8,896]{2,1,0:T(8,128)(2,1)} %broadcast_in_dim.96), calls=%async_computation.1 | async-start | bytes 458752 | tf_op jit(solution)/shard_map/all_to_all | solution.py:33
  86.0 3.1 %reshape.51.got = bf16[256,1664]{1,0:T(8,128)(2,1)} reshape(bf16[128,2,1664]{2,1,0:T(2,128)(2,1)} %all-to-all-done) | data formatting | bytes 1703936 | tf_op jit(solution)/shard_map/reshape | solution.py:500
  96.3 2.4 %all-to-all-done.1 = bf16[16,8,896]{2,1,0:T(8,128)(2,1)S(1)} async-done(((bf16[16,8,896]{2,1,0:T(8,128)(2,1)}), bf16[16,8,896]{2,1,0:T(8,128)(2,1)S(1)}, u32[]{:S(2)}, u32[]{:S(2)}) %all-to-all-start.1) | async-done | bytes 229408 | tf_op jit(solution)/shard_map/all_to_all | solution.py:33
  99.7 17.7 %all_to_all.30 = bf16[8,32,896]{2,1,0:T(8,128)(2,1)S(1)} all-to-all(bf16[8,32,896]{2,1,0:T(8,128)(2,1)S(1)} %bitcast.19), channel_id=1, replica_groups=mesh['section'=4,'z'=16,'y'=4,'core'=2] {'y','core'}, dimensions={0} | all-to-all | bytes 917504 | tf_op jit(solution)/shard_map/all_to_all | solution.py:513
  118.5 3.6 %all-to-all-start.3 = ((bf16[4,64,768]{2,1,0:T(8,128)(2,1)}), bf16[4,64,768]{2,1,0:T(8,128)(2,1)S(1)}, u32[]{:S(2)}, u32[]{:S(2)}) async-start(bf16[4,64,768]{2,1,0:T(8,128)(2,1)} %broadcast_in_dim.97), calls=%async_computation.3 | async-start | bytes 786432 | tf_op jit(solution)/shard_map/all_to_all | solution.py:33
  124.5 4.0 %all-to-all-done.3 = bf16[4,64,768]{2,1,0:T(8,128)(2,1)S(1)} async-done(((bf16[4,64,768]{2,1,0:T(8,128)(2,1)}), bf16[4,64,768]{2,1,0:T(8,128)(2,1)S(1)}, u32[]{:S(2)}, u32[]{:S(2)}) %all-to-all-start.3) | async-done | bytes 393248 | tf_op jit(solution)/shard_map/all_to_all | solution.py:33
  129.5 17.6 %all_to_all.31 = bf16[16,16,384]{2,1,0:T(8,128)(2,1)S(1)} all-to-all(bf16[16,16,384]{2,1,0:T(8,128)(2,1)S(1)} %broadcast_in_dim.100), channel_id=1, replica_groups=mesh['section'=4,'z'=16,'y'=4,'core'=2] {'z'}, dimensions={0} | all-to-all | bytes 393216 | tf_op jit(solution)/shard_map/all_to_all | solution.py:33
  147.0 12.5 %all_gather.3.kv = bf16[1024,384]{1,0:T(8,128)(2,1)} all-gather(bf16[256,384]{1,0:T(8,128)(2,1)S(1)} %bitcast.26), channel_id=1, replica_groups=mesh['section'=4,'z'=16,'y'=4,'core'=2] {'y'}, dimensions={0}, use_global_device_ids=true | all-gather | bytes 983040 | tf_op jit(solution)/shard_map/all_gather | solution.py:544
  159.5 9.9 %collective-permute-start.8 = (bf16[1024,384]{1,0:T(8,128)(2,1)}, bf16[1024,384]{1,0:T(8,128)(2,1)S(1)}, u32[]{:S(2)}, u32[]{:S(2)}) collective-permute-start(bf16[1024,384]{1,0:T(8,128)(2,1)} %all_gather.3.kv), channel_id=1, source_target_pairs={{0,1},{1,0},{2,3},{3,2},{4,5},{5,4},{6,7},{7,6},{8,9},{9,8},{10,11... | collective-permute-start | bytes 2359304 | tf_op jit(solution)/shard_map/ppermute | solution.py:29
  170.6 2.0 %shard_map.208 = (f32[256,192]{1,0:T(8,128)S(1)}, f32[256,192]{1,0:T(8,128)S(1)}, f32[16,192]{1,0:T(8,128)S(1)}, f32[16,192]{1,0:T(8,128)S(1)}, f32[192,256]{1,0:T(8,128)S(1)}) custom-call(s32[6]{0:T(128)S(1)} %stack.27.where, bf16[256,192]{1,0:T(8,128)(2,1)S(1)} %get-tuple-element.49.q, bf16[256,192]{1,0:T(8,128)(2,1)S(1)} %get-tuple-element.50.k, ...), custom_call_target="tpu_custom_call" | custom-call | flops 2000000000 | bytes 2000000 | tf_op jit(solution)/shard_map/pallas_call | solution.py:252
  173.7 10.3 %all_to_all.32.parts = bf16[4,192,256]{2,1,0:T(8,128)(2,1)S(1)} all-to-all(bf16[4,192,256]{2,1,0:T(8,128)(2,1)S(1)} %bitcast.22), channel_id=1, replica_groups=mesh['section'=4,'z'=16,'y'=4,'core'=2] {'section'}, dimensions={0} | all-to-all | bytes 786432 | tf_op jit(solution)/shard_map/all_to_all | solution.py:566
  (114 shorter events, 23.1 us)
Async XLA Ops:
  0.0 10.2 %copy-start.26 = (s32[160]{0:T(256)S(1)}, s32[160]{0:T(256)}, u32[]{:S(2)}) copy-start(s32[160]{0:T(256)} %param.34) | copy-start | bytes 1924
  3.0 32.0 %collective-permute-start.1 = (bf16[1552,384]{1,0:T(8,128)(2,1)}, bf16[1552,384]{1,0:T(8,128)(2,1)S(1)}, u32[]{:S(2)}, u32[]{:S(2)}) collective-permute-start(bf16[1552,384]{1,0:T(8,128)(2,1)} %shard_map.199.block), channel_id=1, source_target_pairs={{0,384},{128,0},{256,128},{384,256},{1,385},{129,1},{257,129},{385... | collective-permute-start | bytes 3575816 | tf_op jit(solution)/shard_map/ppermute | solution.py:29
  8.2 27.5 %collective-permute-start = (bf16[1552,384]{1,0:T(8,128)(2,1)}, bf16[1552,384]{1,0:T(8,128)(2,1)S(1)}, u32[]{:S(2)}, u32[]{:S(2)}) collective-permute-start(bf16[1552,384]{1,0:T(8,128)(2,1)} %shard_map.199.block), channel_id=1, source_target_pairs={{0,128},{128,256},{256,384},{384,0},{1,129},{129,257},{257,385},{3... | collective-permute-start | bytes 3575816 | tf_op jit(solution)/shard_map/ppermute | solution.py:29
  14.0 20.6 %copy-start.19 = (f32[7,7,768]{2,1,0:T(8,128)S(1)}, f32[7,7,768]{2,1,0:T(8,128)}, u32[]{:S(2)}) copy-start(f32[7,7,768]{2,1,0:T(8,128)} %param.22) | copy-start | bytes 451588
  14.0 20.7 %copy-start.20 = (f32[768]{0:T(1024)S(1)}, f32[768]{0:T(1024)}, u32[]{:S(2)}) copy-start(f32[768]{0:T(1024)} %param.23) | copy-start | bytes 9220
  14.0 20.7 %copy-start.21 = (f32[768]{0:T(1024)S(1)}, f32[768]{0:T(1024)}, u32[]{:S(2)}) copy-start(f32[768]{0:T(1024)} %param.24) | copy-start | bytes 9220
  14.0 20.7 %copy-start.22 = (f32[768]{0:T(1024)S(1)}, f32[768]{0:T(1024)}, u32[]{:S(2)}) copy-start(f32[768]{0:T(1024)} %param.29) | copy-start | bytes 9220
  14.1 20.7 %copy-start.23 = (f32[768]{0:T(1024)S(1)}, f32[768]{0:T(1024)}, u32[]{:S(2)}) copy-start(f32[768]{0:T(1024)} %param.28) | copy-start | bytes 9220
  14.1 20.7 %copy-start.24 = (f32[768]{0:T(1024)S(1)}, f32[768]{0:T(1024)}, u32[]{:S(2)}) copy-start(f32[768]{0:T(1024)} %param.30) | copy-start | bytes 9220
  14.1 64.2 %all-to-all-start = ((bf16[128,2,1664]{2,1,0:T(2,128)(2,1)}), bf16[128,2,1664]{2,1,0:T(2,128)(2,1)}, u32[]{:S(2)}, u32[]{:S(2)}) async-start(bf16[128,2,1664]{2,1,0:T(2,128)(2,1)} %reshape.48), calls=%async_computation | async-start | bytes 1703936 | tf_op jit(solution)/shard_map/all_to_all | solution.py:441
  35.0 15.2 %copy-start.15 = (bf16[8,8,8,768]{3,2,1,0:T(8,128)(2,1)S(1)}, bf16[8,8,8,768]{3,2,1,0:T(8,128)(2,1)}, u32[]{:S(2)}) copy-start(bf16[8,8,8,768]{3,2,1,0:T(8,128)(2,1)} %feats) | copy-start | bytes 2359300
  35.8 27.8 %copy-start.12 = (bf16[1552,384]{1,0:T(8,128)(2,1)S(1)}, bf16[1552,384]{1,0:T(8,128)(2,1)}, u32[]{:S(2)}) copy-start(bf16[1552,384]{1,0:T(8,128)(2,1)} %shard_map.199.block) | copy-start | bytes 3575812
  35.8 27.8 %copy-start.13 = (bf16[384,768]{1,0:T(8,128)(2,1)S(1)}, bf16[384,768]{1,0:T(8,128)(2,1)}, u32[]{:S(2)}) copy-start(bf16[384,768]{1,0:T(8,128)(2,1)} %up.1) | copy-start | bytes 1769476
  35.8 23.3 %collective-permute-start.3 = (bf16[784,384]{1,0:T(8,128)(2,1)S(1)}, bf16[784,384]{1,0:T(8,128)(2,1)S(1)}, u32[]{:S(2)}, u32[]{:S(2)}) collective-permute-start(bf16[784,384]{1,0:T(8,128)(2,1)S(1)} %slice.37), channel_id=1, source_target_pairs={{0,384},{128,0},{256,128},{384,256},{1,385},{129,1},{257,129},{385... | collective-permute-start | bytes 1806344 | tf_op jit(solution)/shard_map/ppermute | solution.py:29
  40.1 19.0 %collective-permute-start.2 = (bf16[768,384]{1,0:T(8,128)(2,1)S(1)}, bf16[768,384]{1,0:T(8,128)(2,1)S(1)}, u32[]{:S(2)}, u32[]{:S(2)}) collective-permute-start(bf16[768,384]{1,0:T(8,128)(2,1)S(1)} %slice.36), channel_id=1, source_target_pairs={{0,128},{128,256},{256,384},{384,0},{1,129},{129,257},{257,385},{3... | collective-permute-start | bytes 1769480 | tf_op jit(solution)/shard_map/ppermute | solution.py:29
  42.1 21.5 %collective-permute-start.4 = (bf16[1552,384]{1,0:T(8,128)(2,1)S(1)}, bf16[1552,384]{1,0:T(8,128)(2,1)S(1)}, u32[]{:S(2)}, u32[]{:S(2)}) collective-permute-start(bf16[1552,384]{1,0:T(8,128)(2,1)S(1)} %collective-permute-done.left), channel_id=1, source_target_pairs={{0,1},{1,0},{2,3},{3,2},{4,5},{5,4},{6,7},{7,6},{8,9},{9,8},{10,11... | collective-permute-start | bytes 3575816 | tf_op jit(solution)/shard_map/ppermute | solution.py:29
  48.2 15.4 %collective-permute-start.5 = (bf16[1552,384]{1,0:T(8,128)(2,1)S(1)}, bf16[1552,384]{1,0:T(8,128)(2,1)S(1)}, u32[]{:S(2)}, u32[]{:S(2)}) collective-permute-start(bf16[1552,384]{1,0:T(8,128)(2,1)S(1)} %collective-permute-done.1.right), channel_id=1, source_target_pairs={{0,1},{1,0},{2,3},{3,2},{4,5},{5,4},{6,7},{7,6},{8,9},{9,8},{10,11... | collective-permute-start | bytes 3575816 | tf_op jit(solution)/shard_map/ppermute | solution.py:29
  59.1 6.8 %collective-permute-start.7 = (bf16[784,384]{1,0:T(8,128)(2,1)S(1)}, bf16[784,384]{1,0:T(8,128)(2,1)S(1)}, u32[]{:S(2)}, u32[]{:S(2)}) collective-permute-start(bf16[784,384]{1,0:T(8,128)(2,1)S(1)} %collective-permute-done.3.high), channel_id=1, source_target_pairs={{0,1},{1,0},{2,3},{3,2},{4,5},{5,4},{6,7},{7,6},{8,9},{9,8},{10,11... | collective-permute-start | bytes 1806344 | tf_op jit(solution)/shard_map/ppermute | solution.py:29
  61.5 4.4 %collective-permute-start.6 = (bf16[768,384]{1,0:T(8,128)(2,1)S(1)}, bf16[768,384]{1,0:T(8,128)(2,1)S(1)}, u32[]{:S(2)}, u32[]{:S(2)}) collective-permute-start(bf16[768,384]{1,0:T(8,128)(2,1)S(1)} %collective-permute-done.2.low), channel_id=1, source_target_pairs={{0,1},{1,0},{2,3},{3,2},{4,5},{5,4},{6,7},{7,6},{8,9},{9,8},{10,11... | collective-permute-start | bytes 1769480 | tf_op jit(solution)/shard_map/ppermute | solution.py:29
  79.0 19.7 %all-to-all-start.1 = ((bf16[16,8,896]{2,1,0:T(8,128)(2,1)}), bf16[16,8,896]{2,1,0:T(8,128)(2,1)S(1)}, u32[]{:S(2)}, u32[]{:S(2)}) async-start(bf16[16,8,896]{2,1,0:T(8,128)(2,1)} %broadcast_in_dim.96), calls=%async_computation.1 | async-start | bytes 458752 | tf_op jit(solution)/shard_map/all_to_all | solution.py:33
  118.5 10.0 %all-to-all-start.3 = ((bf16[4,64,768]{2,1,0:T(8,128)(2,1)}), bf16[4,64,768]{2,1,0:T(8,128)(2,1)S(1)}, u32[]{:S(2)}, u32[]{:S(2)}) async-start(bf16[4,64,768]{2,1,0:T(8,128)(2,1)} %broadcast_in_dim.97), calls=%async_computation.3 | async-start | bytes 786432 | tf_op jit(solution)/shard_map/all_to_all | solution.py:33
  128.5 41.0 %copy-start.18 = (bf16[192,768]{1,0:T(8,128)(2,1)S(1)}, bf16[192,768]{1,0:T(8,128)(2,1)}, u32[]{:S(2)}) copy-start(bf16[192,768]{1,0:T(8,128)(2,1)} %param.41) | copy-start | bytes 884740
  129.4 40.3 %copy-start.16 = (bf16[256,192]{1,0:T(8,128)(2,1)}, bf16[256,192]{1,0:T(8,128)(2,1)S(1)}, u32[]{:S(2)}) copy-start(bf16[256,192]{1,0:T(8,128)(2,1)S(1)} %get-tuple-element.51.v) | copy-start | bytes 294916
  159.5 13.1 %collective-permute-start.8 = (bf16[1024,384]{1,0:T(8,128)(2,1)}, bf16[1024,384]{1,0:T(8,128)(2,1)S(1)}, u32[]{:S(2)}, u32[]{:S(2)}) collective-permute-start(bf16[1024,384]{1,0:T(8,128)(2,1)} %all_gather.3.kv), channel_id=1, source_target_pairs={{0,1},{1,0},{2,3},{3,2},{4,5},{5,4},{6,7},{7,6},{8,9},{9,8},{10,11... | collective-permute-start | bytes 2359304 | tf_op jit(solution)/shard_map/ppermute | solution.py:29
  (18 other events, 34.2 us)

commit v7 on v6

--- a/solution.py
+++ b/solution.py
@@ -12,8 +12,8 @@
 RB = 16
 ROWS = 256
 N_SECTION = 4
-N_Z, N_Y, N_CORE = 16, 4, 2
-SEQ_AXES = ("z", "y", "core")
+N_ZH, N_ZL, N_Y, N_CORE = 4, 4, 4, 2
+SEQ_AXES = ("zh", "zl", "y", "core")
 F32 = jnp.float32
 BF16 = jnp.bfloat16
 
@@ -29,10 +29,8 @@
     return lax.ppermute(block, axis, [(i, (i + step) % size) for i in range(size)])
 
 
-def spread(block, axis, size):
-    return lax.all_to_all(
-        jnp.broadcast_to(block[None], (size,) + block.shape), axis, 0, 0, tiled=True
-    )
+def exchange(copies, axis):
+    return lax.all_to_all(copies, axis, 0, 0, tiled=True)
 
 
 NT = (((1,), (1,)), ((), ()))
@@ -91,7 +89,8 @@
 
 
 def conv_kernel(feats, dw_weight, dw_bias, gain, out, mean, conv):
-    tiles, side, _, channels = feats.shape
+    tiles, channels = mean.shape
+    side = math.isqrt(feats.shape[0] // tiles)
     taps = math.isqrt(dw_weight.shape[0])
     reach = (taps - 1) // 2
     column = lax.broadcasted_iota(jnp.int32, (side, side, 128), 1)
@@ -99,9 +98,11 @@
     mean[...] = jnp.zeros_like(mean)
 
     def one_tile(tile, carry):
+        start = pl.multiple_of(tile * side * side, side * side)
         for chunk in range(channels // 128):
             cols = pl.ds(chunk * 128, 128)
-            source = feats[tile, :, :, cols].astype(F32)
+            source = feats[pl.ds(start, side * side), cols].astype(F32)
+            source = source.reshape(side, side, 128)
             total = jnp.sum(jnp.sum(source, axis=0), axis=0, keepdims=True)
             total = jnp.broadcast_to(total * (1.0 / (side * side)), (tiles, 128))
             mean[:, cols] = jnp.where(tile_row == tile, total, mean[:, cols])
@@ -122,11 +123,14 @@
                             sums[i] = sums[i] + moved[i + a - reach] * tap
             for i in range(side):
                 conv[i * side : (i + 1) * side, cols] = sums[i]
-        start = pl.multiple_of(tile * side * side, side * side)
         out[pl.ds(start, side * side), :] = layer_norm(conv[...], gain[...]).astype(BF16)
         return carry
 
     lax.fori_loop(0, tiles, one_tile, 0)
+
+
+def first_row(ref, start):
+    return ref[start : start + 16, :].astype(F32)[0:1, :]
 
 
 def early_kernel(where, maps, up, block, left, right, left_swap, right_swap, hid):
@@ -135,11 +139,11 @@
     tiles = hid.shape[1]
     maps_a, maps_b = lanes(maps, core, n), lanes(maps, 1 - core, n)
     pre = lax.dot_general(maps[...], up[...], NT, preferred_element_type=F32)
-    hid[0] = gelu_mean(pre + block[4 * n : 4 * n + 1, :].astype(F32), tiles)
+    hid[0] = gelu_mean(pre + first_row(block, 4 * n), tiles)
     for slot, (a, b) in enumerate(((left, left_swap), (right, right_swap))):
         pre = lax.dot_general(maps_a, a[0:n, :], NT, preferred_element_type=F32)
         pre += lax.dot_general(maps_b, b[0:n, :], NT, preferred_element_type=F32)
-        hid[slot + 1] = gelu_mean(pre + a[4 * n : 4 * n + 1, :].astype(F32), tiles)
+        hid[slot + 1] = gelu_mean(pre + first_row(a, 4 * n), tiles)
 
 
 def late_kernel(
@@ -153,7 +157,7 @@
     pre += lax.dot_general(
         lanes(maps, 1 - core, n), low_swap[0:n, :], NT, preferred_element_type=F32
     )
-    hid_far = gelu_mean(pre + high[2 * n : 2 * n + 1, :].astype(F32), tiles)
+    hid_far = gelu_mean(pre + first_row(high, 2 * n), tiles)
 
     def exact(block):
         upper = block.astype(BF16)
@@ -234,7 +238,7 @@
     before = jnp.where((dest == dest_row) & (index_a < index_b), 1.0, 0.0)
     rank = jnp.sum(before, axis=0, keepdims=True).astype(jnp.int32)
     shard = dest_row.astype(jnp.int32)
-    plane = N_Y * N_CORE
+    plane = N_ZL * N_Y * N_CORE
     room = out.shape[0] // plane
     inside = shard - where[5] * plane
     bucket = jnp.where((inside >= 0) & (inside < plane), inside * room + rank, -1)
@@ -244,7 +248,9 @@
 
 
 def arrive_kernel(got, earlier, out):
-    out[...] = (place_rows(got, out.shape[0]) + earlier[...]).astype(BF16)
+    rows = (place_rows(got, out.shape[1]) + earlier[...]).astype(BF16)
+    for copy in range(out.shape[0]):
+        out[copy] = rows
 
 
 def local_call(body, outs, scratch, flops, size, *operands):
@@ -293,7 +299,9 @@
     v_rows = dot(normed, w_v[...]).astype(BF16)
     q[...], k[...], v[...] = q_rows, k_rows, v_rows
     far_q[...] = far_rows(q_rows)
-    far_kv[...] = jnp.concatenate([far_rows(k_rows), far_rows(v_rows)], axis=1).astype(BF16)
+    pairs = jnp.concatenate([far_rows(k_rows), far_rows(v_rows)], axis=1).astype(BF16)
+    for copy in range(far_kv.shape[0]):
+        far_kv[copy] = pairs
 
 
 def by_head(block):
@@ -397,7 +405,7 @@
     w_out,
 ):
     n_section = N_SECTION
-    n_seq = N_Z * N_Y * N_CORE
+    n_seq = N_ZH * N_ZL * N_Y * N_CORE
     section_idx = lax.axis_index("section")
     core = lax.axis_index("core")
     tiles = feats.shape[0]
@@ -407,7 +415,7 @@
 
     row = lambda vec: vec[None, :]
     others = [(section_idx + step) % N_SECTION for step in (3, 1, 2)]
-    where = jnp.stack([core, section_idx] + others + [lax.axis_index("z")]).astype(jnp.int32)
+    where = jnp.stack([core, section_idx] + others + [lax.axis_index("zh")]).astype(jnp.int32)
 
     block = pack(core, w_up, w_down, w_head, w_in, b_up)
     block, prior = lax.optimization_barrier((block, prior))
@@ -458,7 +466,7 @@
         30_000_000_000,
         8_000_000,
         0,
-        feats, dw_weight.reshape(-1, channels), row(dw_bias), row(ln1_gain),
+        feats.reshape(-1, channels), dw_weight.reshape(-1, channels), row(dw_bias), row(ln1_gain),
         scratch=[pltpu.VMEM((pixels, channels), F32)],
     )
     low, high, normed_maps, feat_mean = lax.optimization_barrier(
@@ -489,19 +497,9 @@
         code_fresh, w_down, w_head, w_in, left, right, left_swap, right_swap, low, high, low_swap,
         high_swap,
     )
-    got_prior, fresh = lax.optimization_barrier((got_prior, fresh))
-    fresh_z = spread(fresh, "z", N_Z).reshape(N_Z * tiles, channels + 128)
-    x_earlier = local_call(
-        earlier_kernel,
-        jax.ShapeDtypeStruct((q_rows, channels), F32),
-        [pltpu.VMEM((q_rows, prior.shape[1]), BF16)],
-        500_000_000,
-        4_000_000,
-        where, got_prior.reshape(send.shape), w_in, left, right, left_swap, right_swap, high, high_swap,
-    )
-    fresh_z, x_earlier = lax.optimization_barrier((fresh_z, x_earlier))
-    plane = N_Y * N_CORE
-    room = N_Z * capacity
+    fresh_z = lax.all_gather(fresh, "zh", axis=0, tiled=True)
+    plane = N_ZL * N_Y * N_CORE
+    room = N_ZH * capacity
     to_plane = local_call(
         scatter_kernel,
         jax.ShapeDtypeStruct((plane * room, channels + 128), BF16),
@@ -510,18 +508,28 @@
         1_000_000,
         where, fresh_z,
     )
+    to_plane, got_prior = lax.optimization_barrier((to_plane, got_prior))
     got = lax.all_to_all(
-        to_plane.reshape(plane, room, channels + 128), ("y", "core"), 0, 0, tiled=True
+        to_plane.reshape(plane, room, channels + 128), SEQ_AXES[1:], 0, 0, tiled=True
     ).reshape(plane * room, channels + 128)
-    x_local = vmem_call(
+    x_earlier = local_call(
+        earlier_kernel,
+        jax.ShapeDtypeStruct((q_rows, channels), F32),
+        [pltpu.VMEM((q_rows, prior.shape[1]), BF16)],
+        500_000_000,
+        4_000_000,
+        where, got_prior.reshape(send.shape), w_in, left, right, left_swap, right_swap, high,
+        high_swap,
+    )
+    x_copies = vmem_call(
         arrive_kernel,
-        jax.ShapeDtypeStruct((q_rows, channels), BF16),
+        jax.ShapeDtypeStruct((n_section, q_rows, channels), BF16),
         30_000_000,
         1_000_000,
         0,
         got, x_earlier,
     )
-    x_rows = spread(x_local, "section", n_section).reshape(ROWS, channels)
+    x_rows = exchange(x_copies, "section").reshape(ROWS, channels)
 
     heads_here = w_qkv.shape[1] // (3 * HS)
     width = heads_here * HS
@@ -533,15 +541,16 @@
     q, k, v, far_q, far_kv = vmem_call(
         project_kernel,
         (small(ROWS, BF16),) * 3
-        + (small(stride_rows, F32), jax.ShapeDtypeStruct((stride_rows, 2 * width), BF16)),
+        + (small(stride_rows, F32), jax.ShapeDtypeStruct((N_ZH, stride_rows, 2 * width), BF16)),
         300_000_000,
         2_000_000,
         0,
         x_rows, row(ln_gain), w_q, w_k, w_v, row(jnp.tile(qn_gain, heads_here)),
         row(jnp.tile(kn_gain, heads_here)), off_lane,
     )
-    z_kv = spread(far_kv, "z", N_Z).reshape(N_Z * stride_rows, 2 * width)
-    half_kv = lax.all_gather(z_kv, "y", axis=0, tiled=True)
+    z_kv = exchange(far_kv, "zh").reshape(N_ZH * stride_rows, 2 * width)
+    z_copies = jnp.broadcast_to(z_kv[None], (N_ZL * N_Y,) + z_kv.shape)
+    half_kv = exchange(z_copies, ("zl", "y")).reshape(n_seq // N_CORE * stride_rows, 2 * width)
     other_kv = rotate(half_kv, "core", N_CORE, 1)
     width_part = channels // n_section
     den, num, far_den, far_num, residual = local_call(
@@ -579,7 +588,7 @@
 
 def solution(mesh):
     fine = Mesh(
-        mesh.devices.reshape(N_SECTION, N_Z, N_Y, N_CORE), ("section",) + SEQ_AXES
+        mesh.devices.reshape(N_SECTION, N_ZH, N_ZL, N_Y, N_CORE), ("section",) + SEQ_AXES
     )
     both = ("section",) + SEQ_AXES
     placed = (

time: 186 us -> 195 us (1.048)
  blocking collectives: 58.1 us -> 73.9 us
  waiting for transfers between devices: 15.7 us -> 10.9 us
  starting transfers between devices: 66.9 us -> 63.9 us
    all_gather x1, blocking collectives: 12.5 us -> 22.9 us  [shards(): fresh_z = lax.all_gather(fresh, 'zh', axis=0, tiled=True)]
    all_to_all x1, waiting for transfers between devices: 8.57 us -> 0.01 us  [shards(): lax.all_to_all(send.reshape(n_seq, capacity, send.shape[1]), SEQ_AXES, 0,...]
    all_to_all x2, blocking collectives: 35.3 us -> 40.8 us  [exchange(): return lax.all_to_all(copies, axis, 0, 0, tiled=True)]
    ppermute x9, starting transfers between devices: 35.7 us -> 30.3 us  [rotate(): lax.ppermute(block, axis, [(i, (i + step) % size) for i in range(size)])]
    all_to_all x2, waiting for transfers between devices: 6.45 us -> 9.93 us  [the longest x1 5.83 us: exchange(): return lax.all_to_all(copies, axis, 0, 0, tiled=True)]
    all_to_all x2, starting transfers between devices: 10.6 us -> 13 us  [the longest x1 9.39 us: shards(): lax.all_to_all(to_plane.reshape(plane, room, channels + 128), SEQ_AXES[1:...]
    unnamed x64 -> x68, local copies, waits for them, and re-layouts: 9.54 us -> 11.4 us
where the time goes in v7:
time: 195 us; the launch traced here: 194 us
  blocking collectives  73.9 us (38%)
  starting transfers between devices  63.9 us (33%)
  Pallas kernels  25.9 us (13%)
  local copies, waits for them, and re-layouts  17.9 us (9%)
  waiting for transfers between devices  10.9 us (6%)
    all_to_all x2, blocking collectives, exchange(): return lax.all_to_all(copies, axis, 0, 0, tiled=True)  40.8 us
    ppermute x9, starting transfers between devices, rotate(): lax.ppermute(block, axis, [(i, (i + step) % size) for i in range(size)])  30.3 us
    all_gather x1, blocking collectives, shards(): fresh_z = lax.all_gather(fresh, 'zh', axis=0, tiled=True)  22.9 us
    all_to_all x1, starting transfers between devices, shards(): lax.all_to_all(send.reshape(n_seq, capacity, send.shape[1]), SEQ_AXES, 0,...  20.6 us
    pallas_call x6, Pallas kernels, vmem_call(): pl.pallas_call(body, in_specs=[vmem] * len(operands), out_specs=jax.tree....  13.1 us
    unnamed x68, local copies, waits for them, and re-layouts  11.4 us
    all_to_all x1, blocking collectives, shards(): lax.all_to_all(partial_out.reshape(n_section, width_part, ROWS), 'section...  10.2 us
    pallas_call x5, Pallas kernels, local_call(): pl.pallas_call(body, in_specs=[pl.BlockSpec(memory_space=pltpu.SMEM)] + [...  9.72 us
  transfers between devices with their start and end apart: 12, of which 4 were waited for; matrix products, arithmetic and copies ran while one was open for 4% of the time, Pallas kernels for 10%

profile of v7, /device:TPU:1, one launch (start us, length us, event | category | flops | bytes accessed | tf_op | source)
XLA Modules:
  0.0 194.1 jit_solution(13334089821712974169)
XLA Ops:
  0.0 3.0 %shard_map.199.block = bf16[1552,384]{1,0:T(8,128)(2,1)} custom-call(s32[1]{0:T(128)} %bitcast.core_ref, bf16[384,768]{1,0:T(8,128)(2,1)} %up.1, bf16[384,768]{1,0:T(8,128)(2,1)} %w_down.3, bf16[768,384]{1,0:T(8,128)(2,1)} %w_head.3, bf16[384,768]{1,0:T(8,128)(2,1)} %w_in.5, bf16[384]{0:T(512)(128)(2,1)} %bias.1), custom_call_target="tpu_custom_call" | custom-call | bytes 2359296 | tf_op jit(solution)/shard_map/pallas_call | solution.py:75
  3.0 5.2 %collective-permute-start.1 = (bf16[1552,384]{1,0:T(8,128)(2,1)}, bf16[1552,384]{1,0:T(8,128)(2,1)S(1)}, u32[]{:S(2)}, u32[]{:S(2)}) collective-permute-start(bf16[1552,384]{1,0:T(8,128)(2,1)} %shard_map.199.block), channel_id=1, source_target_pairs={{0,384},{128,0},{256,128},{384,256},{1,385},{129,1},{257,129},{385... | collective-permute-start | bytes 3575816 | tf_op jit(solution)/shard_map/ppermute | solution.py:29
  8.3 1.9 collective-permute-start
  14.1 20.6 %all-to-all-start = ((bf16[128,2,1664]{2,1,0:T(2,128)(2,1)}), bf16[128,2,1664]{2,1,0:T(2,128)(2,1)}, u32[]{:S(2)}, u32[]{:S(2)}) async-start(bf16[128,2,1664]{2,1,0:T(2,128)(2,1)} %reshape.48), calls=%async_computation | async-start | bytes 1703936 | tf_op jit(solution)/shard_map/all_to_all | solution.py:449
  35.8 4.3 %collective-permute-start.3 = (bf16[784,384]{1,0:T(8,128)(2,1)S(1)}, bf16[784,384]{1,0:T(8,128)(2,1)S(1)}, u32[]{:S(2)}, u32[]{:S(2)}) collective-permute-start(bf16[784,384]{1,0:T(8,128)(2,1)S(1)} %slice.37), channel_id=1, source_target_pairs={{0,384},{128,0},{256,128},{384,256},{1,385},{129,1},{257,129},{385... | collective-permute-start | bytes 1806344 | tf_op jit(solution)/shard_map/ppermute | solution.py:29
  40.1 1.9 collective-permute-start.2
  42.1 6.0 %collective-permute-start.4 = (bf16[1552,384]{1,0:T(8,128)(2,1)S(1)}, bf16[1552,384]{1,0:T(8,128)(2,1)S(1)}, u32[]{:S(2)}, u32[]{:S(2)}) collective-permute-start(bf16[1552,384]{1,0:T(8,128)(2,1)S(1)} %collective-permute-done.left), channel_id=1, source_target_pairs={{0,1},{1,0},{2,3},{3,2},{4,5},{5,4},{6,7},{7,6},{8,9},{9,8},{10,11... | collective-permute-start | bytes 3575816 | tf_op jit(solution)/shard_map/ppermute | solution.py:29
  48.1 1.9 collective-permute-start.5
  50.0 9.0 %shard_map.200 = (bf16[512,768]{1,0:T(8,128)(2,1)S(1)}, f32[8,768]{1,0:T(8,128)S(1)}) custom-call(bf16[512,768]{1,0:T(8,128)(2,1)S(1)} %bitcast.27, f32[49,768]{1,0:T(8,128)S(1)} %reshape.47.dw_weight, f32[1,768]{1,0:T(1,128)S(1)} %broadcast_in_dim.74.dw_bias, f32[1,768]{1,0:T(1,128)S(1)} %broadcast_in_dim.75.gain), custom_call_target="tpu_custom_call" | custom-call | flops 30000001024 | bytes 8000000 | tf_op jit(solution)/shard_map/pallas_call | solution.py:373
  59.1 2.4 %collective-permute-start.7 = (bf16[784,384]{1,0:T(8,128)(2,1)S(1)}, bf16[784,384]{1,0:T(8,128)(2,1)S(1)}, u32[]{:S(2)}, u32[]{:S(2)}) collective-permute-start(bf16[784,384]{1,0:T(8,128)(2,1)S(1)} %collective-permute-done.3.high), channel_id=1, source_target_pairs={{0,1},{1,0},{2,3},{3,2},{4,5},{5,4},{6,7},{7,6},{8,9},{9,8},{10,11... | collective-permute-start | bytes 1806344 | tf_op jit(solution)/shard_map/ppermute | solution.py:29
  61.5 1.9 collective-permute-start.6
  63.5 2.3 %shard_map.201.hid = f32[3,8,384]{2,1,0:T(8,128)S(1)} custom-call(s32[6]{0:T(128)S(1)} %stack.27.where, bf16[512,768]{1,0:T(8,128)(2,1)S(1)} %get-tuple-element.36.maps, bf16[384,768]{1,0:T(8,128)(2,1)S(1)} %copy-done.17, bf16[1552,384]{1,0:T(8,128)(2,1)S(1)} %copy-done.12, bf16[1552,384]{1,0:T(8,128)(2,1)S(1)} %collective-permute-done.left, ...), custom_call_target="tpu_custom_call" | custom-call | flops 2000000000 | bytes 6000000 | tf_op jit(solution)/shard_map/pallas_call | solution.py:258
  65.9 2.9 %shard_map.202 = bf16[8,896]{1,0:T(8,128)(2,1)S(1)} custom-call(s32[6]{0:T(128)S(1)} %stack.27.where, bf16[512,768]{1,0:T(8,128)(2,1)S(1)} %get-tuple-element.36.maps, f32[3,8,384]{2,1,0:T(8,128)S(1)} %shard_map.201.hid, f32[8,768]{1,0:T(8,128)S(1)} %get-tuple-element.39.feat_mean, f32[1,768]{1,0:T(1,128)S(1)} %broadcast_in_dim.76.layer_scale, ...), custom_call_target="tpu_custom_call" | custom-call | flops 2000000000 | bytes 8000000 | tf_op jit(solution)/shard_map/pallas_call | solution.py:258
  68.8 22.9 %all_gather.3.rows = bf16[32,896]{1,0:T(8,128)(2,1)S(1)} all-gather(bf16[8,896]{1,0:T(8,128)(2,1)S(1)} %shard_map.202), channel_id=1, replica_groups=mesh['section'=4,'zh'=4,'zl'=4,'y'=4,'core'=2] {'zh'}, dimensions={0}, use_global_device_ids=true | all-gather | bytes 71680 | tf_op jit(solution)/shard_map/all_gather | solution.py:500
  91.7 1.7 shard_map.203
  93.4 9.4 %all-to-all-start.1 = ((bf16[32,8,896]{2,1,0:T(8,128)(2,1)}), bf16[32,8,896]{2,1,0:T(8,128)(2,1)S(1)}, u32[]{:S(2)}, u32[]{:S(2)}) async-start(bf16[32,8,896]{2,1,0:T(8,128)(2,1)} %bitcast.9), calls=%async_computation.1 | async-start | bytes 917504 | tf_op jit(solution)/shard_map/all_to_all | solution.py:512
  102.8 3.1 %reshape.51.got = bf16[256,1664]{1,0:T(8,128)(2,1)} reshape(bf16[128,2,1664]{2,1,0:T(2,128)(2,1)} %all-to-all-done) | data formatting | bytes 1703936 | tf_op jit(solution)/shard_map/reshape | solution.py:521
  113.8 4.1 %all-to-all-done.1 = bf16[32,8,896]{2,1,0:T(8,128)(2,1)S(1)} async-done(((bf16[32,8,896]{2,1,0:T(8,128)(2,1)}), bf16[32,8,896]{2,1,0:T(8,128)(2,1)S(1)}, u32[]{:S(2)}, u32[]{:S(2)}) %all-to-all-start.1) | async-done | bytes 458784 | tf_op jit(solution)/shard_map/all_to_all | solution.py:512
  119.9 3.6 %all-to-all-start.2 = ((bf16[4,64,768]{2,1,0:T(8,128)(2,1)}), bf16[4,64,768]{2,1,0:T(8,128)(2,1)S(1)}, u32[]{:S(2)}, u32[]{:S(2)}) async-start(bf16[4,64,768]{2,1,0:T(8,128)(2,1)} %shard_map.206), calls=%async_computation.2 | async-start | bytes 786432 | tf_op jit(solution)/shard_map/all_to_all | solution.py:33
  125.9 5.8 %all-to-all-done.2 = bf16[4,64,768]{2,1,0:T(8,128)(2,1)S(1)} async-done(((bf16[4,64,768]{2,1,0:T(8,128)(2,1)}), bf16[4,64,768]{2,1,0:T(8,128)(2,1)S(1)}, u32[]{:S(2)}, u32[]{:S(2)}) %all-to-all-start.2) | async-done | bytes 393248 | tf_op jit(solution)/shard_map/all_to_all | solution.py:33
  132.6 18.1 %all_to_all.30 = bf16[4,16,384]{2,1,0:T(8,128)(2,1)S(1)} all-to-all(bf16[4,16,384]{2,1,0:T(8,128)(2,1)S(1)} %get-tuple-element.49), channel_id=1, replica_groups=mesh['section'=4,'zh'=4,'zl'=4,'y'=4,'core'=2] {'zh'}, dimensions={0} | all-to-all | bytes 98304 | tf_op jit(solution)/shard_map/all_to_all | solution.py:33
  150.8 22.7 %all_to_all.31 = bf16[16,64,384]{2,1,0:T(8,128)(2,1)S(1)} all-to-all(bf16[16,64,384]{2,1,0:T(8,128)(2,1)S(1)} %broadcast_in_dim.88), channel_id=1, replica_groups=mesh['section'=4,'zh'=4,'zl'=4,'y'=4,'core'=2] {'zl','y'}, dimensions={0} | all-to-all | bytes 1572864 | tf_op jit(solution)/shard_map/all_to_all | solution.py:33
  173.5 4.7 %collective-permute-start.8 = (bf16[1024,384]{1,0:T(8,128)(2,1)S(1)}, bf16[1024,384]{1,0:T(8,128)(2,1)S(1)}, u32[]{:S(2)}, u32[]{:S(2)}) collective-permute-start(bf16[1024,384]{1,0:T(8,128)(2,1)S(1)} %bitcast.24), channel_id=1, source_target_pairs={{0,1},{1,0},{2,3},{3,2},{4,5},{5,4},{6,7},{7,6},{8,9},{9,8},{10,11... | collective-permute-start | bytes 2359304 | tf_op jit(solution)/shard_map/ppermute | solution.py:29
  183.2 10.2 %all_to_all.32.parts = bf16[4,192,256]{2,1,0:T(8,128)(2,1)S(1)} all-to-all(bf16[4,192,256]{2,1,0:T(8,128)(2,1)S(1)} %bitcast.22), channel_id=1, replica_groups=mesh['section'=4,'zh'=4,'zl'=4,'y'=4,'core'=2] {'section'}, dimensions={0} | all-to-all | bytes 786432 | tf_op jit(solution)/shard_map/all_to_all | solution.py:575
  (116 shorter events, 23.1 us)
Async XLA Ops:
  0.0 10.2 %copy-start.28 = (s32[160]{0:T(256)S(1)}, s32[160]{0:T(256)}, u32[]{:S(2)}) copy-start(s32[160]{0:T(256)} %param.34) | copy-start | bytes 1924
  3.0 31.9 %collective-permute-start.1 = (bf16[1552,384]{1,0:T(8,128)(2,1)}, bf16[1552,384]{1,0:T(8,128)(2,1)S(1)}, u32[]{:S(2)}, u32[]{:S(2)}) collective-permute-start(bf16[1552,384]{1,0:T(8,128)(2,1)} %shard_map.199.block), channel_id=1, source_target_pairs={{0,384},{128,0},{256,128},{384,256},{1,385},{129,1},{257,129},{385... | collective-permute-start | bytes 3575816 | tf_op jit(solution)/shard_map/ppermute | solution.py:29
  8.3 27.5 %collective-permute-start = (bf16[1552,384]{1,0:T(8,128)(2,1)}, bf16[1552,384]{1,0:T(8,128)(2,1)S(1)}, u32[]{:S(2)}, u32[]{:S(2)}) collective-permute-start(bf16[1552,384]{1,0:T(8,128)(2,1)} %shard_map.199.block), channel_id=1, source_target_pairs={{0,128},{128,256},{256,384},{384,0},{1,129},{129,257},{257,385},{3... | collective-permute-start | bytes 3575816 | tf_op jit(solution)/shard_map/ppermute | solution.py:29
  14.0 20.6 %copy-start.21 = (f32[7,7,768]{2,1,0:T(8,128)S(1)}, f32[7,7,768]{2,1,0:T(8,128)}, u32[]{:S(2)}) copy-start(f32[7,7,768]{2,1,0:T(8,128)} %param.22) | copy-start | bytes 451588
  14.0 20.7 %copy-start.22 = (f32[768]{0:T(1024)S(1)}, f32[768]{0:T(1024)}, u32[]{:S(2)}) copy-start(f32[768]{0:T(1024)} %param.23) | copy-start | bytes 9220
  14.1 20.7 %copy-start.23 = (f32[768]{0:T(1024)S(1)}, f32[768]{0:T(1024)}, u32[]{:S(2)}) copy-start(f32[768]{0:T(1024)} %param.24) | copy-start | bytes 9220
  14.1 20.7 %copy-start.24 = (f32[768]{0:T(1024)S(1)}, f32[768]{0:T(1024)}, u32[]{:S(2)}) copy-start(f32[768]{0:T(1024)} %param.29) | copy-start | bytes 9220
  14.1 20.7 %copy-start.25 = (f32[768]{0:T(1024)S(1)}, f32[768]{0:T(1024)}, u32[]{:S(2)}) copy-start(f32[768]{0:T(1024)} %param.28) | copy-start | bytes 9220
  14.1 20.7 %copy-start.26 = (f32[768]{0:T(1024)S(1)}, f32[768]{0:T(1024)}, u32[]{:S(2)}) copy-start(f32[768]{0:T(1024)} %param.30) | copy-start | bytes 9220
  14.1 79.3 %all-to-all-start = ((bf16[128,2,1664]{2,1,0:T(2,128)(2,1)}), bf16[128,2,1664]{2,1,0:T(2,128)(2,1)}, u32[]{:S(2)}, u32[]{:S(2)}) async-start(bf16[128,2,1664]{2,1,0:T(2,128)(2,1)} %reshape.48), calls=%async_computation | async-start | bytes 1703936 | tf_op jit(solution)/shard_map/all_to_all | solution.py:449
  35.0 15.0 %copy-start.19 = (bf16[8,8,8,768]{3,2,1,0:T(8,128)(2,1)S(1)}, bf16[8,8,8,768]{3,2,1,0:T(8,128)(2,1)}, u32[]{:S(2)}) copy-start(bf16[8,8,8,768]{3,2,1,0:T(8,128)(2,1)} %param.21) | copy-start | bytes 2359300
  35.8 23.3 %collective-permute-start.3 = (bf16[784,384]{1,0:T(8,128)(2,1)S(1)}, bf16[784,384]{1,0:T(8,128)(2,1)S(1)}, u32[]{:S(2)}, u32[]{:S(2)}) collective-permute-start(bf16[784,384]{1,0:T(8,128)(2,1)S(1)} %slice.37), channel_id=1, source_target_pairs={{0,384},{128,0},{256,128},{384,256},{1,385},{129,1},{257,129},{385... | collective-permute-start | bytes 1806344 | tf_op jit(solution)/shard_map/ppermute | solution.py:29
  40.1 18.9 %collective-permute-start.2 = (bf16[768,384]{1,0:T(8,128)(2,1)S(1)}, bf16[768,384]{1,0:T(8,128)(2,1)S(1)}, u32[]{:S(2)}, u32[]{:S(2)}) collective-permute-start(bf16[768,384]{1,0:T(8,128)(2,1)S(1)} %slice.36), channel_id=1, source_target_pairs={{0,128},{128,256},{256,384},{384,0},{1,129},{129,257},{257,385},{3... | collective-permute-start | bytes 1769480 | tf_op jit(solution)/shard_map/ppermute | solution.py:29
  42.1 21.4 %collective-permute-start.4 = (bf16[1552,384]{1,0:T(8,128)(2,1)S(1)}, bf16[1552,384]{1,0:T(8,128)(2,1)S(1)}, u32[]{:S(2)}, u32[]{:S(2)}) collective-permute-start(bf16[1552,384]{1,0:T(8,128)(2,1)S(1)} %collective-permute-done.left), channel_id=1, source_target_pairs={{0,1},{1,0},{2,3},{3,2},{4,5},{5,4},{6,7},{7,6},{8,9},{9,8},{10,11... | collective-permute-start | bytes 3575816 | tf_op jit(solution)/shard_map/ppermute | solution.py:29
  48.1 15.4 %collective-permute-start.5 = (bf16[1552,384]{1,0:T(8,128)(2,1)S(1)}, bf16[1552,384]{1,0:T(8,128)(2,1)S(1)}, u32[]{:S(2)}, u32[]{:S(2)}) collective-permute-start(bf16[1552,384]{1,0:T(8,128)(2,1)S(1)} %collective-permute-done.1.right), channel_id=1, source_target_pairs={{0,1},{1,0},{2,3},{3,2},{4,5},{5,4},{6,7},{7,6},{8,9},{9,8},{10,11... | collective-permute-start | bytes 3575816 | tf_op jit(solution)/shard_map/ppermute | solution.py:29
  50.0 13.5 %copy-start.12 = (bf16[1552,384]{1,0:T(8,128)(2,1)S(1)}, bf16[1552,384]{1,0:T(8,128)(2,1)}, u32[]{:S(2)}) copy-start(bf16[1552,384]{1,0:T(8,128)(2,1)} %shard_map.199.block) | copy-start | bytes 3575812
  50.0 13.5 %copy-start.17 = (bf16[384,768]{1,0:T(8,128)(2,1)S(1)}, bf16[384,768]{1,0:T(8,128)(2,1)}, u32[]{:S(2)}) copy-start(bf16[384,768]{1,0:T(8,128)(2,1)} %up.1) | copy-start | bytes 1769476
  59.1 6.8 %collective-permute-start.7 = (bf16[784,384]{1,0:T(8,128)(2,1)S(1)}, bf16[784,384]{1,0:T(8,128)(2,1)S(1)}, u32[]{:S(2)}, u32[]{:S(2)}) collective-permute-start(bf16[784,384]{1,0:T(8,128)(2,1)S(1)} %collective-permute-done.3.high), channel_id=1, source_target_pairs={{0,1},{1,0},{2,3},{3,2},{4,5},{5,4},{6,7},{7,6},{8,9},{9,8},{10,11... | collective-permute-start | bytes 1806344 | tf_op jit(solution)/shard_map/ppermute | solution.py:29
  61.5 4.3 %collective-permute-start.6 = (bf16[768,384]{1,0:T(8,128)(2,1)S(1)}, bf16[768,384]{1,0:T(8,128)(2,1)S(1)}, u32[]{:S(2)}, u32[]{:S(2)}) collective-permute-start(bf16[768,384]{1,0:T(8,128)(2,1)S(1)} %collective-permute-done.2.low), channel_id=1, source_target_pairs={{0,1},{1,0},{2,3},{3,2},{4,5},{5,4},{6,7},{7,6},{8,9},{9,8},{10,11... | collective-permute-start | bytes 1769480 | tf_op jit(solution)/shard_map/ppermute | solution.py:29
  93.4 24.5 %all-to-all-start.1 = ((bf16[32,8,896]{2,1,0:T(8,128)(2,1)}), bf16[32,8,896]{2,1,0:T(8,128)(2,1)S(1)}, u32[]{:S(2)}, u32[]{:S(2)}) async-start(bf16[32,8,896]{2,1,0:T(8,128)(2,1)} %bitcast.9), calls=%async_computation.1 | async-start | bytes 917504 | tf_op jit(solution)/shard_map/all_to_all | solution.py:512
  113.8 9.7 %copy-start.31 = (s32[12]{0:T(128)S(1)}, s32[12]{0:T(128)}, u32[]{:S(2)}) copy-start(s32[12]{0:T(128)} %param.40) | copy-start | bytes 148
  119.9 11.8 %all-to-all-start.2 = ((bf16[4,64,768]{2,1,0:T(8,128)(2,1)}), bf16[4,64,768]{2,1,0:T(8,128)(2,1)S(1)}, u32[]{:S(2)}, u32[]{:S(2)}) async-start(bf16[4,64,768]{2,1,0:T(8,128)(2,1)} %shard_map.206), calls=%async_computation.2 | async-start | bytes 786432 | tf_op jit(solution)/shard_map/all_to_all | solution.py:33
  150.7 27.5 %copy-start.20 = (bf16[192,768]{1,0:T(8,128)(2,1)S(1)}, bf16[192,768]{1,0:T(8,128)(2,1)}, u32[]{:S(2)}) copy-start(bf16[192,768]{1,0:T(8,128)(2,1)} %param.41) | copy-start | bytes 884740
  173.5 6.6 %collective-permute-start.8 = (bf16[1024,384]{1,0:T(8,128)(2,1)S(1)}, bf16[1024,384]{1,0:T(8,128)(2,1)S(1)}, u32[]{:S(2)}, u32[]{:S(2)}) collective-permute-start(bf16[1024,384]{1,0:T(8,128)(2,1)S(1)} %bitcast.24), channel_id=1, source_target_pairs={{0,1},{1,0},{2,3},{3,2},{4,5},{5,4},{6,7},{7,6},{8,9},{9,8},{10,11... | collective-permute-start | bytes 2359304 | tf_op jit(solution)/shard_map/ppermute | solution.py:29
  (20 other events, 34.2 us)

commit v8 on v6

--- a/solution.py
+++ b/solution.py
@@ -29,10 +29,8 @@
     return lax.ppermute(block, axis, [(i, (i + step) % size) for i in range(size)])
 
 
-def spread(block, axis, size):
-    return lax.all_to_all(
-        jnp.broadcast_to(block[None], (size,) + block.shape), axis, 0, 0, tiled=True
-    )
+def exchange(copies, axis):
+    return lax.all_to_all(copies, axis, 0, 0, tiled=True)
 
 
 NT = (((1,), (1,)), ((), ()))
@@ -51,7 +49,7 @@
     return ref[:, pl.ds(pl.multiple_of(index * width, 128), width)]
 
 
-def pack_kernel(core_ref, w_up, w_down, w_head, w_in, bias, out, sems):
+def pack_kernel(core_ref, w_up, w_down, w_head, w_in, bias, out, rows, sems):
     n = w_up.shape[0]
     start = pl.multiple_of(core_ref[0] * n, n)
     parts = (
@@ -66,7 +64,9 @@
     ]
     for copy in copies:
         copy.start()
-    out[4 * n :, :] = jnp.broadcast_to(bias[...][None, :], (16, n))
+    rows[...] = jnp.broadcast_to(bias[...][None, :], (16, n))
+    copies.append(pltpu.make_async_copy(rows, out.at[pl.ds(4 * n, 16), :], sems.at[4]))
+    copies[-1].start()
     for copy in copies:
         copy.wait()
 
@@ -79,9 +79,9 @@
         in_specs=[pl.BlockSpec(memory_space=pltpu.SMEM)]
         + [pl.BlockSpec(memory_space=pl.ANY)] * 4
         + [vmem],
-        out_specs=vmem,
+        out_specs=pl.BlockSpec(memory_space=pl.ANY),
         out_shape=jax.ShapeDtypeStruct((4 * n + 16, n), BF16),
-        scratch_shapes=[pltpu.SemaphoreType.DMA((4,))],
+        scratch_shapes=[pltpu.VMEM((16, n), BF16), pltpu.SemaphoreType.DMA((5,))],
         cost_estimate=pl.CostEstimate(flops=0, bytes_accessed=4 * n * n * 4, transcendentals=0),
     )(core.astype(jnp.int32)[None], w_up, w_down, w_head, w_in, bias)
 
@@ -91,7 +91,8 @@
 
 
 def conv_kernel(feats, dw_weight, dw_bias, gain, out, mean, conv):
-    tiles, side, _, channels = feats.shape
+    tiles, channels = mean.shape
+    side = math.isqrt(feats.shape[0] // tiles)
     taps = math.isqrt(dw_weight.shape[0])
     reach = (taps - 1) // 2
     column = lax.broadcasted_iota(jnp.int32, (side, side, 128), 1)
@@ -99,9 +100,11 @@
     mean[...] = jnp.zeros_like(mean)
 
     def one_tile(tile, carry):
+        start = pl.multiple_of(tile * side * side, side * side)
         for chunk in range(channels // 128):
             cols = pl.ds(chunk * 128, 128)
-            source = feats[tile, :, :, cols].astype(F32)
+            source = feats[pl.ds(start, side * side), cols].astype(F32)
+            source = source.reshape(side, side, 128)
             total = jnp.sum(jnp.sum(source, axis=0), axis=0, keepdims=True)
             total = jnp.broadcast_to(total * (1.0 / (side * side)), (tiles, 128))
             mean[:, cols] = jnp.where(tile_row == tile, total, mean[:, cols])
@@ -122,11 +125,14 @@
                             sums[i] = sums[i] + moved[i + a - reach] * tap
             for i in range(side):
                 conv[i * side : (i + 1) * side, cols] = sums[i]
-        start = pl.multiple_of(tile * side * side, side * side)
         out[pl.ds(start, side * side), :] = layer_norm(conv[...], gain[...]).astype(BF16)
         return carry
 
     lax.fori_loop(0, tiles, one_tile, 0)
+
+
+def first_row(ref, start):
+    return ref[start : start + 16, :].astype(F32)[0:1, :]
 
 
 def early_kernel(where, maps, up, block, left, right, left_swap, right_swap, hid):
@@ -135,11 +141,11 @@
     tiles = hid.shape[1]
     maps_a, maps_b = lanes(maps, core, n), lanes(maps, 1 - core, n)
     pre = lax.dot_general(maps[...], up[...], NT, preferred_element_type=F32)
-    hid[0] = gelu_mean(pre + block[4 * n : 4 * n + 1, :].astype(F32), tiles)
+    hid[0] = gelu_mean(pre + first_row(block, 4 * n), tiles)
     for slot, (a, b) in enumerate(((left, left_swap), (right, right_swap))):
         pre = lax.dot_general(maps_a, a[0:n, :], NT, preferred_element_type=F32)
         pre += lax.dot_general(maps_b, b[0:n, :], NT, preferred_element_type=F32)
-        hid[slot + 1] = gelu_mean(pre + a[4 * n : 4 * n + 1, :].astype(F32), tiles)
+        hid[slot + 1] = gelu_mean(pre + first_row(a, 4 * n), tiles)
 
 
 def late_kernel(
@@ -153,7 +159,7 @@
     pre += lax.dot_general(
         lanes(maps, 1 - core, n), low_swap[0:n, :], NT, preferred_element_type=F32
     )
-    hid_far = gelu_mean(pre + high[2 * n : 2 * n + 1, :].astype(F32), tiles)
+    hid_far = gelu_mean(pre + first_row(high, 2 * n), tiles)
 
     def exact(block):
         upper = block.astype(BF16)
@@ -244,7 +250,9 @@
 
 
 def arrive_kernel(got, earlier, out):
-    out[...] = (place_rows(got, out.shape[0]) + earlier[...]).astype(BF16)
+    rows = (place_rows(got, out.shape[1]) + earlier[...]).astype(BF16)
+    for copy in range(out.shape[0]):
+        out[copy] = rows
 
 
 def local_call(body, outs, scratch, flops, size, *operands):
@@ -293,7 +301,9 @@
     v_rows = dot(normed, w_v[...]).astype(BF16)
     q[...], k[...], v[...] = q_rows, k_rows, v_rows
     far_q[...] = far_rows(q_rows)
-    far_kv[...] = jnp.concatenate([far_rows(k_rows), far_rows(v_rows)], axis=1).astype(BF16)
+    pairs = jnp.concatenate([far_rows(k_rows), far_rows(v_rows)], axis=1).astype(BF16)
+    for copy in range(far_kv.shape[0]):
+        far_kv[copy] = pairs
 
 
 def by_head(block):
@@ -458,7 +468,7 @@
         30_000_000_000,
         8_000_000,
         0,
-        feats, dw_weight.reshape(-1, channels), row(dw_bias), row(ln1_gain),
+        feats.reshape(-1, channels), dw_weight.reshape(-1, channels), row(dw_bias), row(ln1_gain),
         scratch=[pltpu.VMEM((pixels, channels), F32)],
     )
     low, high, normed_maps, feat_mean = lax.optimization_barrier(
@@ -490,14 +500,16 @@
         high_swap,
     )
     got_prior, fresh = lax.optimization_barrier((got_prior, fresh))
-    fresh_z = spread(fresh, "z", N_Z).reshape(N_Z * tiles, channels + 128)
+    fresh_z = exchange(jnp.broadcast_to(fresh[None], (N_Z,) + fresh.shape), "z")
+    fresh_z = fresh_z.reshape(N_Z * tiles, channels + 128)
     x_earlier = local_call(
         earlier_kernel,
         jax.ShapeDtypeStruct((q_rows, channels), F32),
         [pltpu.VMEM((q_rows, prior.shape[1]), BF16)],
         500_000_000,
         4_000_000,
-        where, got_prior.reshape(send.shape), w_in, left, right, left_swap, right_swap, high, high_swap,
+        where, got_prior.reshape(send.shape), w_in, left, right, left_swap, right_swap, high,
+        high_swap,
     )
     fresh_z, x_earlier = lax.optimization_barrier((fresh_z, x_earlier))
     plane = N_Y * N_CORE
@@ -511,17 +523,17 @@
         where, fresh_z,
     )
     got = lax.all_to_all(
-        to_plane.reshape(plane, room, channels + 128), ("y", "core"), 0, 0, tiled=True
+        to_plane.reshape(plane, room, channels + 128), SEQ_AXES[1:], 0, 0, tiled=True
     ).reshape(plane * room, channels + 128)
-    x_local = vmem_call(
+    x_copies = vmem_call(
         arrive_kernel,
-        jax.ShapeDtypeStruct((q_rows, channels), BF16),
+        jax.ShapeDtypeStruct((n_section, q_rows, channels), BF16),
         30_000_000,
         1_000_000,
         0,
         got, x_earlier,
     )
-    x_rows = spread(x_local, "section", n_section).reshape(ROWS, channels)
+    x_rows = exchange(x_copies, "section").reshape(ROWS, channels)
 
     heads_here = w_qkv.shape[1] // (3 * HS)
     width = heads_here * HS
@@ -533,14 +545,14 @@
     q, k, v, far_q, far_kv = vmem_call(
         project_kernel,
         (small(ROWS, BF16),) * 3
-        + (small(stride_rows, F32), jax.ShapeDtypeStruct((stride_rows, 2 * width), BF16)),
+        + (small(stride_rows, F32), jax.ShapeDtypeStruct((N_Z, stride_rows, 2 * width), BF16)),
         300_000_000,
         2_000_000,
         0,
         x_rows, row(ln_gain), w_q, w_k, w_v, row(jnp.tile(qn_gain, heads_here)),
         row(jnp.tile(kn_gain, heads_here)), off_lane,
     )
-    z_kv = spread(far_kv, "z", N_Z).reshape(N_Z * stride_rows, 2 * width)
+    z_kv = exchange(far_kv, "z").reshape(N_Z * stride_rows, 2 * width)
     half_kv = lax.all_gather(z_kv, "y", axis=0, tiled=True)
     other_kv = rotate(half_kv, "core", N_CORE, 1)
     width_part = channels // n_section

time: 186 us -> 220 us (1.18)
  Pallas kernels: 24.9 us -> 60.3 us
    pallas_call x1, Pallas kernels: 3 us -> 37.6 us  [pack(): pl.pallas_call(pack_kernel, in_specs=[pl.BlockSpec(memory_space=pltpu.SME...]
  transfers between devices with their start and end apart: 12 -> 12, of which waited for: 4 -> 4; matrix products, arithmetic and copies ran while one was open for 4% -> 3% of each run, Pallas kernels for 10% -> 8%
where the time goes in v8:
time: 220 us; the launch traced here: 219 us
  starting transfers between devices  66.7 us (30%)
  Pallas kernels  60.3 us (27%)
  blocking collectives  58 us (26%)
  local copies, waits for them, and re-layouts  16.7 us (8%)
  waiting for transfers between devices  15.9 us (7%)
    pallas_call x1, Pallas kernels, pack(): pl.pallas_call(pack_kernel, in_specs=[pl.BlockSpec(memory_space=pltpu.SME...  37.6 us
    ppermute x9, starting transfers between devices, rotate(): lax.ppermute(block, axis, [(i, (i + step) % size) for i in range(size)])  35.6 us
    all_to_all x1, starting transfers between devices, shards(): lax.all_to_all(send.reshape(n_seq, capacity, send.shape[1]), SEQ_AXES, 0,...  20.6 us
    all_to_all x1, blocking collectives, exchange(): return lax.all_to_all(copies, axis, 0, 0, tiled=True)  17.6 us
    all_to_all x1, blocking collectives, shards(): lax.all_to_all(to_plane.reshape(plane, room, channels + 128), SEQ_AXES[1:...  17.6 us
    pallas_call x6, Pallas kernels, vmem_call(): pl.pallas_call(body, in_specs=[vmem] * len(operands), out_specs=jax.tree....  13.1 us
    all_gather x1, blocking collectives, shards(): half_kv = lax.all_gather(z_kv, 'y', axis=0, tiled=True)  12.5 us
    all_to_all x2, starting transfers between devices, exchange(): return lax.all_to_all(copies, axis, 0, 0, tiled=True)  10.6 us
  transfers between devices with their start and end apart: 12, of which 4 were waited for; matrix products, arithmetic and copies ran while one was open for 3% of the time, Pallas kernels for 8%

profile of v8, /device:TPU:1, one launch (start us, length us, event | category | flops | bytes accessed | tf_op | source)
XLA Modules:
  0.0 219.3 jit_solution(6308201542814353590)
XLA Ops:
  0.0 37.6 %shard_map.199.block = bf16[1552,384]{1,0:T(8,128)(2,1)} custom-call(s32[1]{0:T(128)} %bitcast.core_ref, bf16[384,768]{1,0:T(8,128)(2,1)} %up.1, bf16[384,768]{1,0:T(8,128)(2,1)} %w_down.3, bf16[768,384]{1,0:T(8,128)(2,1)} %w_head.3, bf16[384,768]{1,0:T(8,128)(2,1)} %w_in.5, bf16[384]{0:T(512)(128)(2,1)} %bias.1), custom_call_target="tpu_custom_call" | custom-call | bytes 2359296 | tf_op jit(solution)/shard_map/pallas_call | solution.py:77
  37.6 5.2 %collective-permute-start.1 = (bf16[1552,384]{1,0:T(8,128)(2,1)}, bf16[1552,384]{1,0:T(8,128)(2,1)S(1)}, u32[]{:S(2)}, u32[]{:S(2)}) collective-permute-start(bf16[1552,384]{1,0:T(8,128)(2,1)} %shard_map.199.block), channel_id=1, source_target_pairs={{0,384},{128,0},{256,128},{384,256},{1,385},{129,1},{257,129},{385... | collective-permute-start | bytes 3575816 | tf_op jit(solution)/shard_map/ppermute | solution.py:29
  48.7 20.6 %all-to-all-start = ((bf16[128,2,1664]{2,1,0:T(2,128)(2,1)}), bf16[128,2,1664]{2,1,0:T(2,128)(2,1)}, u32[]{:S(2)}, u32[]{:S(2)}) async-start(bf16[128,2,1664]{2,1,0:T(2,128)(2,1)} %reshape.49), calls=%async_computation | async-start | bytes 1703936 | tf_op jit(solution)/shard_map/all_to_all | solution.py:451
  70.3 4.4 %collective-permute-start.3 = (bf16[784,384]{1,0:T(8,128)(2,1)S(1)}, bf16[784,384]{1,0:T(8,128)(2,1)S(1)}, u32[]{:S(2)}, u32[]{:S(2)}) collective-permute-start(bf16[784,384]{1,0:T(8,128)(2,1)S(1)} %slice.37), channel_id=1, source_target_pairs={{0,384},{128,0},{256,128},{384,256},{1,385},{129,1},{257,129},{385... | collective-permute-start | bytes 1806344 | tf_op jit(solution)/shard_map/ppermute | solution.py:29
  74.7 1.9 collective-permute-start.2
  76.6 6.0 %collective-permute-start.4 = (bf16[1552,384]{1,0:T(8,128)(2,1)S(1)}, bf16[1552,384]{1,0:T(8,128)(2,1)S(1)}, u32[]{:S(2)}, u32[]{:S(2)}) collective-permute-start(bf16[1552,384]{1,0:T(8,128)(2,1)S(1)} %collective-permute-done.left), channel_id=1, source_target_pairs={{0,1},{1,0},{2,3},{3,2},{4,5},{5,4},{6,7},{7,6},{8,9},{9,8},{10,11... | collective-permute-start | bytes 3575816 | tf_op jit(solution)/shard_map/ppermute | solution.py:29
  82.6 1.9 collective-permute-start.5
  84.6 9.0 %shard_map.201 = (bf16[512,768]{1,0:T(8,128)(2,1)S(1)}, f32[8,768]{1,0:T(8,128)S(1)}) custom-call(bf16[512,768]{1,0:T(8,128)(2,1)S(1)} %bitcast.27, f32[49,768]{1,0:T(8,128)S(1)} %reshape.51.dw_weight, f32[1,768]{1,0:T(1,128)S(1)} %broadcast_in_dim.76.dw_bias, f32[1,768]{1,0:T(1,128)S(1)} %broadcast_in_dim.77.gain), custom_call_target="tpu_custom_call" | custom-call | flops 30000001024 | bytes 8000000 | tf_op jit(solution)/shard_map/pallas_call | solution.py:375
  93.6 2.4 %collective-permute-start.7 = (bf16[784,384]{1,0:T(8,128)(2,1)S(1)}, bf16[784,384]{1,0:T(8,128)(2,1)S(1)}, u32[]{:S(2)}, u32[]{:S(2)}) collective-permute-start(bf16[784,384]{1,0:T(8,128)(2,1)S(1)} %collective-permute-done.3.high), channel_id=1, source_target_pairs={{0,1},{1,0},{2,3},{3,2},{4,5},{5,4},{6,7},{7,6},{8,9},{9,8},{10,11... | collective-permute-start | bytes 1806344 | tf_op jit(solution)/shard_map/ppermute | solution.py:29
  96.0 1.9 collective-permute-start.6
  98.1 2.3 %shard_map.202.hid = f32[3,8,384]{2,1,0:T(8,128)S(1)} custom-call(s32[6]{0:T(128)S(1)} %stack.27.where, bf16[512,768]{1,0:T(8,128)(2,1)S(1)} %get-tuple-element.39.maps, bf16[384,768]{1,0:T(8,128)(2,1)S(1)} %copy-done.13, bf16[1552,384]{1,0:T(8,128)(2,1)S(1)} %copy-done.12, bf16[1552,384]{1,0:T(8,128)(2,1)S(1)} %collective-permute-done.left, ...), custom_call_target="tpu_custom_call" | custom-call | flops 2000000000 | bytes 6000000 | tf_op jit(solution)/shard_map/pallas_call | solution.py:260
  100.4 2.9 %shard_map.203 = bf16[8,896]{1,0:T(8,128)(2,1)S(1)} custom-call(s32[6]{0:T(128)S(1)} %stack.27.where, bf16[512,768]{1,0:T(8,128)(2,1)S(1)} %get-tuple-element.39.maps, f32[3,8,384]{2,1,0:T(8,128)S(1)} %shard_map.202.hid, f32[8,768]{1,0:T(8,128)S(1)} %get-tuple-element.42.feat_mean, f32[1,768]{1,0:T(1,128)S(1)} %broadcast_in_dim.78.layer_scale, ...), custom_call_target="tpu_custom_call" | custom-call | flops 2000000000 | bytes 8000000 | tf_op jit(solution)/shard_map/pallas_call | solution.py:260
  104.2 8.7 %all-to-all-done = bf16[128,2,1664]{2,1,0:T(2,128)(2,1)} async-done(((bf16[128,2,1664]{2,1,0:T(2,128)(2,1)}), bf16[128,2,1664]{2,1,0:T(2,128)(2,1)}, u32[]{:S(2)}, u32[]{:S(2)}) %all-to-all-start) | async-done | bytes 852000 | tf_op jit(solution)/shard_map/all_to_all | solution.py:451
  113.6 7.0 %all-to-all-start.1 = ((bf16[16,8,896]{2,1,0:T(8,128)(2,1)}), bf16[16,8,896]{2,1,0:T(8,128)(2,1)S(1)}, u32[]{:S(2)}, u32[]{:S(2)}) async-start(bf16[16,8,896]{2,1,0:T(8,128)(2,1)} %broadcast_in_dim.84), calls=%async_computation.1 | async-start | bytes 458752 | tf_op jit(solution)/shard_map/all_to_all | solution.py:33
  120.6 3.1 %reshape.53.got = bf16[256,1664]{1,0:T(8,128)(2,1)} reshape(bf16[128,2,1664]{2,1,0:T(2,128)(2,1)} %all-to-all-done) | data formatting | bytes 1703936 | tf_op jit(solution)/shard_map/reshape | solution.py:511
  130.9 2.4 %all-to-all-done.1 = bf16[16,8,896]{2,1,0:T(8,128)(2,1)S(1)} async-done(((bf16[16,8,896]{2,1,0:T(8,128)(2,1)}), bf16[16,8,896]{2,1,0:T(8,128)(2,1)S(1)}, u32[]{:S(2)}, u32[]{:S(2)}) %all-to-all-start.1) | async-done | bytes 229408 | tf_op jit(solution)/shard_map/all_to_all | solution.py:33
  134.3 17.6 %all_to_all.30 = bf16[8,32,896]{2,1,0:T(8,128)(2,1)S(1)} all-to-all(bf16[8,32,896]{2,1,0:T(8,128)(2,1)S(1)} %bitcast.20), channel_id=1, replica_groups=mesh['section'=4,'z'=16,'y'=4,'core'=2] {'y','core'}, dimensions={0} | all-to-all | bytes 917504 | tf_op jit(solution)/shard_map/all_to_all | solution.py:525
  153.0 3.6 %all-to-all-start.3 = ((bf16[4,64,768]{2,1,0:T(8,128)(2,1)}), bf16[4,64,768]{2,1,0:T(8,128)(2,1)S(1)}, u32[]{:S(2)}, u32[]{:S(2)}) async-start(bf16[4,64,768]{2,1,0:T(8,128)(2,1)} %shard_map.206), calls=%async_computation.3 | async-start | bytes 786432 | tf_op jit(solution)/shard_map/all_to_all | solution.py:33
  158.9 4.2 %all-to-all-done.3 = bf16[4,64,768]{2,1,0:T(8,128)(2,1)S(1)} async-done(((bf16[4,64,768]{2,1,0:T(8,128)(2,1)}), bf16[4,64,768]{2,1,0:T(8,128)(2,1)S(1)}, u32[]{:S(2)}, u32[]{:S(2)}) %all-to-all-start.3) | async-done | bytes 393248 | tf_op jit(solution)/shard_map/all_to_all | solution.py:33
  164.0 17.6 %all_to_all.31 = bf16[16,16,384]{2,1,0:T(8,128)(2,1)S(1)} all-to-all(bf16[16,16,384]{2,1,0:T(8,128)(2,1)S(1)} %get-tuple-element.53), channel_id=1, replica_groups=mesh['section'=4,'z'=16,'y'=4,'core'=2] {'z'}, dimensions={0} | all-to-all | bytes 393216 | tf_op jit(solution)/shard_map/all_to_all | solution.py:33
  181.6 12.5 %all_gather.3.kv = bf16[1024,384]{1,0:T(8,128)(2,1)} all-gather(bf16[256,384]{1,0:T(8,128)(2,1)S(1)} %bitcast.28), channel_id=1, replica_groups=mesh['section'=4,'z'=16,'y'=4,'core'=2] {'y'}, dimensions={0}, use_global_device_ids=true | all-gather | bytes 983040 | tf_op jit(solution)/shard_map/all_gather | solution.py:556
  194.1 9.9 %collective-permute-start.8 = (bf16[1024,384]{1,0:T(8,128)(2,1)}, bf16[1024,384]{1,0:T(8,128)(2,1)S(1)}, u32[]{:S(2)}, u32[]{:S(2)}) collective-permute-start(bf16[1024,384]{1,0:T(8,128)(2,1)} %all_gather.3.kv), channel_id=1, source_target_pairs={{0,1},{1,0},{2,3},{3,2},{4,5},{5,4},{6,7},{7,6},{8,9},{9,8},{10,11... | collective-permute-start | bytes 2359304 | tf_op jit(solution)/shard_map/ppermute | solution.py:29
  205.1 2.0 shard_map.208
  208.3 10.3 %all_to_all.32.parts = bf16[4,192,256]{2,1,0:T(8,128)(2,1)S(1)} all-to-all(bf16[4,192,256]{2,1,0:T(8,128)(2,1)S(1)} %bitcast.23), channel_id=1, replica_groups=mesh['section'=4,'z'=16,'y'=4,'core'=2] {'section'}, dimensions={0} | all-to-all | bytes 786432 | tf_op jit(solution)/shard_map/all_to_all | solution.py:578
  (112 shorter events, 23.1 us)
Async XLA Ops:
  0.0 44.7 %copy-start.26 = (s32[160]{0:T(256)S(1)}, s32[160]{0:T(256)}, u32[]{:S(2)}) copy-start(s32[160]{0:T(256)} %param.34) | copy-start | bytes 1924
  37.6 32.0 %collective-permute-start.1 = (bf16[1552,384]{1,0:T(8,128)(2,1)}, bf16[1552,384]{1,0:T(8,128)(2,1)S(1)}, u32[]{:S(2)}, u32[]{:S(2)}) collective-permute-start(bf16[1552,384]{1,0:T(8,128)(2,1)} %shard_map.199.block), channel_id=1, source_target_pairs={{0,384},{128,0},{256,128},{384,256},{1,385},{129,1},{257,129},{385... | collective-permute-start | bytes 3575816 | tf_op jit(solution)/shard_map/ppermute | solution.py:29
  42.8 27.5 %collective-permute-start = (bf16[1552,384]{1,0:T(8,128)(2,1)}, bf16[1552,384]{1,0:T(8,128)(2,1)S(1)}, u32[]{:S(2)}, u32[]{:S(2)}) collective-permute-start(bf16[1552,384]{1,0:T(8,128)(2,1)} %shard_map.199.block), channel_id=1, source_target_pairs={{0,128},{128,256},{256,384},{384,0},{1,129},{129,257},{257,385},{3... | collective-permute-start | bytes 3575816 | tf_op jit(solution)/shard_map/ppermute | solution.py:29
  48.6 20.6 %copy-start.19 = (f32[7,7,768]{2,1,0:T(8,128)S(1)}, f32[7,7,768]{2,1,0:T(8,128)}, u32[]{:S(2)}) copy-start(f32[7,7,768]{2,1,0:T(8,128)} %param.22) | copy-start | bytes 451588
  48.6 20.7 %copy-start.20 = (f32[768]{0:T(1024)S(1)}, f32[768]{0:T(1024)}, u32[]{:S(2)}) copy-start(f32[768]{0:T(1024)} %param.23) | copy-start | bytes 9220
  48.6 20.7 %copy-start.21 = (f32[768]{0:T(1024)S(1)}, f32[768]{0:T(1024)}, u32[]{:S(2)}) copy-start(f32[768]{0:T(1024)} %param.24) | copy-start | bytes 9220
  48.6 20.7 %copy-start.22 = (f32[768]{0:T(1024)S(1)}, f32[768]{0:T(1024)}, u32[]{:S(2)}) copy-start(f32[768]{0:T(1024)} %param.29) | copy-start | bytes 9220
  48.6 20.7 %copy-start.23 = (f32[768]{0:T(1024)S(1)}, f32[768]{0:T(1024)}, u32[]{:S(2)}) copy-start(f32[768]{0:T(1024)} %param.28) | copy-start | bytes 9220
  48.6 20.7 %copy-start.24 = (f32[768]{0:T(1024)S(1)}, f32[768]{0:T(1024)}, u32[]{:S(2)}) copy-start(f32[768]{0:T(1024)} %param.30) | copy-start | bytes 9220
  48.7 64.2 %all-to-all-start = ((bf16[128,2,1664]{2,1,0:T(2,128)(2,1)}), bf16[128,2,1664]{2,1,0:T(2,128)(2,1)}, u32[]{:S(2)}, u32[]{:S(2)}) async-start(bf16[128,2,1664]{2,1,0:T(2,128)(2,1)} %reshape.49), calls=%async_computation | async-start | bytes 1703936 | tf_op jit(solution)/shard_map/all_to_all | solution.py:451
  69.5 15.0 %copy-start.15 = (bf16[8,8,8,768]{3,2,1,0:T(8,128)(2,1)S(1)}, bf16[8,8,8,768]{3,2,1,0:T(8,128)(2,1)}, u32[]{:S(2)}) copy-start(bf16[8,8,8,768]{3,2,1,0:T(8,128)(2,1)} %param.21) | copy-start | bytes 2359300
  70.3 23.3 %collective-permute-start.3 = (bf16[784,384]{1,0:T(8,128)(2,1)S(1)}, bf16[784,384]{1,0:T(8,128)(2,1)S(1)}, u32[]{:S(2)}, u32[]{:S(2)}) collective-permute-start(bf16[784,384]{1,0:T(8,128)(2,1)S(1)} %slice.37), channel_id=1, source_target_pairs={{0,384},{128,0},{256,128},{384,256},{1,385},{129,1},{257,129},{385... | collective-permute-start | bytes 1806344 | tf_op jit(solution)/shard_map/ppermute | solution.py:29
  74.7 18.9 %collective-permute-start.2 = (bf16[768,384]{1,0:T(8,128)(2,1)S(1)}, bf16[768,384]{1,0:T(8,128)(2,1)S(1)}, u32[]{:S(2)}, u32[]{:S(2)}) collective-permute-start(bf16[768,384]{1,0:T(8,128)(2,1)S(1)} %slice.36), channel_id=1, source_target_pairs={{0,128},{128,256},{256,384},{384,0},{1,129},{129,257},{257,385},{3... | collective-permute-start | bytes 1769480 | tf_op jit(solution)/shard_map/ppermute | solution.py:29
  76.6 21.4 %collective-permute-start.4 = (bf16[1552,384]{1,0:T(8,128)(2,1)S(1)}, bf16[1552,384]{1,0:T(8,128)(2,1)S(1)}, u32[]{:S(2)}, u32[]{:S(2)}) collective-permute-start(bf16[1552,384]{1,0:T(8,128)(2,1)S(1)} %collective-permute-done.left), channel_id=1, source_target_pairs={{0,1},{1,0},{2,3},{3,2},{4,5},{5,4},{6,7},{7,6},{8,9},{9,8},{10,11... | collective-permute-start | bytes 3575816 | tf_op jit(solution)/shard_map/ppermute | solution.py:29
  82.6 15.4 %collective-permute-start.5 = (bf16[1552,384]{1,0:T(8,128)(2,1)S(1)}, bf16[1552,384]{1,0:T(8,128)(2,1)S(1)}, u32[]{:S(2)}, u32[]{:S(2)}) collective-permute-start(bf16[1552,384]{1,0:T(8,128)(2,1)S(1)} %collective-permute-done.1.right), channel_id=1, source_target_pairs={{0,1},{1,0},{2,3},{3,2},{4,5},{5,4},{6,7},{7,6},{8,9},{9,8},{10,11... | collective-permute-start | bytes 3575816 | tf_op jit(solution)/shard_map/ppermute | solution.py:29
  84.5 13.5 %copy-start.12 = (bf16[1552,384]{1,0:T(8,128)(2,1)S(1)}, bf16[1552,384]{1,0:T(8,128)(2,1)}, u32[]{:S(2)}) copy-start(bf16[1552,384]{1,0:T(8,128)(2,1)} %shard_map.199.block) | copy-start | bytes 3575812
  93.6 6.8 %collective-permute-start.7 = (bf16[784,384]{1,0:T(8,128)(2,1)S(1)}, bf16[784,384]{1,0:T(8,128)(2,1)S(1)}, u32[]{:S(2)}, u32[]{:S(2)}) collective-permute-start(bf16[784,384]{1,0:T(8,128)(2,1)S(1)} %collective-permute-done.3.high), channel_id=1, source_target_pairs={{0,1},{1,0},{2,3},{3,2},{4,5},{5,4},{6,7},{7,6},{8,9},{9,8},{10,11... | collective-permute-start | bytes 1806344 | tf_op jit(solution)/shard_map/ppermute | solution.py:29
  96.0 4.4 %collective-permute-start.6 = (bf16[768,384]{1,0:T(8,128)(2,1)S(1)}, bf16[768,384]{1,0:T(8,128)(2,1)S(1)}, u32[]{:S(2)}, u32[]{:S(2)}) collective-permute-start(bf16[768,384]{1,0:T(8,128)(2,1)S(1)} %collective-permute-done.2.low), channel_id=1, source_target_pairs={{0,1},{1,0},{2,3},{3,2},{4,5},{5,4},{6,7},{7,6},{8,9},{9,8},{10,11... | collective-permute-start | bytes 1769480 | tf_op jit(solution)/shard_map/ppermute | solution.py:29
  113.6 19.7 %all-to-all-start.1 = ((bf16[16,8,896]{2,1,0:T(8,128)(2,1)}), bf16[16,8,896]{2,1,0:T(8,128)(2,1)S(1)}, u32[]{:S(2)}, u32[]{:S(2)}) async-start(bf16[16,8,896]{2,1,0:T(8,128)(2,1)} %broadcast_in_dim.84), calls=%async_computation.1 | async-start | bytes 458752 | tf_op jit(solution)/shard_map/all_to_all | solution.py:33
  134.3 22.3 %copy-start.29 = (s32[12]{0:T(128)S(1)}, s32[12]{0:T(128)}, u32[]{:S(2)}) copy-start(s32[12]{0:T(128)} %param.40) | copy-start | bytes 148
  153.0 10.1 %all-to-all-start.3 = ((bf16[4,64,768]{2,1,0:T(8,128)(2,1)}), bf16[4,64,768]{2,1,0:T(8,128)(2,1)S(1)}, u32[]{:S(2)}, u32[]{:S(2)}) async-start(bf16[4,64,768]{2,1,0:T(8,128)(2,1)} %shard_map.206), calls=%async_computation.3 | async-start | bytes 786432 | tf_op jit(solution)/shard_map/all_to_all | solution.py:33
  163.1 40.9 %copy-start.18 = (bf16[192,768]{1,0:T(8,128)(2,1)S(1)}, bf16[192,768]{1,0:T(8,128)(2,1)}, u32[]{:S(2)}) copy-start(bf16[192,768]{1,0:T(8,128)(2,1)} %param.41) | copy-start | bytes 884740
  164.0 40.2 %copy-start.16 = (bf16[256,192]{1,0:T(8,128)(2,1)}, bf16[256,192]{1,0:T(8,128)(2,1)S(1)}, u32[]{:S(2)}) copy-start(bf16[256,192]{1,0:T(8,128)(2,1)S(1)} %get-tuple-element.51.v) | copy-start | bytes 294916
  194.1 13.1 %collective-permute-start.8 = (bf16[1024,384]{1,0:T(8,128)(2,1)}, bf16[1024,384]{1,0:T(8,128)(2,1)S(1)}, u32[]{:S(2)}, u32[]{:S(2)}) collective-permute-start(bf16[1024,384]{1,0:T(8,128)(2,1)} %all_gather.3.kv), channel_id=1, source_target_pairs={{0,1},{1,0},{2,3},{3,2},{4,5},{5,4},{6,7},{7,6},{8,9},{9,8},{10,11... | collective-permute-start | bytes 2359304 | tf_op jit(solution)/shard_map/ppermute | solution.py:29
  (18 other events, 43.0 us)

commit v9 on v8

--- a/solution.py
+++ b/solution.py
@@ -49,7 +49,7 @@
     return ref[:, pl.ds(pl.multiple_of(index * width, 128), width)]
 
 
-def pack_kernel(core_ref, w_up, w_down, w_head, w_in, bias, out, rows, sems):
+def pack_kernel(core_ref, w_up, w_down, w_head, w_in, bias, out, sems):
     n = w_up.shape[0]
     start = pl.multiple_of(core_ref[0] * n, n)
     parts = (
@@ -64,9 +64,7 @@
     ]
     for copy in copies:
         copy.start()
-    rows[...] = jnp.broadcast_to(bias[...][None, :], (16, n))
-    copies.append(pltpu.make_async_copy(rows, out.at[pl.ds(4 * n, 16), :], sems.at[4]))
-    copies[-1].start()
+    out[4 * n :, :] = jnp.broadcast_to(bias[...][None, :], (16, n))
     for copy in copies:
         copy.wait()
 
@@ -79,9 +77,9 @@
         in_specs=[pl.BlockSpec(memory_space=pltpu.SMEM)]
         + [pl.BlockSpec(memory_space=pl.ANY)] * 4
         + [vmem],
-        out_specs=pl.BlockSpec(memory_space=pl.ANY),
+        out_specs=vmem,
         out_shape=jax.ShapeDtypeStruct((4 * n + 16, n), BF16),
-        scratch_shapes=[pltpu.VMEM((16, n), BF16), pltpu.SemaphoreType.DMA((5,))],
+        scratch_shapes=[pltpu.SemaphoreType.DMA((4,))],
         cost_estimate=pl.CostEstimate(flops=0, bytes_accessed=4 * n * n * 4, transcendentals=0),
     )(core.astype(jnp.int32)[None], w_up, w_down, w_head, w_in, bias)
 

time: 220 us -> 186 us (0.85)
  Pallas kernels: 60.3 us -> 25.7 us
    pallas_call x1, Pallas kernels: 37.6 us -> 3 us  [pack(): pl.pallas_call(pack_kernel, in_specs=[pl.BlockSpec(memory_space=pltpu.SME...]
  transfers between devices with their start and end apart: 12 -> 12, of which waited for: 4 -> 4; matrix products, arithmetic and copies ran while one was open for 3% -> 4% of each run, Pallas kernels for 8% -> 10%
where the time goes in v9:
time: 186 us; the launch traced here: 185 us
  starting transfers between devices  66.7 us (36%)
  blocking collectives  58 us (31%)
  Pallas kernels  25.7 us (14%)
  local copies, waits for them, and re-layouts  16.7 us (9%)
  waiting for transfers between devices  15.9 us (9%)
    ppermute x9, starting transfers between devices, rotate(): lax.ppermute(block, axis, [(i, (i + step) % size) for i in range(size)])  35.6 us
    all_to_all x1, starting transfers between devices, shards(): lax.all_to_all(send.reshape(n_seq, capacity, send.shape[1]), SEQ_AXES, 0,...  20.6 us
    all_to_all x1, blocking collectives, shards(): lax.all_to_all(to_plane.reshape(plane, room, channels + 128), SEQ_AXES[1:...  17.6 us
    all_to_all x1, blocking collectives, exchange(): return lax.all_to_all(copies, axis, 0, 0, tiled=True)  17.6 us
    pallas_call x6, Pallas kernels, vmem_call(): pl.pallas_call(body, in_specs=[vmem] * len(operands), out_specs=jax.tree....  13.1 us
    all_gather x1, blocking collectives, shards(): half_kv = lax.all_gather(z_kv, 'y', axis=0, tiled=True)  12.5 us
    all_to_all x2, starting transfers between devices, exchange(): return lax.all_to_all(copies, axis, 0, 0, tiled=True)  10.6 us
    all_to_all x1, blocking collectives, shards(): lax.all_to_all(partial_out.reshape(n_section, width_part, ROWS), 'section...  10.3 us
  transfers between devices with their start and end apart: 12, of which 4 were waited for; matrix products, arithmetic and copies ran while one was open for 4% of the time, Pallas kernels for 10%

profile of v9, /device:TPU:1, one launch (start us, length us, event | category | flops | bytes accessed | tf_op | source)
XLA Modules:
  0.0 184.8 jit_solution(8430394197897345951)
XLA Ops:
  0.0 3.0 %shard_map.199.block = bf16[1552,384]{1,0:T(8,128)(2,1)} custom-call(s32[1]{0:T(128)} %bitcast.core_ref, bf16[384,768]{1,0:T(8,128)(2,1)} %up.1, bf16[384,768]{1,0:T(8,128)(2,1)} %w_down.3, bf16[768,384]{1,0:T(8,128)(2,1)} %w_head.3, bf16[384,768]{1,0:T(8,128)(2,1)} %w_in.5, bf16[384]{0:T(512)(128)(2,1)} %bias.1), custom_call_target="tpu_custom_call" | custom-call | bytes 2359296 | tf_op jit(solution)/shard_map/pallas_call | solution.py:75
  3.0 5.2 %collective-permute-start.1 = (bf16[1552,384]{1,0:T(8,128)(2,1)}, bf16[1552,384]{1,0:T(8,128)(2,1)S(1)}, u32[]{:S(2)}, u32[]{:S(2)}) collective-permute-start(bf16[1552,384]{1,0:T(8,128)(2,1)} %shard_map.199.block), channel_id=1, source_target_pairs={{0,384},{128,0},{256,128},{384,256},{1,385},{129,1},{257,129},{385... | collective-permute-start | bytes 3575816 | tf_op jit(solution)/shard_map/ppermute | solution.py:29
  14.1 20.6 %all-to-all-start = ((bf16[128,2,1664]{2,1,0:T(2,128)(2,1)}), bf16[128,2,1664]{2,1,0:T(2,128)(2,1)}, u32[]{:S(2)}, u32[]{:S(2)}) async-start(bf16[128,2,1664]{2,1,0:T(2,128)(2,1)} %reshape.49), calls=%async_computation | async-start | bytes 1703936 | tf_op jit(solution)/shard_map/all_to_all | solution.py:449
  35.8 4.4 %collective-permute-start.3 = (bf16[784,384]{1,0:T(8,128)(2,1)S(1)}, bf16[784,384]{1,0:T(8,128)(2,1)S(1)}, u32[]{:S(2)}, u32[]{:S(2)}) collective-permute-start(bf16[784,384]{1,0:T(8,128)(2,1)S(1)} %slice.37), channel_id=1, source_target_pairs={{0,384},{128,0},{256,128},{384,256},{1,385},{129,1},{257,129},{385... | collective-permute-start | bytes 1806344 | tf_op jit(solution)/shard_map/ppermute | solution.py:29
  40.1 1.9 %collective-permute-start.2 = (bf16[768,384]{1,0:T(8,128)(2,1)S(1)}, bf16[768,384]{1,0:T(8,128)(2,1)S(1)}, u32[]{:S(2)}, u32[]{:S(2)}) collective-permute-start(bf16[768,384]{1,0:T(8,128)(2,1)S(1)} %slice.36), channel_id=1, source_target_pairs={{0,128},{128,256},{256,384},{384,0},{1,129},{129,257},{257,385},{3... | collective-permute-start | bytes 1769480 | tf_op jit(solution)/shard_map/ppermute | solution.py:29
  42.0 6.0 %collective-permute-start.4 = (bf16[1552,384]{1,0:T(8,128)(2,1)S(1)}, bf16[1552,384]{1,0:T(8,128)(2,1)S(1)}, u32[]{:S(2)}, u32[]{:S(2)}) collective-permute-start(bf16[1552,384]{1,0:T(8,128)(2,1)S(1)} %collective-permute-done.left), channel_id=1, source_target_pairs={{0,1},{1,0},{2,3},{3,2},{4,5},{5,4},{6,7},{7,6},{8,9},{9,8},{10,11... | collective-permute-start | bytes 3575816 | tf_op jit(solution)/shard_map/ppermute | solution.py:29
  48.0 1.9 %collective-permute-start.5 = (bf16[1552,384]{1,0:T(8,128)(2,1)S(1)}, bf16[1552,384]{1,0:T(8,128)(2,1)S(1)}, u32[]{:S(2)}, u32[]{:S(2)}) collective-permute-start(bf16[1552,384]{1,0:T(8,128)(2,1)S(1)} %collective-permute-done.1.right), channel_id=1, source_target_pairs={{0,1},{1,0},{2,3},{3,2},{4,5},{5,4},{6,7},{7,6},{8,9},{9,8},{10,11... | collective-permute-start | bytes 3575816 | tf_op jit(solution)/shard_map/ppermute | solution.py:29
  50.0 9.0 %shard_map.201 = (bf16[512,768]{1,0:T(8,128)(2,1)S(1)}, f32[8,768]{1,0:T(8,128)S(1)}) custom-call(bf16[512,768]{1,0:T(8,128)(2,1)S(1)} %bitcast.27, f32[49,768]{1,0:T(8,128)S(1)} %reshape.51.dw_weight, f32[1,768]{1,0:T(1,128)S(1)} %broadcast_in_dim.76.dw_bias, f32[1,768]{1,0:T(1,128)S(1)} %broadcast_in_dim.77.gain), custom_call_target="tpu_custom_call" | custom-call | flops 30000001024 | bytes 8000000 | tf_op jit(solution)/shard_map/pallas_call | solution.py:373
  59.0 2.4 %collective-permute-start.7 = (bf16[784,384]{1,0:T(8,128)(2,1)S(1)}, bf16[784,384]{1,0:T(8,128)(2,1)S(1)}, u32[]{:S(2)}, u32[]{:S(2)}) collective-permute-start(bf16[784,384]{1,0:T(8,128)(2,1)S(1)} %collective-permute-done.3.high), channel_id=1, source_target_pairs={{0,1},{1,0},{2,3},{3,2},{4,5},{5,4},{6,7},{7,6},{8,9},{9,8},{10,11... | collective-permute-start | bytes 1806344 | tf_op jit(solution)/shard_map/ppermute | solution.py:29
  61.4 1.9 %collective-permute-start.6 = (bf16[768,384]{1,0:T(8,128)(2,1)S(1)}, bf16[768,384]{1,0:T(8,128)(2,1)S(1)}, u32[]{:S(2)}, u32[]{:S(2)}) collective-permute-start(bf16[768,384]{1,0:T(8,128)(2,1)S(1)} %collective-permute-done.2.low), channel_id=1, source_target_pairs={{0,1},{1,0},{2,3},{3,2},{4,5},{5,4},{6,7},{7,6},{8,9},{9,8},{10,11... | collective-permute-start | bytes 1769480 | tf_op jit(solution)/shard_map/ppermute | solution.py:29
  63.5 2.3 %shard_map.202.hid = f32[3,8,384]{2,1,0:T(8,128)S(1)} custom-call(s32[6]{0:T(128)S(1)} %stack.27.where, bf16[512,768]{1,0:T(8,128)(2,1)S(1)} %get-tuple-element.39.maps, bf16[384,768]{1,0:T(8,128)(2,1)S(1)} %copy-done.13, bf16[1552,384]{1,0:T(8,128)(2,1)S(1)} %copy-done.12, bf16[1552,384]{1,0:T(8,128)(2,1)S(1)} %collective-permute-done.left, ...), custom_call_target="tpu_custom_call" | custom-call | flops 2000000000 | bytes 6000000 | tf_op jit(solution)/shard_map/pallas_call | solution.py:258
  65.9 2.9 %shard_map.203 = bf16[8,896]{1,0:T(8,128)(2,1)S(1)} custom-call(s32[6]{0:T(128)S(1)} %stack.27.where, bf16[512,768]{1,0:T(8,128)(2,1)S(1)} %get-tuple-element.39.maps, f32[3,8,384]{2,1,0:T(8,128)S(1)} %shard_map.202.hid, f32[8,768]{1,0:T(8,128)S(1)} %get-tuple-element.42.feat_mean, f32[1,768]{1,0:T(1,128)S(1)} %broadcast_in_dim.78.layer_scale, ...), custom_call_target="tpu_custom_call" | custom-call | flops 2000000000 | bytes 8000000 | tf_op jit(solution)/shard_map/pallas_call | solution.py:258
  69.7 8.7 %all-to-all-done = bf16[128,2,1664]{2,1,0:T(2,128)(2,1)} async-done(((bf16[128,2,1664]{2,1,0:T(2,128)(2,1)}), bf16[128,2,1664]{2,1,0:T(2,128)(2,1)}, u32[]{:S(2)}, u32[]{:S(2)}) %all-to-all-start) | async-done | bytes 852000 | tf_op jit(solution)/shard_map/all_to_all | solution.py:449
  79.0 7.0 %all-to-all-start.1 = ((bf16[16,8,896]{2,1,0:T(8,128)(2,1)}), bf16[16,8,896]{2,1,0:T(8,128)(2,1)S(1)}, u32[]{:S(2)}, u32[]{:S(2)}) async-start(bf16[16,8,896]{2,1,0:T(8,128)(2,1)} %broadcast_in_dim.84), calls=%async_computation.1 | async-start | bytes 458752 | tf_op jit(solution)/shard_map/all_to_all | solution.py:33
  86.0 3.1 %reshape.53.got = bf16[256,1664]{1,0:T(8,128)(2,1)} reshape(bf16[128,2,1664]{2,1,0:T(2,128)(2,1)} %all-to-all-done) | data formatting | bytes 1703936 | tf_op jit(solution)/shard_map/reshape | solution.py:509
  96.3 2.4 %all-to-all-done.1 = bf16[16,8,896]{2,1,0:T(8,128)(2,1)S(1)} async-done(((bf16[16,8,896]{2,1,0:T(8,128)(2,1)}), bf16[16,8,896]{2,1,0:T(8,128)(2,1)S(1)}, u32[]{:S(2)}, u32[]{:S(2)}) %all-to-all-start.1) | async-done | bytes 229408 | tf_op jit(solution)/shard_map/all_to_all | solution.py:33
  99.7 17.6 %all_to_all.30 = bf16[8,32,896]{2,1,0:T(8,128)(2,1)S(1)} all-to-all(bf16[8,32,896]{2,1,0:T(8,128)(2,1)S(1)} %bitcast.20), channel_id=1, replica_groups=mesh['section'=4,'z'=16,'y'=4,'core'=2] {'y','core'}, dimensions={0} | all-to-all | bytes 917504 | tf_op jit(solution)/shard_map/all_to_all | solution.py:523
  118.4 3.6 %all-to-all-start.3 = ((bf16[4,64,768]{2,1,0:T(8,128)(2,1)}), bf16[4,64,768]{2,1,0:T(8,128)(2,1)S(1)}, u32[]{:S(2)}, u32[]{:S(2)}) async-start(bf16[4,64,768]{2,1,0:T(8,128)(2,1)} %shard_map.206), calls=%async_computation.3 | async-start | bytes 786432 | tf_op jit(solution)/shard_map/all_to_all | solution.py:33
  124.4 4.1 %all-to-all-done.3 = bf16[4,64,768]{2,1,0:T(8,128)(2,1)S(1)} async-done(((bf16[4,64,768]{2,1,0:T(8,128)(2,1)}), bf16[4,64,768]{2,1,0:T(8,128)(2,1)S(1)}, u32[]{:S(2)}, u32[]{:S(2)}) %all-to-all-start.3) | async-done | bytes 393248 | tf_op jit(solution)/shard_map/all_to_all | solution.py:33
  129.4 17.6 %all_to_all.31 = bf16[16,16,384]{2,1,0:T(8,128)(2,1)S(1)} all-to-all(bf16[16,16,384]{2,1,0:T(8,128)(2,1)S(1)} %get-tuple-element.53), channel_id=1, replica_groups=mesh['section'=4,'z'=16,'y'=4,'core'=2] {'z'}, dimensions={0} | all-to-all | bytes 393216 | tf_op jit(solution)/shard_map/all_to_all | solution.py:33
  147.0 12.5 %all_gather.3.kv = bf16[1024,384]{1,0:T(8,128)(2,1)} all-gather(bf16[256,384]{1,0:T(8,128)(2,1)S(1)} %bitcast.28), channel_id=1, replica_groups=mesh['section'=4,'z'=16,'y'=4,'core'=2] {'y'}, dimensions={0}, use_global_device_ids=true | all-gather | bytes 983040 | tf_op jit(solution)/shard_map/all_gather | solution.py:554
  159.5 9.9 %collective-permute-start.8 = (bf16[1024,384]{1,0:T(8,128)(2,1)}, bf16[1024,384]{1,0:T(8,128)(2,1)S(1)}, u32[]{:S(2)}, u32[]{:S(2)}) collective-permute-start(bf16[1024,384]{1,0:T(8,128)(2,1)} %all_gather.3.kv), channel_id=1, source_target_pairs={{0,1},{1,0},{2,3},{3,2},{4,5},{5,4},{6,7},{7,6},{8,9},{9,8},{10,11... | collective-permute-start | bytes 2359304 | tf_op jit(solution)/shard_map/ppermute | solution.py:29
  170.6 2.0 %shard_map.208 = (f32[256,192]{1,0:T(8,128)S(1)}, f32[256,192]{1,0:T(8,128)S(1)}, f32[16,192]{1,0:T(8,128)S(1)}, f32[16,192]{1,0:T(8,128)S(1)}, f32[192,256]{1,0:T(8,128)S(1)}) custom-call(s32[6]{0:T(128)S(1)} %stack.27.where, bf16[256,192]{1,0:T(8,128)(2,1)S(1)} %get-tuple-element.49.q, bf16[256,192]{1,0:T(8,128)(2,1)S(1)} %get-tuple-element.50.k, ...), custom_call_target="tpu_custom_call" | custom-call | flops 2000000000 | bytes 2000000 | tf_op jit(solution)/shard_map/pallas_call | solution.py:258
  173.7 10.3 %all_to_all.32.parts = bf16[4,192,256]{2,1,0:T(8,128)(2,1)S(1)} all-to-all(bf16[4,192,256]{2,1,0:T(8,128)(2,1)S(1)} %bitcast.23), channel_id=1, replica_groups=mesh['section'=4,'z'=16,'y'=4,'core'=2] {'section'}, dimensions={0} | all-to-all | bytes 786432 | tf_op jit(solution)/shard_map/all_to_all | solution.py:576
  (112 shorter events, 23.1 us)
Async XLA Ops:
  3.0 32.0 %collective-permute-start.1 = (bf16[1552,384]{1,0:T(8,128)(2,1)}, bf16[1552,384]{1,0:T(8,128)(2,1)S(1)}, u32[]{:S(2)}, u32[]{:S(2)}) collective-permute-start(bf16[1552,384]{1,0:T(8,128)(2,1)} %shard_map.199.block), channel_id=1, source_target_pairs={{0,384},{128,0},{256,128},{384,256},{1,385},{129,1},{257,129},{385... | collective-permute-start | bytes 3575816 | tf_op jit(solution)/shard_map/ppermute | solution.py:29
  8.2 27.5 %collective-permute-start = (bf16[1552,384]{1,0:T(8,128)(2,1)}, bf16[1552,384]{1,0:T(8,128)(2,1)S(1)}, u32[]{:S(2)}, u32[]{:S(2)}) collective-permute-start(bf16[1552,384]{1,0:T(8,128)(2,1)} %shard_map.199.block), channel_id=1, source_target_pairs={{0,128},{128,256},{256,384},{384,0},{1,129},{129,257},{257,385},{3... | collective-permute-start | bytes 3575816 | tf_op jit(solution)/shard_map/ppermute | solution.py:29
  14.0 20.6 %copy-start.19 = (f32[7,7,768]{2,1,0:T(8,128)S(1)}, f32[7,7,768]{2,1,0:T(8,128)}, u32[]{:S(2)}) copy-start(f32[7,7,768]{2,1,0:T(8,128)} %param.22) | copy-start | bytes 451588
  14.0 20.7 %copy-start.20 = (f32[768]{0:T(1024)S(1)}, f32[768]{0:T(1024)}, u32[]{:S(2)}) copy-start(f32[768]{0:T(1024)} %param.23) | copy-start | bytes 9220
  14.0 20.7 %copy-start.21 = (f32[768]{0:T(1024)S(1)}, f32[768]{0:T(1024)}, u32[]{:S(2)}) copy-start(f32[768]{0:T(1024)} %param.24) | copy-start | bytes 9220
  14.0 20.7 %copy-start.22 = (f32[768]{0:T(1024)S(1)}, f32[768]{0:T(1024)}, u32[]{:S(2)}) copy-start(f32[768]{0:T(1024)} %param.29) | copy-start | bytes 9220
  14.1 20.7 %copy-start.23 = (f32[768]{0:T(1024)S(1)}, f32[768]{0:T(1024)}, u32[]{:S(2)}) copy-start(f32[768]{0:T(1024)} %param.28) | copy-start | bytes 9220
  14.1 20.7 %copy-start.24 = (f32[768]{0:T(1024)S(1)}, f32[768]{0:T(1024)}, u32[]{:S(2)}) copy-start(f32[768]{0:T(1024)} %param.30) | copy-start | bytes 9220
  14.1 64.2 %all-to-all-start = ((bf16[128,2,1664]{2,1,0:T(2,128)(2,1)}), bf16[128,2,1664]{2,1,0:T(2,128)(2,1)}, u32[]{:S(2)}, u32[]{:S(2)}) async-start(bf16[128,2,1664]{2,1,0:T(2,128)(2,1)} %reshape.49), calls=%async_computation | async-start | bytes 1703936 | tf_op jit(solution)/shard_map/all_to_all | solution.py:449
  35.0 15.0 %copy-start.15 = (bf16[8,8,8,768]{3,2,1,0:T(8,128)(2,1)S(1)}, bf16[8,8,8,768]{3,2,1,0:T(8,128)(2,1)}, u32[]{:S(2)}) copy-start(bf16[8,8,8,768]{3,2,1,0:T(8,128)(2,1)} %param.21) | copy-start | bytes 2359300
  35.8 23.3 %collective-permute-start.3 = (bf16[784,384]{1,0:T(8,128)(2,1)S(1)}, bf16[784,384]{1,0:T(8,128)(2,1)S(1)}, u32[]{:S(2)}, u32[]{:S(2)}) collective-permute-start(bf16[784,384]{1,0:T(8,128)(2,1)S(1)} %slice.37), channel_id=1, source_target_pairs={{0,384},{128,0},{256,128},{384,256},{1,385},{129,1},{257,129},{385... | collective-permute-start | bytes 1806344 | tf_op jit(solution)/shard_map/ppermute | solution.py:29
  40.1 18.9 %collective-permute-start.2 = (bf16[768,384]{1,0:T(8,128)(2,1)S(1)}, bf16[768,384]{1,0:T(8,128)(2,1)S(1)}, u32[]{:S(2)}, u32[]{:S(2)}) collective-permute-start(bf16[768,384]{1,0:T(8,128)(2,1)S(1)} %slice.36), channel_id=1, source_target_pairs={{0,128},{128,256},{256,384},{384,0},{1,129},{129,257},{257,385},{3... | collective-permute-start | bytes 1769480 | tf_op jit(solution)/shard_map/ppermute | solution.py:29
  42.0 21.4 %collective-permute-start.4 = (bf16[1552,384]{1,0:T(8,128)(2,1)S(1)}, bf16[1552,384]{1,0:T(8,128)(2,1)S(1)}, u32[]{:S(2)}, u32[]{:S(2)}) collective-permute-start(bf16[1552,384]{1,0:T(8,128)(2,1)S(1)} %collective-permute-done.left), channel_id=1, source_target_pairs={{0,1},{1,0},{2,3},{3,2},{4,5},{5,4},{6,7},{7,6},{8,9},{9,8},{10,11... | collective-permute-start | bytes 3575816 | tf_op jit(solution)/shard_map/ppermute | solution.py:29
  48.0 15.4 %collective-permute-start.5 = (bf16[1552,384]{1,0:T(8,128)(2,1)S(1)}, bf16[1552,384]{1,0:T(8,128)(2,1)S(1)}, u32[]{:S(2)}, u32[]{:S(2)}) collective-permute-start(bf16[1552,384]{1,0:T(8,128)(2,1)S(1)} %collective-permute-done.1.right), channel_id=1, source_target_pairs={{0,1},{1,0},{2,3},{3,2},{4,5},{5,4},{6,7},{7,6},{8,9},{9,8},{10,11... | collective-permute-start | bytes 3575816 | tf_op jit(solution)/shard_map/ppermute | solution.py:29
  50.0 13.5 %copy-start.12 = (bf16[1552,384]{1,0:T(8,128)(2,1)S(1)}, bf16[1552,384]{1,0:T(8,128)(2,1)}, u32[]{:S(2)}) copy-start(bf16[1552,384]{1,0:T(8,128)(2,1)} %shard_map.199.block) | copy-start | bytes 3575812
  50.0 13.5 %copy-start.13 = (bf16[384,768]{1,0:T(8,128)(2,1)S(1)}, bf16[384,768]{1,0:T(8,128)(2,1)}, u32[]{:S(2)}) copy-start(bf16[384,768]{1,0:T(8,128)(2,1)} %up.1) | copy-start | bytes 1769476
  59.0 6.8 %collective-permute-start.7 = (bf16[784,384]{1,0:T(8,128)(2,1)S(1)}, bf16[784,384]{1,0:T(8,128)(2,1)S(1)}, u32[]{:S(2)}, u32[]{:S(2)}) collective-permute-start(bf16[784,384]{1,0:T(8,128)(2,1)S(1)} %collective-permute-done.3.high), channel_id=1, source_target_pairs={{0,1},{1,0},{2,3},{3,2},{4,5},{5,4},{6,7},{7,6},{8,9},{9,8},{10,11... | collective-permute-start | bytes 1806344 | tf_op jit(solution)/shard_map/ppermute | solution.py:29
  61.4 4.4 %collective-permute-start.6 = (bf16[768,384]{1,0:T(8,128)(2,1)S(1)}, bf16[768,384]{1,0:T(8,128)(2,1)S(1)}, u32[]{:S(2)}, u32[]{:S(2)}) collective-permute-start(bf16[768,384]{1,0:T(8,128)(2,1)S(1)} %collective-permute-done.2.low), channel_id=1, source_target_pairs={{0,1},{1,0},{2,3},{3,2},{4,5},{5,4},{6,7},{7,6},{8,9},{9,8},{10,11... | collective-permute-start | bytes 1769480 | tf_op jit(solution)/shard_map/ppermute | solution.py:29
  79.0 19.7 %all-to-all-start.1 = ((bf16[16,8,896]{2,1,0:T(8,128)(2,1)}), bf16[16,8,896]{2,1,0:T(8,128)(2,1)S(1)}, u32[]{:S(2)}, u32[]{:S(2)}) async-start(bf16[16,8,896]{2,1,0:T(8,128)(2,1)} %broadcast_in_dim.84), calls=%async_computation.1 | async-start | bytes 458752 | tf_op jit(solution)/shard_map/all_to_all | solution.py:33
  99.7 22.3 %copy-start.29 = (s32[12]{0:T(128)S(1)}, s32[12]{0:T(128)}, u32[]{:S(2)}) copy-start(s32[12]{0:T(128)} %param.40) | copy-start | bytes 148
  118.4 10.1 %all-to-all-start.3 = ((bf16[4,64,768]{2,1,0:T(8,128)(2,1)}), bf16[4,64,768]{2,1,0:T(8,128)(2,1)S(1)}, u32[]{:S(2)}, u32[]{:S(2)}) async-start(bf16[4,64,768]{2,1,0:T(8,128)(2,1)} %shard_map.206), calls=%async_computation.3 | async-start | bytes 786432 | tf_op jit(solution)/shard_map/all_to_all | solution.py:33
  128.5 40.9 %copy-start.18 = (bf16[192,768]{1,0:T(8,128)(2,1)S(1)}, bf16[192,768]{1,0:T(8,128)(2,1)}, u32[]{:S(2)}) copy-start(bf16[192,768]{1,0:T(8,128)(2,1)} %param.41) | copy-start | bytes 884740
  129.4 40.2 %copy-start.16 = (bf16[256,192]{1,0:T(8,128)(2,1)}, bf16[256,192]{1,0:T(8,128)(2,1)S(1)}, u32[]{:S(2)}) copy-start(bf16[256,192]{1,0:T(8,128)(2,1)S(1)} %get-tuple-element.51.v) | copy-start | bytes 294916
  159.5 13.1 %collective-permute-start.8 = (bf16[1024,384]{1,0:T(8,128)(2,1)}, bf16[1024,384]{1,0:T(8,128)(2,1)S(1)}, u32[]{:S(2)}, u32[]{:S(2)}) collective-permute-start(bf16[1024,384]{1,0:T(8,128)(2,1)} %all_gather.3.kv), channel_id=1, source_target_pairs={{0,1},{1,0},{2,3},{3,2},{4,5},{5,4},{6,7},{7,6},{8,9},{9,8},{10,11... | collective-permute-start | bytes 2359304 | tf_op jit(solution)/shard_map/ppermute | solution.py:29
  (18 other events, 39.6 us)
